TPU v7x, 32 devices: a whole 2x2x4 slice. The times are simulated.
32 devices in a mesh: groups: 2 (over x), dom: 16 (over z, y, core).
Axes of the slice: x: 2, y: 2, z: 4, core: 2. Of those that a mesh axis runs over, the one named last changes fastest.
Arguments:
- displacement: float32 [3, 69632], P(None, ('groups', 'dom')), parts along dimension 1, may hold values from -6 to 6
- velocity: float32 [3, 69632], P(None, ('groups', 'dom')), parts along dimension 1, may hold values from -6 to 6
- node_mass: float32 [69632], P(('groups', 'dom')), parts along dimension 0, may hold values from 0.5 to 2
- connectivity: int32 [8, 65536], P(None, ('groups', 'dom')), parts along dimension 1, may hold values from 0 to 2175
- modulus: float32 [65536], P(('groups', 'dom')), parts along dimension 0, may hold values from 0.3 to 1.2
- elem_stiffness: float32 [24, 24], replicated, as said below
- slave_nodes: int32 [2048, 128], P(('groups', 'dom')), parts along dimension 0, may hold values from 0 to 2175
- slave_gap: float32 [2048, 128], P(('groups', 'dom')), parts along dimension 0, may hold values from -6 to 6
- master_nodes: int32 [1024, 128], P(('groups', 'dom')), parts along dimension 0, may hold values from 0 to 2175
- pair_slave: int32 [4096], P(('groups', 'dom')), parts along dimension 0, may hold values from 0 to 63
- pair_owner: int32 [4096, 1], P(('groups', 'dom')), parts along dimension 0, may hold values from 0 to 15; in each aligned block of 128 rows (0 to 127, 128 to 255, ...) at most 16 rows name the same one
- pair_master: int32 [4096], P(('groups', 'dom')), parts along dimension 0, may hold values from 0 to 31
- pair_normal: float32 [3, 4096], P(None, ('groups', 'dom')), parts along dimension 1, may hold values from -4 to 4
- lower_face: int32 [16384], P(('groups', 'dom')), parts along dimension 0, may hold values from 0 to 2175
- upper_face: int32 [16384], P(('groups', 'dom')), parts along dimension 0, may hold values from 0 to 2175
- mortar: float32 [128, 128], replicated, as said below
Outputs:
- new_displacement: float32 [3, 69632], P(None, ('groups', 'dom')), parts along dimension 1
- new_velocity: float32 [3, 69632], P(None, ('groups', 'dom')), parts along dimension 1
There are 2 independent parts, one for each index of `groups`. A program takes and returns all parts, laid end to end along the dimension named above; an argument that names none is the same for every part. Nothing has to cross between parts.
Inputs may be any that keep to these rules, and one draw needn't show every extreme that they name: `pair_owner`: in the 128 pairs of one partition at most 16 name the same owner, a bound that some block reaches. `elem_stiffness`: symmetric with a dominant positive diagonal. `mortar`: full rank with a positive diagonal.
All inputs are finite; a program needn't handle non-finite values.
Results may differ from a plain program's by a relative error of at most 0.0001.
Values sent between devices are 32-bit elements; how exact they have to be, the bound alone decides.
No kernel may reach another device: no remote copies, remote signals or barrier semaphores. Data moves between devices by JAX's collectives and lax.ppermute only.
A program may use at most 128 MiB of HBM per device.

v0:
```python
import jax
import jax.numpy as jnp
from jax import lax
from jax.sharding import PartitionSpec as P

PATCH = 128
STEPS = 3


time_step = 0.1


def extended_2(value, sides, width):
    for axis, dim in sides:
        devices, length = (lax.axis_size(axis), value.shape[dim])
        up = [(i, (i + 1) % devices) for i in range(devices - 1)]
        down = [(j, i) for i, j in up]
        last = lax.slice_in_dim(value, length - width, length, axis=dim)
        first = lax.slice_in_dim(value, 0, width, axis=dim)
        before = lax.ppermute(last, axis, up)
        after = lax.ppermute(first, axis, down)
        value = jnp.concatenate([before, value, after], axis=dim)
    return value


def elastic_force(disp, connectivity, modulus, elem_stiffness):
    count = connectivity.shape[1]
    ue = disp[:, connectivity].reshape(24, count)
    fe = jnp.dot(elem_stiffness, ue, precision=lax.Precision.HIGHEST) * modulus[None, :]
    return jnp.zeros_like(disp).at[:, connectivity.reshape(-1)].add(fe.reshape(3, -1))


def pair_forces(us, um, gap0, normal, mortar):
    mapped = jnp.einsum("ij,pcj->pci", mortar, um, precision=lax.Precision.HIGHEST)
    gap = gap0 + jnp.sum(normal[:, :, None] * (us - mapped), axis=1)
    press = jnp.maximum(-gap, 0.0)
    slave_force = press[:, None, :] * normal[:, :, None]
    master_force = -jnp.einsum("ij,pci->pcj", mortar, slave_force, precision=lax.Precision.HIGHEST)
    return (slave_force, master_force)


def shards(
    displacement,
    velocity,
    node_mass,
    connectivity,
    modulus,
    elem_stiffness,
    slave_nodes,
    slave_gap,
    master_nodes,
    pair_slave,
    pair_owner,
    pair_master,
    pair_normal,
    lower_face,
    upper_face,
    mortar,
):
    n_dom = lax.axis_size("dom")
    owner = pair_owner[:, 0]
    patches = master_nodes.shape[0]
    s_nodes = slave_nodes[pair_slave]
    gap0 = slave_gap[pair_slave]
    normal = pair_normal.T
    u = displacement
    v = velocity
    for step in range(STEPS):
        local = -elastic_force(u, connectivity, modulus, elem_stiffness)
        us = jnp.moveaxis(u[:, s_nodes], 0, 1)
        own = jnp.moveaxis(u[:, master_nodes], 0, 1)
        table = lax.all_gather(own, "dom", axis=0, tiled=True)
        um = table[owner * patches + pair_master]
        slave_force, master_force = pair_forces(us, um, gap0, normal, mortar)
        local = local.at[:, s_nodes.reshape(-1)].add(jnp.moveaxis(slave_force, 1, 0).reshape(3, -1))
        stacked = jnp.stack([local[:, lower_face], local[:, upper_face]])
        extended = extended_2(stacked, (("dom", 0),), 1)
        force = local.at[:, lower_face].add(extended[0]).at[:, upper_face].add(extended[3])
        whole = (
            jnp.zeros((n_dom * patches, 3, PATCH), jnp.float32)
            .at[owner * patches + pair_master]
            .add(master_force)
        )
        mine = lax.psum_scatter(whole, "dom", scatter_dimension=0, tiled=True)
        force = force.at[:, master_nodes.reshape(-1)].add(jnp.moveaxis(mine, 1, 0).reshape(3, -1))
        v = v + time_step * force / node_mass[None, :]
        u = u + time_step * v
    return (u, v)


def solution(mesh):
    return jax.shard_map(
        shards,
        mesh=mesh,
        in_specs=(
            P(None, ("groups", "dom")),
            P(None, ("groups", "dom")),
            P(("groups", "dom")),
            P(None, ("groups", "dom")),
            P(("groups", "dom")),
            P(),
            P(("groups", "dom"), None),
            P(("groups", "dom"), None),
            P(("groups", "dom"), None),
            P(("groups", "dom")),
            P(("groups", "dom"), None),
            P(("groups", "dom")),
            P(None, ("groups", "dom")),
            P(("groups", "dom")),
            P(("groups", "dom")),
            P(),
        ),
        out_specs=(P(None, ("groups", "dom")), P(None, ("groups", "dom"))),
        check_vma=False,
    )
```

profile of v0, /device:TPU:1, one launch (start us, length us, event | category | flops | bytes accessed | tf_op | source)
XLA Modules:
  0.0 1264.7 jit_solution(17780146472861615497)
XLA Ops:
  10.3 54.4 %gather_fusion = f32[16384,3]{1,0:T(8,128)} fusion(f32[3,2176]{0,1:T(8,128)S(1)} %copy.143, s32[16384]{0:T(1024)S(1)} %broadcast_clamp_fusion), kind=kCustom, calls=%fused_computation | custom fusion | bytes 458752 | tf_op jit(solution)/shard_map/gather | solution.py:28
  64.7 5.3 copy.144
  70.5 5.1 copy.145
  75.6 80.0 %scatter_custom_fusion = f32[3,2176]{0,1:T(8,128)S(1)} fusion(s32[16384]{0:T(1024)S(1)} %bitcast.202, f32[3,16384]{0,1:T(8,128)} %copy.145, f32[]{:T(128)} %constant.7.clone.1), kind=kCustom, calls=%fused_computation.51 | custom fusion | flops 49152 | bytes 222724 | tf_op jit(solution)/shard_map/scatter-add | solution.py:30
  157.9 54.4 %gather_fusion.3 = f32[16384,3]{1,0:T(8,128)} fusion(f32[3,2176]{0,1:T(8,128)S(1)} %copy.143, s32[16384]{0:T(1024)S(1)} %fusion.53), kind=kCustom, calls=%fused_computation.3 | custom fusion | bytes 458752 | tf_op jit(solution)/shard_map/gather | solution.py:70
  212.3 5.2 copy.180
  217.6 14.1 %gather_fusion.4 = f32[4096,3]{1,0:T(8,128)} fusion(f32[3,2176]{0,1:T(8,128)S(1)} %copy.143, s32[4096]{0:T(1024)S(1)} %fusion.61), kind=kCustom, calls=%fused_computation.4 | custom fusion | bytes 114688 | tf_op jit(solution)/shard_map/gather | solution.py:71
  231.6 2.2 copy.149
  233.9 25.4 %all_gather.9 = f32[512,3,128]{2,0,1:T(8,128)S(1)} all-gather(f32[32,3,128]{2,0,1:T(8,128)S(1)} %bitcast.193), channel_id=1, replica_groups=mesh['groups'=2,'dom'=16] {'dom'}, dimensions={0}, use_global_device_ids=true | all-gather | bytes 835584 | tf_op jit(solution)/shard_map/all_gather | solution.py:72
  261.1 4.6 bitcast_multiply_fusion.2
  265.7 88.6 %scatter_custom_fusion.1 = f32[3,2176]{0,1:T(8,128)S(1)} fusion(f32[3,2176]{0,1:T(8,128)S(1)} %neg.45, s32[16384]{0:T(1024)S(1)} %bitcast.205, f32[3,16384]{0,1:T(8,128)} %bitcast_multiply_fusion.2), kind=kCustom, calls=%fused_computation.49 | custom fusion | flops 49152 | bytes 222720 | tf_op jit(solution)/shard_map/scatter-add | solution.py:75
  359.6 2.4 collective-permute-start.1
  362.7 4.9 scatter_fusion
  370.0 4.2 scatter_custom_fusion.2
  374.2 4.1 scatter_custom_fusion.3
  378.4 80.8 %all-reduce.7.cloned.1.call-done = f32[512,3,128]{2,1,0:T(4,128)} async-done(((f32[512,3,128]{2,1,0:T(4,128)}), f32[512,3,128]{2,1,0:T(4,128)}) %all-reduce.7.cloned.1.call-update) | async-done | bytes 786448
  462.1 23.1 %scatter_fusion.1 = f32[3,2176]{0,1:T(8,128)S(1)} fusion(f32[3,2176]{0,1:T(8,128)S(1)} %scatter_custom_fusion.3, s32[4096]{0:T(1024)S(1)} %bitcast.187, f32[4096,3]{1,0:T(8,128)} %copy.154), kind=kCustom, calls=%fused_computation.25 | custom fusion | flops 12288 | bytes 163840 | tf_op jit(solution)/shard_map/scatter-add | solution.py:85
  486.2 54.4 %gather_fusion.9 = f32[16384,3]{1,0:T(8,128)} fusion(f32[3,2176]{0,1:T(8,128)S(1)} %copy.156, s32[16384]{0:T(1024)S(1)} %fusion.53), kind=kCustom, calls=%fused_computation.9 | custom fusion | bytes 458752 | tf_op jit(solution)/shard_map/gather | solution.py:70
  540.6 12.7 %gather_fusion.10 = f32[4096,3]{1,0:T(8,128)S(1)} fusion(f32[3,2176]{0,1:T(8,128)S(1)} %copy.156, s32[4096]{0:T(1024)} %copy-done.14), kind=kCustom, calls=%fused_computation.10 | custom fusion | bytes 114688 | tf_op jit(solution)/shard_map/gather | solution.py:71
  553.4 5.9 copy.181
  560.5 23.2 %all_gather.10 = f32[512,3,128]{2,0,1:T(8,128)S(1)} all-gather(f32[32,3,128]{2,0,1:T(8,128)} %bitcast.194), channel_id=1, replica_groups=mesh['groups'=2,'dom'=16] {'dom'}, dimensions={0}, use_global_device_ids=true | all-gather | bytes 835584 | tf_op jit(solution)/shard_map/all_gather | solution.py:72
  586.2 4.9 scatter_fusion.2
  592.3 54.4 %gather_fusion.8 = f32[16384,3]{1,0:T(8,128)} fusion(f32[3,2176]{0,1:T(8,128)S(1)} %copy.156, s32[16384]{0:T(1024)S(1)} %broadcast_clamp_fusion), kind=kCustom, calls=%fused_computation.8 | custom fusion | bytes 458752 | tf_op jit(solution)/shard_map/gather | solution.py:28
  646.7 5.3 copy.157
  652.5 5.1 copy.158
  657.6 80.0 %scatter_custom_fusion.6 = f32[3,2176]{0,1:T(8,128)S(1)} fusion(s32[16384]{0:T(1024)} %bitcast.203, f32[3,16384]{0,1:T(8,128)} %copy.158, f32[]{:T(128)} %constant.7.clone.1), kind=kCustom, calls=%fused_computation.47 | custom fusion | flops 49152 | bytes 8415232 | tf_op jit(solution)/shard_map/scatter-add | solution.py:30
  737.6 4.6 bitcast_multiply_fusion.1
  742.2 88.6 %scatter_custom_fusion.7 = f32[3,2176]{0,1:T(8,128)S(1)} fusion(f32[3,2176]{0,1:T(8,128)S(1)} %neg.48, s32[16384]{0:T(1024)} %bitcast.206, f32[3,16384]{0,1:T(8,128)} %bitcast_multiply_fusion.1), kind=kCustom, calls=%fused_computation.45 | custom fusion | flops 49152 | bytes 8414720 | tf_op jit(solution)/shard_map/scatter-add | solution.py:75
  834.8 2.4 collective-permute-start.3
  838.1 3.8 scatter_custom_fusion.8
  842.5 3.8 scatter_custom_fusion.9
  849.3 23.0 %scatter_fusion.3 = f32[3,2176]{0,1:T(8,128)S(1)} fusion(f32[3,2176]{0,1:T(8,128)S(1)} %scatter_custom_fusion.9, s32[4096]{0:T(1024)S(1)} %bitcast.188, f32[4096,3]{1,0:T(8,128)S(1)} %copy.166), kind=kCustom, calls=%fused_computation.31 | custom fusion | flops 12288 | bytes 163840 | tf_op jit(solution)/shard_map/scatter-add | solution.py:85
  874.4 54.4 %gather_fusion.15 = f32[16384,3]{1,0:T(8,128)} fusion(f32[3,2176]{0,1:T(8,128)S(1)} %copy.168, s32[16384]{0:T(1024)S(1)} %fusion.53), kind=kCustom, calls=%fused_computation.15 | custom fusion | bytes 458752 | tf_op jit(solution)/shard_map/gather | solution.py:70
  928.8 12.7 %gather_fusion.16 = f32[4096,3]{1,0:T(8,128)S(1)} fusion(f32[3,2176]{0,1:T(8,128)S(1)} %copy.168, s32[4096]{0:T(1024)} %copy-done.14), kind=kCustom, calls=%fused_computation.16 | custom fusion | bytes 114688 | tf_op jit(solution)/shard_map/gather | solution.py:71
  941.6 5.9 copy.182
  948.1 21.5 %all_gather.11 = f32[512,3,128]{2,0,1:T(8,128)S(1)} all-gather(f32[32,3,128]{2,0,1:T(8,128)S(1)} %bitcast.195), channel_id=1, replica_groups=mesh['groups'=2,'dom'=16] {'dom'}, dimensions={0}, use_global_device_ids=true | all-gather | bytes 835584 | tf_op jit(solution)/shard_map/all_gather | solution.py:72
  972.1 4.9 scatter_fusion.4
  978.0 54.4 %gather_fusion.14 = f32[16384,3]{1,0:T(8,128)} fusion(f32[3,2176]{0,1:T(8,128)S(1)} %copy.168, s32[16384]{0:T(1024)S(1)} %broadcast_clamp_fusion), kind=kCustom, calls=%fused_computation.14 | custom fusion | bytes 458752 | tf_op jit(solution)/shard_map/gather | solution.py:28
  1032.5 5.3 copy.169
  1038.2 5.1 copy.170
  1043.3 80.0 %scatter_custom_fusion.12 = f32[3,2176]{0,1:T(8,128)S(1)} fusion(s32[16384]{0:T(1024)} %bitcast.204, f32[3,16384]{0,1:T(8,128)} %copy.170, f32[]{:T(128)} %constant.7.clone.1), kind=kCustom, calls=%fused_computation.43 | custom fusion | flops 49152 | bytes 8415232 | tf_op jit(solution)/shard_map/scatter-add | solution.py:30
  1123.4 4.6 bitcast_multiply_fusion
  1127.9 88.6 %scatter_custom_fusion.13 = f32[3,2176]{0,1:T(8,128)S(1)} fusion(f32[3,2176]{0,1:T(8,128)S(1)} %neg.51, s32[16384]{0:T(1024)} %bitcast.207, f32[3,16384]{0,1:T(8,128)} %bitcast_multiply_fusion), kind=kCustom, calls=%fused_computation.41 | custom fusion | flops 49152 | bytes 8414720 | tf_op jit(solution)/shard_map/scatter-add | solution.py:75
  1218.6 2.2 collective-permute-start.4
  1220.8 2.4 collective-permute-start.5
  1224.1 3.8 scatter_custom_fusion.14
  1228.5 3.8 scatter_custom_fusion.15
  1233.9 22.8 %scatter_fusion.5 = f32[3,2176]{0,1:T(8,128)S(1)} fusion(f32[3,2176]{0,1:T(8,128)S(1)} %scatter_custom_fusion.15, s32[4096]{0:T(1024)S(1)} %bitcast.189, f32[4096,3]{1,0:T(8,128)S(1)} %copy.178), kind=kCustom, calls=%fused_computation.37 | custom fusion | flops 12288 | bytes 163840 | tf_op jit(solution)/shard_map/scatter-add | solution.py:85
  (194 shorter events, 45.5 us)
Async XLA Ops:
  7.2 253.6 %copy-start = (f32[128,128]{1,0:T(8,128)S(1)}, f32[128,128]{1,0:T(8,128)}, u32[]{:S(2)}) copy-start(f32[128,128]{1,0:T(8,128)} %param.31) | copy-start | bytes 196612
  7.2 452.0 %all-reduce.7.cloned.1.call-start = ((), (), s32[]{:S(2)}) async-start(), calls=%async_computation | async-start | bytes 2097152
  9.1 66.5 %copy-start.31 = (s32[16384,1]{0,1:T(1,128)}, s32[16384,1]{0,1:T(1,128)S(1)}, u32[]{:S(2)}) copy-start(s32[16384,1]{0,1:T(1,128)S(1)} %compare_select_fusion.1) | copy-start | bytes 196612
  64.7 5.3 copy-start.19
  64.7 5.3 copy-start.28
  155.6 1.5 copy-start.25
  155.6 1.6 copy-start.2
  157.1 108.6 %copy-start.32 = (s32[16384,1]{0,1:T(1,128)}, s32[16384,1]{0,1:T(1,128)S(1)}, u32[]{:S(2)}) copy-start(s32[16384,1]{0,1:T(1,128)S(1)} %compare_select_fusion) | copy-start | bytes 196612
  212.3 5.2 copy-start.33
  217.5 16.3 %copy-start.14 = (s32[4096]{0:T(1024)}, s32[4096]{0:T(1024)S(1)}, u32[]{:S(2)}) copy-start(s32[4096]{0:T(1024)S(1)} %fusion.61) | copy-start | bytes 49156
  259.9 102.8 %copy-start.42 = (s32[128]{0:T(128)}, s32[128]{0:T(128)S(1)}, u32[]{:S(2)}) copy-start(s32[128]{0:T(128)S(1)} %compare_select_fusion.8) | copy-start | bytes 1540
  259.9 0.8 copy-start.45
  259.9 114.3 %copy-start.40 = (s32[512]{0:T(512)}, s32[512]{0:T(512)S(1)}, u32[]{:S(2)}) copy-start(s32[512]{0:T(512)S(1)} %compare_select_fusion.6) | copy-start | bytes 6148
  260.0 94.3 %copy-start.34 = (s32[1024]{0:T(1024)}, s32[1024]{0:T(1024)S(1)}, u32[]{:S(2)}) copy-start(s32[1024]{0:T(1024)S(1)} %pad_clamp_fusion.1) | copy-start | bytes 12292
  265.7 92.2 %copy-start.47 = (s32[512]{0:T(512)S(1)}, s32[512]{0:T(512)}, u32[]{:S(2)}) copy-start(s32[512]{0:T(512)} %param.29) | copy-start | bytes 6148
  355.9 14.1 %collective-permute-start = (f32[1,3,512]{1,2,0:T(8,128)}, f32[1,3,512]{1,2,0:T(8,128)S(1)}, u32[]{:S(2)}, u32[]{:S(2)}) collective-permute-start(f32[1,3,512]{1,2,0:T(8,128)} %bitcast.22), channel_id=1, source_target_pairs={{0,1},{1,2},{2,3},{3,4},{4,5},{5,6},{6,7},{7,8},{8,9},{9,10},{10,1... | collective-permute-start | bytes 18440 | tf_op jit(solution)/shard_map/ppermute | solution.py:20
  357.9 12.1 copy-start.41
  357.9 9.7 copy-start.37
  359.6 14.7 %collective-permute-start.1 = (f32[1,3,512]{1,2,0:T(8,128)}, f32[1,3,512]{1,2,0:T(8,128)}, u32[]{:S(2)}, u32[]{:S(2)}) collective-permute-start(f32[1,3,512]{1,2,0:T(8,128)} %bitcast.26), channel_id=1, source_target_pairs={{1,0},{2,1},{3,2},{4,3},{5,4},{6,5},{7,6},{8,7},{9,8},{10,9},{11,1... | collective-permute-start | bytes 18440 | tf_op jit(solution)/shard_map/ppermute | solution.py:21
  362.6 6.1 copy-start.51
  367.6 1.0 copy-start.4
  368.7 477.7 %all-reduce.9.cloned.1.call-start = ((), (), s32[]{:S(2)}) async-start(), calls=%async_computation.1 | async-start | bytes 2097152
  462.1 23.4 %copy-start.15 = (f32[3,2176]{1,0:T(4,128)S(1)}, f32[3,2176]{1,0:T(4,128)}, u32[]{:S(2)}) copy-start(f32[3,2176]{1,0:T(4,128)} %param.16) | copy-start | bytes 78340
  462.1 23.4 %copy-start.16 = (f32[3,2176]{1,0:T(4,128)S(1)}, f32[3,2176]{1,0:T(4,128)}, u32[]{:S(2)}) copy-start(f32[3,2176]{1,0:T(4,128)} %param.17) | copy-start | bytes 78340
  462.1 23.5 %copy-start.22 = (f32[2176]{0:T(1024)S(1)}, f32[2176]{0:T(1024)}, u32[]{:S(2)}) copy-start(f32[2176]{0:T(1024)} %param.18) | copy-start | bytes 26116
  583.7 1.4 copy-start.7
  583.7 1.4 copy-start.26
  591.1 1.0 copy-start.5
  592.1 640.3 %all-reduce.11.cloned.1.call-start = ((), (), s32[]{:S(2)}) async-start(), calls=%async_computation.2 | async-start | bytes 2097152
  646.7 5.3 copy-start.20
  646.7 5.3 copy-start.29
  742.2 88.6 %copy-start.38 = (s32[1024]{0:T(1024)S(1)}, s32[1024]{0:T(1024)}, u32[]{:S(2)}) copy-start(s32[1024]{0:T(1024)} %copy-done.37) | copy-start | bytes 12292
  742.2 89.7 %copy-start.35 = (s32[1024]{0:T(1024)S(1)}, s32[1024]{0:T(1024)}, u32[]{:S(2)}) copy-start(s32[1024]{0:T(1024)} %copy-done.34) | copy-start | bytes 12292
  832.9 5.2 collective-permute-start.2
  834.8 7.7 collective-permute-start.3
  872.4 0.8 copy-start.17
  969.6 1.4 copy-start.6
  969.6 1.4 copy-start.27
  977.0 1.0 copy-start.3
  1032.5 5.3 copy-start.21
  1032.5 5.3 copy-start.30
  1127.9 88.6 %copy-start.39 = (s32[1024]{0:T(1024)S(1)}, s32[1024]{0:T(1024)}, u32[]{:S(2)}) copy-start(s32[1024]{0:T(1024)} %copy-done.37) | copy-start | bytes 12292
  1127.9 89.7 %copy-start.36 = (s32[1024]{0:T(1024)S(1)}, s32[1024]{0:T(1024)}, u32[]{:S(2)}) copy-start(s32[1024]{0:T(1024)} %copy-done.34) | copy-start | bytes 12292
  1218.6 5.5 collective-permute-start.4
  1220.8 7.7 collective-permute-start.5
  1233.9 23.2 %copy-start.9 = (f32[3,2176]{1,0:T(4,128)S(1)}, f32[3,2176]{1,0:T(4,128)}, u32[]{:S(2)}) copy-start(f32[3,2176]{1,0:T(4,128)} %copy-done.8) | copy-start | bytes 78340
  1233.9 23.2 %copy-start.18 = (f32[3,2176]{1,0:T(4,128)S(1)}, f32[3,2176]{1,0:T(4,128)}, u32[]{:S(2)}) copy-start(f32[3,2176]{1,0:T(4,128)} %get-tuple-element.13) | copy-start | bytes 78340
  1233.9 23.2 %copy-start.24 = (f32[2176]{0:T(1024)S(1)}, f32[2176]{0:T(1024)}, u32[]{:S(2)}) copy-start(f32[2176]{0:T(1024)} %param.18) | copy-start | bytes 26116
  (13 other events, 9.0 us)
Sparse Core Ops, SparseCore 0:
  368.8 90.3 all-reduce.6
  592.2 89.4 all-reduce.8
  978.2 89.3 all-reduce.10
where the time goes:
time: 1270 us; the launch traced here: 1260 us
  other arithmetic  629 us (50%)
  local copies, waits for them, and re-layouts  449 us (35%)
  waiting for transfers between devices  83.8 us (7%)
  blocking collectives  70.1 us (6%)
  between operations  16 us (1%)
  starting transfers between devices  13.5 us (1%)
    scatter-add x3, other arithmetic, shards(): local.at[:, s_nodes.reshape(-1)]  266 us
    scatter-add x3, other arithmetic, elastic_force(): jnp.zeros_like(disp).at[:, connectivity.reshape(-1)].add(fe.reshape(3, -1))  240 us
    gather x6, local copies, waits for them, and re-layouts, shards(): us = jnp.moveaxis(u[:, s_nodes], 0, 1)  180 us
    gather x6, local copies, waits for them, and re-layouts, elastic_force(): ue = disp[:, connectivity].reshape(24, count)  179 us
    unnamed x6, waiting for transfers between devices  80.9 us
    all_gather x3, blocking collectives, shards(): table = lax.all_gather(own, 'dom', axis=0, tiled=True)  70.1 us
    scatter-add x3, other arithmetic, shards(): force.at[:, master_nodes.reshape(-1)]  68.9 us
    gather x6, local copies, waits for them, and re-layouts, shards(): own = jnp.moveaxis(u[:, master_nodes], 0, 1)  43.6 us
  transfers between devices with their start and end apart: 9, of which 5 were waited for; matrix products, arithmetic and copies ran while one was open for 41% of the time, Pallas kernels for 0%

commit v1 on v0

v1 whole, which is shorter than its diff:
```python
import functools

import jax
import jax.numpy as jnp
from jax import lax
from jax.experimental import pallas as pl
from jax.experimental.pallas import tpu as pltpu
from jax.sharding import PartitionSpec as P

LANES = 128
STEPS = 3
TIME_STEP = 0.1
SLOTS = 256
CHUNK = 16

F32 = jnp.float32
BF16 = jnp.bfloat16
HIGH = lax.Precision.HIGHEST
NN = (((1,), (0,)), ((), ()))
NT = (((1,), (1,)), ((), ()))
TN = (((0,), (0,)), ((), ()))

MAIN = 16
ROWS = 56
FACTOR_ROWS = 112


def dot_exact(a, b, dims):
    return lax.dot_general(a, b, dims, precision=HIGH, preferred_element_type=F32)


def iota(shape, dim):
    return lax.broadcasted_iota(jnp.int32, shape, dim)


def field_row(c, h):
    return c * MAIN + h if h < MAIN else 3 * MAIN + c


def to_field(flat_ref, field_ref):
    field_ref[...] = jnp.zeros_like(field_ref)
    for c in range(3):
        for h in range(MAIN + 1):
            r = field_row(c, h)
            field_ref[r : r + 1, :] = flat_ref[c : c + 1, h * LANES : (h + 1) * LANES]


def from_field(field, flat_ref):
    for c in range(3):
        for h in range(MAIN + 1):
            r = field_row(c, h)
            flat_ref[c : c + 1, h * LANES : (h + 1) * LANES] = field[r : r + 1, :]


def gather8(field_ref, index):
    lane = index & (LANES - 1)
    row = index >> 7
    found = [jnp.zeros((8, LANES), F32) for _ in range(3)]
    for h in range(MAIN + 1):
        here = row == h
        for c in range(3):
            r = field_row(c, h)
            table = jnp.broadcast_to(field_ref[r : r + 1, :], (8, LANES))
            value = jnp.take_along_axis(table, lane, axis=1, mode="promise_in_bounds")
            found[c] = jnp.where(here, value, found[c])
    return found


def scatter_factors(index, values, a_ref, b_ref, k):
    columns = slice(k * LANES, (k + 1) * LANES)
    i128 = iota((LANES, LANES), 0).astype(F32).astype(BF16)
    i16 = iota((16, LANES), 0).astype(F32).astype(BF16)
    lane = jnp.broadcast_to((index & (LANES - 1)).astype(F32), (LANES, LANES)).astype(BF16)
    row = jnp.broadcast_to((index >> 7).astype(F32), (16, LANES)).astype(BF16)
    one, zero = jnp.ones((LANES, LANES), BF16), jnp.zeros((LANES, LANES), BF16)
    b_ref[:, columns] = jnp.where(i128 == lane, one, zero)
    here = i16 == row
    zero16 = jnp.zeros((16, LANES), BF16)
    tail = zero16
    for c in range(3):
        high = values[c].astype(BF16).astype(F32)
        for s, part in enumerate((high, values[c] - high)):
            wide = jnp.broadcast_to(part, (16, LANES)).astype(BF16)
            q = (s * 3 + c) * MAIN
            a_ref[q : q + MAIN, columns] = jnp.where(here, wide, zero16)
            tail = jnp.where(i16 == jnp.full((16, LANES), c + 8 * s, BF16), wide, tail)
    a_ref[6 * MAIN :, columns] = jnp.where(row == jnp.full((16, LANES), MAIN, BF16), tail, zero16)


def factor_product(a_ref, b_ref, rows):
    return lax.dot_general(
        a_ref[:, : rows * LANES], b_ref[:, : rows * LANES], NT, preferred_element_type=F32
    )


def scatter(count, index_row, value_rows, a_ref, b_ref):
    def body(j, total):
        for k in range(CHUNK):
            r = j * CHUNK + k
            scatter_factors(index_row(r), value_rows(r), a_ref, b_ref, k)
        return total + factor_product(a_ref, b_ref, CHUNK)

    return lax.fori_loop(0, count // CHUNK, body, jnp.zeros((FACTOR_ROWS, LANES), F32))


def factor_sum(total):
    m = 3 * MAIN
    return jnp.concatenate([total[:m] + total[m : 2 * m], total[2 * m : 2 * m + 8] + total[2 * m + 8 :]], axis=0)


def pair_slots(owner_col, owner_row, cap):
    n = owner_row.shape[1]
    same = (owner_col == owner_row) & (iota((n, n), 0) < iota((n, n), 1))
    return jnp.sum(same.astype(F32), axis=0, keepdims=True)


def info_kernel(owner_col_ref, owner_row_ref, master_ref, normal_ref, out_ref, *, n_dom, cap):
    owner = owner_row_ref[...]
    n = owner.shape[1]
    rank = pair_slots(owner_col_ref[...], owner, cap)
    at = (iota((n_dom, n), 0) == owner).astype(F32)
    q = iota((4 * cap, n), 0)
    which = lax.div(q, cap)
    value = jnp.broadcast_to(master_ref[...].astype(F32), q.shape)
    for c in range(3):
        value = jnp.where(which == c, jnp.broadcast_to(normal_ref[c : c + 1, :], q.shape), value)
    value = jnp.where(lax.rem(q, cap).astype(F32) == rank, value, 0.0)
    out_ref[...] = dot_exact(at, value, NT)


def slave_side(owner_col_ref, owner_row_ref, slave_ref, normal_ref, patches, cap):
    owner = owner_row_ref[...]
    n = owner.shape[1]
    slot = owner.astype(F32) * cap + pair_slots(owner_col_ref[...], owner, cap)
    rho = iota((2 * SLOTS, n), 0)
    mine = (lax.div(rho, 2 * cap) * cap + lax.rem(rho, cap)).astype(F32)
    place = (mine == slot).astype(F32)
    hit = iota((patches, n), 0) == slave_ref[...]
    parts = [jnp.where(hit, jnp.broadcast_to(-normal_ref[c : c + 1, :], hit.shape), 0.0) for c in range(3)]
    parts.append(jnp.where(hit, -1.0, 0.0))
    return dot_exact(place, jnp.concatenate(parts, axis=0), NT)


def master_side(info, patches, n_dom, cap):
    rho = iota((2 * SLOTS, n_dom), 0)
    source = (lax.div(rho, 2 * cap) == iota((2 * SLOTS, n_dom), 1)).astype(F32)
    taken = dot_exact(source, info, NN)
    q = iota(taken.shape, 1)
    taken = jnp.where(lax.rem(q, cap) == lax.rem(iota(taken.shape, 0), cap), taken, 0.0)
    f = lax.div(iota((4 * cap, 3 * patches), 0), cap)
    normal = dot_exact(taken, (f == lax.div(iota(f.shape, 1), patches)).astype(F32), NN)
    master = dot_exact(taken, (f == 3).astype(F32), NN)
    column = lax.rem(iota(normal.shape, 1), patches).astype(F32)
    return jnp.where(jnp.abs(master - column) < 0.5, normal, 0.0)


def prepare_kernel(
    owner_col_ref, owner_row_ref, slave_ref, normal_ref, u_ref, v_ref, mass_ref, side_ref, fu_ref, fv_ref, fm_ref, *, patches, cap
):
    side_ref[...] = slave_side(owner_col_ref, owner_row_ref, slave_ref, normal_ref, patches, cap)
    to_field(u_ref, fu_ref)
    to_field(v_ref, fv_ref)
    fm_ref[...] = jnp.ones_like(fm_ref)
    for c in range(3):
        for h in range(MAIN + 1):
            r = field_row(c, h)
            fm_ref[r : r + 1, :] = mass_ref[0:1, h * LANES : (h + 1) * LANES]


def matrices_kernel(info_ref, side_ref, send_ref, keep_ref, *, masters, n_dom, cap):
    side = side_ref[...]
    owned = master_side(info_ref[...], masters, n_dom, cap)
    whole = jnp.concatenate([owned, side], axis=1)
    half = lax.rem(lax.div(iota(whole.shape, 0), cap), 2)
    right = jnp.where(iota(whole.shape, 1) < owned.shape[1], 0, 1)
    send_ref[...] = jnp.where(half == right, whole, 0.0)
    keep_ref[...] = jnp.where(half == right, 0.0, whole)


def pair_values(u_ref, snodes_ref, mnodes_ref, gap_ref, mortar_ref, x_ref, um_ref):
    masters, slaves = mnodes_ref.shape[0], snodes_ref.shape[0]

    def master_body(j, _):
        found = gather8(u_ref, mnodes_ref[pl.ds(j * 8, 8), :])
        for c in range(3):
            um_ref[pl.ds(c * masters + j * 8, 8), :] = found[c]
        return 0

    def slave_body(j, _):
        found = gather8(u_ref, snodes_ref[pl.ds(j * 8, 8), :])
        for c in range(3):
            x_ref[pl.ds(3 * masters + c * slaves + j * 8, 8), :] = found[c]
        return 0

    lax.fori_loop(0, masters // 8, master_body, 0, unroll=2)
    lax.fori_loop(0, slaves // 8, slave_body, 0, unroll=4)
    x_ref[: 3 * masters, :] = dot_exact(um_ref[...], mortar_ref[...], NT)
    x_ref[3 * (masters + slaves) :, :] = gap_ref[...]


def first_kernel(u_ref, snodes_ref, mnodes_ref, gap_ref, mortar_ref, send_ref, x_ref, out_ref, um_ref):
    pair_values(u_ref, snodes_ref, mnodes_ref, gap_ref, mortar_ref, x_ref, um_ref)
    out_ref[...] = dot_exact(send_ref[...], x_ref[...], NN)


def elastic_kernel(u_ref, conn_ref, modulus_ref, stiff_ref, keep_ref, x_ref, out_ref, kept_ref, ue_ref, idx_ref, a_ref, b_ref):
    kept_ref[...] = dot_exact(keep_ref[...], x_ref[...], NN)
    tiles = conn_ref.shape[1] // LANES

    def gather_body(j, _):
        columns = pl.ds(pl.multiple_of(j * LANES, LANES), LANES)
        index = conn_ref[:, columns]
        idx_ref[pl.ds(j * 8, 8), :] = index
        found = gather8(u_ref, index)
        for c in range(3):
            ue_ref[c * 8 : (c + 1) * 8, columns] = found[c]
        return 0

    lax.fori_loop(0, tiles, gather_body, 0, unroll=4)
    ue_ref[...] = dot_exact(stiff_ref[...], ue_ref[...], NN) * modulus_ref[...]

    def body(t, total):
        for k in range(CHUNK):
            j, a = t * (CHUNK // 8) + k // 8, k % 8
            columns = pl.ds(pl.multiple_of(j * LANES, LANES), LANES)
            values = [ue_ref[c * 8 + a : c * 8 + a + 1, columns] for c in range(3)]
            scatter_factors(idx_ref[pl.ds(t * CHUNK + k, 1), :], values, a_ref, b_ref, k)
        return total + factor_product(a_ref, b_ref, CHUNK)

    total = lax.fori_loop(0, tiles * 8 // CHUNK, body, jnp.zeros((FACTOR_ROWS, LANES), F32))
    out_ref[...] = factor_sum(total)


def contact_kernel(
    recv_ref, kept_ref, keep_ref, elastic_ref, snodes_ref, faces_ref, mortar_ref,
    local_ref, fa_ref, fb_ref, mf_ref, y_ref, a_ref, b_ref, *, masters,
):
    slaves = snodes_ref.shape[0]
    press = jnp.maximum(recv_ref[...] + kept_ref[...], 0.0)
    used = 3 * (masters + slaves)
    y_ref[...] = dot_exact(keep_ref[:, :used], press, TN)
    total = scatter(
        slaves,
        lambda r: snodes_ref[pl.ds(r, 1), :],
        lambda r: [y_ref[pl.ds(3 * masters + c * slaves + r, 1), :] for c in range(3)],
        a_ref,
        b_ref,
    )
    local_ref[...] = elastic_ref[...] + factor_sum(total)
    found = gather8(local_ref, faces_ref[...])
    for c in range(3):
        fa_ref[c, :, :] = found[c][:4]
        fb_ref[c, :, :] = found[c][4:]
    mf_ref[...] = dot_exact(y_ref[: 3 * masters, :], mortar_ref[...], NN)


def master_kernel(local_ref, mf_ref, mnodes_ref, out_ref, a_ref, b_ref):
    masters = mnodes_ref.shape[0]
    total = scatter(
        masters,
        lambda r: mnodes_ref[pl.ds(r, 1), :],
        lambda r: [mf_ref[pl.ds(c * masters + r, 1), :] for c in range(3)],
        a_ref,
        b_ref,
    )
    out_ref[...] = local_ref[...] + factor_sum(total)


def advance(negforce_ref, ra_ref, rb_ref, faces_ref, u_ref, v_ref, mass_ref, a_ref, b_ref):
    for k in range(8):
        r_ref = ra_ref if k < 4 else rb_ref
        values = [r_ref[c, k % 4 : k % 4 + 1, :] for c in range(3)]
        scatter_factors(faces_ref[k : k + 1, :], values, a_ref, b_ref, k)
    force = negforce_ref[...] + factor_sum(factor_product(a_ref, b_ref, 8))
    v = v_ref[...] - TIME_STEP * force / mass_ref[...]
    return u_ref[...] + TIME_STEP * v, v


def next_kernel(
    negforce_ref, ra_ref, rb_ref, faces_ref, u_ref, v_ref, mass_ref, snodes_ref, mnodes_ref, gap_ref, mortar_ref, send_ref,
    nu_ref, nv_ref, x_ref, out_ref, um_ref, a_ref, b_ref,
):
    u, v = advance(negforce_ref, ra_ref, rb_ref, faces_ref, u_ref, v_ref, mass_ref, a_ref, b_ref)
    nu_ref[...] = u
    nv_ref[...] = v
    pair_values(nu_ref, snodes_ref, mnodes_ref, gap_ref, mortar_ref, x_ref, um_ref)
    out_ref[...] = dot_exact(send_ref[...], x_ref[...], NN)


def last_kernel(negforce_ref, ra_ref, rb_ref, faces_ref, u_ref, v_ref, mass_ref, nu_ref, nv_ref, a_ref, b_ref):
    u, v = advance(negforce_ref, ra_ref, rb_ref, faces_ref, u_ref, v_ref, mass_ref, a_ref, b_ref)
    from_field(u, nu_ref)
    from_field(v, nv_ref)


def call(kernel, outs, args, scratch=(), us=1.0):
    vmem = pl.BlockSpec(memory_space=pltpu.VMEM)
    return pl.pallas_call(
        kernel,
        out_shape=[jax.ShapeDtypeStruct(s, F32) for s in outs],
        in_specs=[vmem] * len(args),
        out_specs=[vmem] * len(outs),
        scratch_shapes=list(scratch),
        compiler_params=pltpu.CompilerParams(vmem_limit_bytes=40 << 20),
        cost_estimate=pl.CostEstimate(flops=int(us * 1e9), bytes_accessed=int(us * 3e6), transcendentals=0),
    )(*args)


def shards(
    displacement,
    velocity,
    node_mass,
    connectivity,
    modulus,
    elem_stiffness,
    slave_nodes,
    slave_gap,
    master_nodes,
    pair_slave,
    pair_owner,
    pair_master,
    pair_normal,
    lower_face,
    upper_face,
    mortar,
):
    n_dom = lax.axis_size("dom")
    cap = SLOTS // n_dom
    slaves, masters = slave_nodes.shape[0], master_nodes.shape[0]
    elements = connectivity.shape[1]
    width = 3 * masters + 4 * slaves
    owner_row = pair_owner.reshape(1, -1)
    even = lax.axis_index("dom") % 2 == 0
    faces = jnp.concatenate(
        [jnp.where(even, upper_face, lower_face), jnp.where(even, lower_face, upper_face)]
    ).reshape(8, LANES)
    inside = [(i, i ^ 1) for i in range(n_dom)]
    across = [(i, i + 1) for i in range(1, n_dom - 1, 2)]
    across = across + [(j, i) for i, j in across]
    factors = (pltpu.VMEM((FACTOR_ROWS, CHUNK * LANES), BF16), pltpu.VMEM((LANES, CHUNK * LANES), BF16))

    (info,) = call(
        functools.partial(info_kernel, n_dom=n_dom, cap=cap),
        [(n_dom, 4 * cap)],
        (pair_owner, owner_row, pair_master.reshape(1, -1), pair_normal),
    )
    info = lax.all_to_all(info, "dom", 0, 0, tiled=True)
    side, u, v, mass = call(
        functools.partial(prepare_kernel, patches=slaves, cap=cap),
        [(2 * SLOTS, 4 * slaves)] + [(ROWS, LANES)] * 3,
        (pair_owner, owner_row, pair_slave.reshape(1, -1), pair_normal, displacement, velocity, node_mass.reshape(1, -1)),
    )
    send, keep = call(
        functools.partial(matrices_kernel, masters=masters, n_dom=n_dom, cap=cap), [(2 * SLOTS, width)] * 2, (info, side)
    )
    patch_scratch = pltpu.VMEM((3 * masters, LANES), F32)
    x, out = call(
        first_kernel,
        [(width, LANES), (2 * SLOTS, LANES)],
        (u, slave_nodes, master_nodes, slave_gap, mortar, send),
        [patch_scratch],
    )
    for step in range(STEPS):
        recv = lax.all_to_all(out.reshape(n_dom, 2 * cap, LANES), "dom", 0, 0).reshape(2 * SLOTS, LANES)
        elastic, kept = call(
            elastic_kernel,
            [(ROWS, LANES), (2 * SLOTS, LANES)],
            (u, connectivity, modulus.reshape(1, -1), elem_stiffness, keep, x),
            [pltpu.VMEM((24, elements), F32), pltpu.VMEM((8 * elements // LANES, LANES), jnp.int32), *factors],
            us=6.0,
        )
        local, fa, fb, mf = call(
            functools.partial(contact_kernel, masters=masters),
            [(ROWS, LANES), (3, 4, LANES), (3, 4, LANES), (3 * masters, LANES)],
            (recv, kept, keep, elastic, slave_nodes, faces, mortar),
            [pltpu.VMEM((3 * (masters + slaves), LANES), F32), *factors],
            us=3.0,
        )
        ra = lax.ppermute(fa, "dom", inside)
        rb = lax.ppermute(fb, "dom", across)
        (negforce,) = call(master_kernel, [(ROWS, LANES)], (local, mf, master_nodes), factors)
        state = (negforce, ra, rb, faces, u, v, mass)
        if step < STEPS - 1:
            u, v, x, out = call(
                next_kernel,
                [(ROWS, LANES), (ROWS, LANES), (width, LANES), (2 * SLOTS, LANES)],
                (*state, slave_nodes, master_nodes, slave_gap, mortar, send),
                [patch_scratch, *factors],
                us=3.0,
            )
        else:
            u, v = call(last_kernel, [displacement.shape, velocity.shape], state, factors)
    return (u, v)


def solution(mesh):
    return jax.shard_map(
        shards,
        mesh=mesh,
        in_specs=(
            P(None, ("groups", "dom")),
            P(None, ("groups", "dom")),
            P(("groups", "dom")),
            P(None, ("groups", "dom")),
            P(("groups", "dom")),
            P(),
            P(("groups", "dom"), None),
            P(("groups", "dom"), None),
            P(("groups", "dom"), None),
            P(("groups", "dom")),
            P(("groups", "dom"), None),
            P(("groups", "dom")),
            P(None, ("groups", "dom")),
            P(("groups", "dom")),
            P(("groups", "dom")),
            P(),
        ),
        out_specs=(P(None, ("groups", "dom")), P(None, ("groups", "dom"))),
        check_vma=False,
    )
```

time: 1270 us -> 93 us (0.07)
  other arithmetic: 629 us -> 0.01 us
  local copies, waits for them, and re-layouts: 449 us -> 2.15 us
  blocking collectives: 70.1 us -> 0 us
  waiting for transfers between devices: 83.8 us -> 20.1 us
  Pallas kernels: 0 us -> 42 us
  between operations: 16 us -> 0.92 us
  starting transfers between devices: 13.5 us -> 27.1 us
    scatter-add x18 -> x0, other arithmetic: 613 us -> none  [the longest x3 266 us: shards(): local.at[:, s_nodes.reshape(-1)]]
    gather x29 -> x0, local copies, waits for them, and re-layouts: 414 us -> none  [the longest x6 180 us: shards(): us = jnp.moveaxis(u[:, s_nodes], 0, 1)]
    unnamed x6 -> x0, waiting for transfers between devices: 80.9 us -> none
    all_gather x3 -> x0, blocking collectives: 70.1 us -> none  [shards(): table = lax.all_gather(own, 'dom', axis=0, tiled=True)]
    pallas_call x0 -> x16, Pallas kernels: none -> 42 us  [call(): pl.pallas_call(kernel, out_shape=[jax.ShapeDtypeStruct(s, F32) for s in o...]
    reshape x12 -> x1, local copies, waits for them, and re-layouts: 23 us -> 0.01 us  [shards(): node_mass.reshape(1, -1)]
    all_to_all x0 -> x4, starting transfers between devices: none -> 18.6 us  [the longest x3 11.2 us: shards(): lax.all_to_all(out.reshape(n_dom, 2 * cap, LANES), 'dom', 0, 0)]
    all_to_all x0 -> x4, waiting for transfers between devices: none -> 14.3 us  [the longest x3 10.1 us: shards(): lax.all_to_all(out.reshape(n_dom, 2 * cap, LANES), 'dom', 0, 0)]
  transfers between devices with their start and end apart: 9 -> 10, of which waited for: 5 -> 7; matrix products, arithmetic and copies ran while one was open for 41% -> 0% of each run, Pallas kernels for 0% -> 24%
where the time goes in v1:
time: 93 us; the launch traced here: 92.3 us
  Pallas kernels  42 us (45%)
  starting transfers between devices  27.1 us (29%)
  waiting for transfers between devices  20.1 us (22%)
  local copies, waits for them, and re-layouts  2.15 us (2%)
    pallas_call x16, Pallas kernels, call(): pl.pallas_call(kernel, out_shape=[jax.ShapeDtypeStruct(s, F32) for s in o...  42 us
    all_to_all x3, starting transfers between devices, shards(): lax.all_to_all(out.reshape(n_dom, 2 * cap, LANES), 'dom', 0, 0)  11.2 us
    all_to_all x3, waiting for transfers between devices, shards(): lax.all_to_all(out.reshape(n_dom, 2 * cap, LANES), 'dom', 0, 0)  10.1 us
    all_to_all x1, starting transfers between devices, shards(): info = lax.all_to_all(info, 'dom', 0, 0, tiled=True)  7.48 us
    ppermute x3, starting transfers between devices, shards(): rb = lax.ppermute(fb, 'dom', across)  6.27 us
    ppermute x3, waiting for transfers between devices, shards(): rb = lax.ppermute(fb, 'dom', across)  5.73 us
    all_to_all x1, waiting for transfers between devices, shards(): info = lax.all_to_all(info, 'dom', 0, 0, tiled=True)  4.27 us
    ppermute x3, starting transfers between devices, shards(): ra = lax.ppermute(fa, 'dom', inside)  2.17 us
  transfers between devices with their start and end apart: 10, of which 7 were waited for; matrix products, arithmetic and copies ran while one was open for 0% of the time, Pallas kernels for 24%

profile of v1, /device:TPU:1, one launch (start us, length us, event | category | flops | bytes accessed | tf_op | source)
XLA Modules:
  0.0 92.3 jit_solution(4975414255639768687)
XLA Ops:
  0.6 0.8 copy.20.owner_col_ref
  1.4 0.0 copy-start
  1.4 0.0 copy-start.11
  1.4 0.7 copy-done.10
  2.1 0.9 shard_map.168
  2.9 7.5 %all-to-all-start = ((f32[16,1,64]{2,1,0:T(1,128)}), f32[16,1,64]{2,1,0:T(1,128)S(1)}, u32[]{:S(2)}, u32[]{:S(2)}) async-start(f32[16,1,64]{2,1,0:T(1,128)} %bitcast.4), calls=%async_computation | async-start | bytes 16384 | tf_op jit(solution)/shard_map/all_to_all | solution.py:347
  10.4 0.0 copy-start.3
  10.5 0.0 copy-done.14
  10.5 0.0 copy-done.15
  10.5 0.0 copy-start.12
  10.5 0.6 copy-done.4
  11.2 0.0 copy-done.3
  11.2 0.0 copy-done.12
  11.2 0.6 shard_map.167
  11.9 4.3 %all-to-all-done = f32[16,1,64]{2,1,0:T(1,128)S(1)} async-done(((f32[16,1,64]{2,1,0:T(1,128)}), f32[16,1,64]{2,1,0:T(1,128)S(1)}, u32[]{:S(2)}, u32[]{:S(2)}) %all-to-all-start) | async-done | bytes 4128 | tf_op jit(solution)/shard_map/all_to_all | solution.py:347
  16.1 0.9 shard_map.169
  17.0 2.8 %shard_map.170 = (f32[352,128]{1,0:T(8,128)S(1)}, f32[512,128]{1,0:T(8,128)}) custom-call(f32[56,128]{1,0:T(8,128)S(1)} %get-tuple-element.36.u_ref, s32[64,128]{1,0:T(8,128)S(1)} %copy-done.6, s32[32,128]{1,0:T(8,128)S(1)} %copy-done.7, f32[64,128]{1,0:T(8,128)S(1)} %copy-done.5, f32[128,128]{1,0:T(8,128)S(1)} %copy-done.2, ...), custom_call_target="tpu_custom_call" | custom-call | flops 1000000000 | bytes 3000000 | tf_op jit(solution)/shard_map/pallas_call | solution.py:298
  19.9 4.2 %all-to-all-start.1 = ((f32[16,32,128]{2,1,0:T(8,128)}), f32[16,32,128]{2,1,0:T(8,128)S(1)}, u32[]{:S(2)}, u32[]{:S(2)}) async-start(f32[16,32,128]{2,1,0:T(8,128)} %bitcast.6), calls=%async_computation.1 | async-start | bytes 524288 | tf_op jit(solution)/shard_map/all_to_all | solution.py:364
  24.1 0.0 copy-done.1
  24.1 6.1 %shard_map.171 = (f32[56,128]{1,0:T(8,128)S(1)}, f32[512,128]{1,0:T(8,128)S(1)}) custom-call(f32[56,128]{1,0:T(8,128)S(1)} %get-tuple-element.36.u_ref, s32[8,2048]{1,0:T(8,128)S(1)} %copy-done.1, f32[1,2048]{1,0:T(1,128)S(1)} %bitcast.24, f32[24,24]{1,0:T(8,128)S(1)} %copy-done.8, f32[512,352]{1,0:T(8,128)S(1)} %get-tuple-element.40.keep_ref, ...), custom_call_target="tpu_custom_call" | custom-call | flops 6000000000 | bytes 18000000 | tf_op jit(solution)/shard_map/pallas_call | solution.py:298
  30.2 3.4 %all-to-all-done.1 = f32[16,32,128]{2,1,0:T(8,128)S(1)} async-done(((f32[16,32,128]{2,1,0:T(8,128)}), f32[16,32,128]{2,1,0:T(8,128)S(1)}, u32[]{:S(2)}, u32[]{:S(2)}) %all-to-all-start.1) | async-done | bytes 262176 | tf_op jit(solution)/shard_map/all_to_all | solution.py:364
  33.6 2.8 %shard_map.172 = (f32[56,128]{1,0:T(8,128)S(1)}, f32[3,4,128]{2,1,0:T(4,128)S(1)}, f32[3,4,128]{2,1,0:T(4,128)S(1)}, f32[96,128]{1,0:T(8,128)S(1)}) custom-call(f32[512,128]{1,0:T(8,128)S(1)} %bitcast.18, f32[512,128]{1,0:T(8,128)S(1)} %get-tuple-element.42.kept_ref, f32[512,352]{1,0:T(8,128)S(1)} %get-tuple-element.40.keep_ref, ...), custom_call_target="tpu_custom_call" | custom-call | flops 3000000000 | bytes 9000000 | tf_op jit(solution)/shard_map/pallas_call | solution.py:298
  36.4 0.7 collective-permute-start
  37.2 2.0 %collective-permute-start.1 = (f32[3,4,128]{2,1,0:T(4,128)S(1)}, f32[3,4,128]{2,1,0:T(4,128)S(1)}, u32[]{:S(2)}, u32[]{:S(2)}) collective-permute-start(f32[3,4,128]{2,1,0:T(4,128)S(1)} %get-tuple-element.47), channel_id=1, source_target_pairs={{1,2},{3,4},{5,6},{7,8},{9,10},{11,12},{13,14},{2,1},{4,3},{6,5},{... | collective-permute-start | bytes 18440 | tf_op jit(solution)/shard_map/ppermute | solution.py:380
  39.2 0.9 shard_map.173.negforce_ref
  40.1 0.0 collective-permute-done.ra_ref
  40.1 2.0 %collective-permute-done.1.rb_ref = f32[3,4,128]{2,1,0:T(4,128)S(1)} collective-permute-done((f32[3,4,128]{2,1,0:T(4,128)S(1)}, f32[3,4,128]{2,1,0:T(4,128)S(1)}, u32[]{:S(2)}, u32[]{:S(2)}) %collective-permute-start.1) | collective-permute-done | bytes 6176 | tf_op jit(solution)/shard_map/ppermute | solution.py:380
  42.1 3.1 %shard_map.174 = (f32[56,128]{1,0:T(8,128)S(1)}, f32[56,128]{1,0:T(8,128)S(1)}, f32[352,128]{1,0:T(8,128)S(1)}, f32[512,128]{1,0:T(8,128)}) custom-call(f32[56,128]{1,0:T(8,128)S(1)} %shard_map.173.negforce_ref, f32[3,4,128]{2,1,0:T(4,128)S(1)} %collective-permute-done.ra_ref, f32[3,4,128]{2,1,0:T(4,128)S(1)} %collective-permute-done.1.rb_ref, ...), custom_call_target="tpu_custom_call" | custom-call | flops 3000000000 | bytes 9000000 | tf_op jit(solution)/shard_map/pallas_call | solution.py:298
  45.3 3.5 %all-to-all-start.2 = ((f32[16,32,128]{2,1,0:T(8,128)}), f32[16,32,128]{2,1,0:T(8,128)S(1)}, u32[]{:S(2)}, u32[]{:S(2)}) async-start(f32[16,32,128]{2,1,0:T(8,128)} %bitcast.11), calls=%async_computation.2 | async-start | bytes 524288 | tf_op jit(solution)/shard_map/all_to_all | solution.py:364
  48.7 6.1 %shard_map.175 = (f32[56,128]{1,0:T(8,128)S(1)}, f32[512,128]{1,0:T(8,128)S(1)}) custom-call(f32[56,128]{1,0:T(8,128)S(1)} %get-tuple-element.51.u_ref, s32[8,2048]{1,0:T(8,128)S(1)} %copy-done.1, f32[1,2048]{1,0:T(1,128)S(1)} %bitcast.25, f32[24,24]{1,0:T(8,128)S(1)} %copy-done.8, f32[512,352]{1,0:T(8,128)S(1)} %get-tuple-element.40.keep_ref, ...), custom_call_target="tpu_custom_call" | custom-call | flops 6000000000 | bytes 18000000 | tf_op jit(solution)/shard_map/pallas_call | solution.py:298
  54.9 3.3 %all-to-all-done.2 = f32[16,32,128]{2,1,0:T(8,128)S(1)} async-done(((f32[16,32,128]{2,1,0:T(8,128)}), f32[16,32,128]{2,1,0:T(8,128)S(1)}, u32[]{:S(2)}, u32[]{:S(2)}) %all-to-all-start.2) | async-done | bytes 262176 | tf_op jit(solution)/shard_map/all_to_all | solution.py:364
  58.2 2.8 %shard_map.176 = (f32[56,128]{1,0:T(8,128)S(1)}, f32[3,4,128]{2,1,0:T(4,128)S(1)}, f32[3,4,128]{2,1,0:T(4,128)S(1)}, f32[96,128]{1,0:T(8,128)S(1)}) custom-call(f32[512,128]{1,0:T(8,128)S(1)} %bitcast.20, f32[512,128]{1,0:T(8,128)S(1)} %get-tuple-element.53.kept_ref, f32[512,352]{1,0:T(8,128)S(1)} %get-tuple-element.40.keep_ref, ...), custom_call_target="tpu_custom_call" | custom-call | flops 3000000000 | bytes 9000000 | tf_op jit(solution)/shard_map/pallas_call | solution.py:298
  61.0 0.7 collective-permute-start.2
  61.8 2.2 %collective-permute-start.3 = (f32[3,4,128]{2,1,0:T(4,128)S(1)}, f32[3,4,128]{2,1,0:T(4,128)S(1)}, u32[]{:S(2)}, u32[]{:S(2)}) collective-permute-start(f32[3,4,128]{2,1,0:T(4,128)S(1)} %get-tuple-element.58), channel_id=1, source_target_pairs={{1,2},{3,4},{5,6},{7,8},{9,10},{11,12},{13,14},{2,1},{4,3},{6,5},{... | collective-permute-start | bytes 18440 | tf_op jit(solution)/shard_map/ppermute | solution.py:380
  64.0 0.9 shard_map.177.negforce_ref
  64.9 0.0 collective-permute-done.2.ra_ref
  64.9 1.8 %collective-permute-done.3.rb_ref = f32[3,4,128]{2,1,0:T(4,128)S(1)} collective-permute-done((f32[3,4,128]{2,1,0:T(4,128)S(1)}, f32[3,4,128]{2,1,0:T(4,128)S(1)}, u32[]{:S(2)}, u32[]{:S(2)}) %collective-permute-start.3) | collective-permute-done | bytes 6176 | tf_op jit(solution)/shard_map/ppermute | solution.py:380
  66.7 3.1 %shard_map.178 = (f32[56,128]{1,0:T(8,128)S(1)}, f32[56,128]{1,0:T(8,128)S(1)}, f32[352,128]{1,0:T(8,128)S(1)}, f32[512,128]{1,0:T(8,128)}) custom-call(f32[56,128]{1,0:T(8,128)S(1)} %shard_map.177.negforce_ref, f32[3,4,128]{2,1,0:T(4,128)S(1)} %collective-permute-done.2.ra_ref, f32[3,4,128]{2,1,0:T(4,128)S(1)} %collective-permute-done.3.rb_ref, ...), custom_call_target="tpu_custom_call" | custom-call | flops 3000000000 | bytes 9000000 | tf_op jit(solution)/shard_map/pallas_call | solution.py:298
  69.8 3.5 %all-to-all-start.3 = ((f32[16,32,128]{2,1,0:T(8,128)}), f32[16,32,128]{2,1,0:T(8,128)S(1)}, u32[]{:S(2)}, u32[]{:S(2)}) async-start(f32[16,32,128]{2,1,0:T(8,128)} %bitcast.13), calls=%async_computation.3 | async-start | bytes 524288 | tf_op jit(solution)/shard_map/all_to_all | solution.py:364
  73.4 6.1 %shard_map.179 = (f32[56,128]{1,0:T(8,128)S(1)}, f32[512,128]{1,0:T(8,128)S(1)}) custom-call(f32[56,128]{1,0:T(8,128)S(1)} %get-tuple-element.61.u_ref, s32[8,2048]{1,0:T(8,128)S(1)} %copy-done.1, f32[1,2048]{1,0:T(1,128)S(1)} %bitcast.26, f32[24,24]{1,0:T(8,128)S(1)} %copy-done.8, f32[512,352]{1,0:T(8,128)S(1)} %get-tuple-element.40.keep_ref, ...), custom_call_target="tpu_custom_call" | custom-call | flops 6000000000 | bytes 18000000 | tf_op jit(solution)/shard_map/pallas_call | solution.py:298
  79.5 3.3 %all-to-all-done.3 = f32[16,32,128]{2,1,0:T(8,128)S(1)} async-done(((f32[16,32,128]{2,1,0:T(8,128)}), f32[16,32,128]{2,1,0:T(8,128)S(1)}, u32[]{:S(2)}, u32[]{:S(2)}) %all-to-all-start.3) | async-done | bytes 262176 | tf_op jit(solution)/shard_map/all_to_all | solution.py:364
  82.9 2.8 %shard_map.180 = (f32[56,128]{1,0:T(8,128)S(1)}, f32[3,4,128]{2,1,0:T(4,128)S(1)}, f32[3,4,128]{2,1,0:T(4,128)S(1)}, f32[96,128]{1,0:T(8,128)S(1)}) custom-call(f32[512,128]{1,0:T(8,128)S(1)} %bitcast.19, f32[512,128]{1,0:T(8,128)S(1)} %get-tuple-element.63.kept_ref, f32[512,352]{1,0:T(8,128)S(1)} %get-tuple-element.40.keep_ref, ...), custom_call_target="tpu_custom_call" | custom-call | flops 3000000000 | bytes 9000000 | tf_op jit(solution)/shard_map/pallas_call | solution.py:298
  85.7 0.7 collective-permute-start.4
  86.4 2.0 %collective-permute-start.5 = (f32[3,4,128]{2,1,0:T(4,128)S(1)}, f32[3,4,128]{2,1,0:T(4,128)S(1)}, u32[]{:S(2)}, u32[]{:S(2)}) collective-permute-start(f32[3,4,128]{2,1,0:T(4,128)S(1)} %get-tuple-element.68), channel_id=1, source_target_pairs={{1,2},{3,4},{5,6},{7,8},{9,10},{11,12},{13,14},{2,1},{4,3},{6,5},{... | collective-permute-start | bytes 18440 | tf_op jit(solution)/shard_map/ppermute | solution.py:380
  88.5 0.9 shard_map.181.negforce_ref
  89.4 0.0 collective-permute-done.4.ra_ref
  89.4 2.0 %collective-permute-done.5.rb_ref = f32[3,4,128]{2,1,0:T(4,128)S(1)} collective-permute-done((f32[3,4,128]{2,1,0:T(4,128)S(1)}, f32[3,4,128]{2,1,0:T(4,128)S(1)}, u32[]{:S(2)}, u32[]{:S(2)}) %collective-permute-start.5) | collective-permute-done | bytes 6176 | tf_op jit(solution)/shard_map/ppermute | solution.py:380
  91.3 0.9 %shard_map.182 = (f32[3,2176]{1,0:T(4,128)}, f32[3,2176]{1,0:T(4,128)}) custom-call(f32[56,128]{1,0:T(8,128)S(1)} %shard_map.181.negforce_ref, f32[3,4,128]{2,1,0:T(4,128)S(1)} %collective-permute-done.4.ra_ref, f32[3,4,128]{2,1,0:T(4,128)S(1)} %collective-permute-done.5.rb_ref, s32[8,128]{1,0:T(8,128)S(1)} %pad_add_fusion.faces_ref, ...), custom_call_target="tpu_custom_call" | custom-call | flops 1000000000 | bytes 3000000 | tf_op jit(solution)/shard_map/pallas_call | solution.py:298
  (24 shorter events, 0.1 us)
Async XLA Ops:
  1.4 0.7 copy-start.10
  1.4 0.7 copy-start
  1.4 0.7 copy-start.11
  2.9 7.5 %copy-start.13 = (f32[2176]{0:T(1024)S(1)}, f32[2176]{0:T(1024)}, u32[]{:S(2)}) copy-start(f32[2176]{0:T(1024)} %param.18) | copy-start | bytes 26116
  2.9 7.5 %copy-start.14 = (s32[512]{0:T(512)S(1)}, s32[512]{0:T(512)}, u32[]{:S(2)}) copy-start(s32[512]{0:T(512)} %param.30) | copy-start | bytes 6148
  2.9 7.6 %copy-start.15 = (s32[512]{0:T(512)S(1)}, s32[512]{0:T(512)}, u32[]{:S(2)}) copy-start(s32[512]{0:T(512)} %param.29) | copy-start | bytes 6148
  2.9 13.2 %all-to-all-start = ((f32[16,1,64]{2,1,0:T(1,128)}), f32[16,1,64]{2,1,0:T(1,128)S(1)}, u32[]{:S(2)}, u32[]{:S(2)}) async-start(f32[16,1,64]{2,1,0:T(1,128)} %bitcast.4), calls=%async_computation | async-start | bytes 16384 | tf_op jit(solution)/shard_map/all_to_all | solution.py:347
  10.4 0.8 copy-start.4
  10.4 0.8 copy-start.3
  10.5 0.7 copy-start.12
  16.1 0.9 copy-start.2
  16.1 0.9 copy-start.5
  16.1 0.9 copy-start.6
  16.1 0.9 copy-start.7
  19.9 4.2 %copy-start.1 = (s32[8,2048]{1,0:T(8,128)S(1)}, s32[8,2048]{1,0:T(8,128)}, u32[]{:S(2)}) copy-start(s32[8,2048]{1,0:T(8,128)} %conn_ref.5) | copy-start | bytes 196612
  19.9 4.2 %copy-start.8 = (f32[24,24]{1,0:T(8,128)S(1)}, f32[24,24]{1,0:T(8,128)}, u32[]{:S(2)}) copy-start(f32[24,24]{1,0:T(8,128)} %stiff_ref.5) | copy-start | bytes 6916
  19.9 4.2 %copy-start.9 = (f32[2048]{0:T(1024)S(1)}, f32[2048]{0:T(1024)}, u32[]{:S(2)}) copy-start(f32[2048]{0:T(1024)} %param.20) | copy-start | bytes 24580
  19.9 13.7 %all-to-all-start.1 = ((f32[16,32,128]{2,1,0:T(8,128)}), f32[16,32,128]{2,1,0:T(8,128)S(1)}, u32[]{:S(2)}, u32[]{:S(2)}) async-start(f32[16,32,128]{2,1,0:T(8,128)} %bitcast.6), calls=%async_computation.1 | async-start | bytes 524288 | tf_op jit(solution)/shard_map/all_to_all | solution.py:364
  36.4 3.7 %collective-permute-start = (f32[3,4,128]{2,1,0:T(4,128)S(1)}, f32[3,4,128]{2,1,0:T(4,128)S(1)}, u32[]{:S(2)}, u32[]{:S(2)}) collective-permute-start(f32[3,4,128]{2,1,0:T(4,128)S(1)} %get-tuple-element.46), channel_id=1, source_target_pairs={{0,1},{1,0},{2,3},{3,2},{4,5},{5,4},{6,7},{7,6},{8,9},{9,8},{10,11... | collective-permute-start | bytes 18440 | tf_op jit(solution)/shard_map/ppermute | solution.py:379
  37.2 4.9 %collective-permute-start.1 = (f32[3,4,128]{2,1,0:T(4,128)S(1)}, f32[3,4,128]{2,1,0:T(4,128)S(1)}, u32[]{:S(2)}, u32[]{:S(2)}) collective-permute-start(f32[3,4,128]{2,1,0:T(4,128)S(1)} %get-tuple-element.47), channel_id=1, source_target_pairs={{1,2},{3,4},{5,6},{7,8},{9,10},{11,12},{13,14},{2,1},{4,3},{6,5},{... | collective-permute-start | bytes 18440 | tf_op jit(solution)/shard_map/ppermute | solution.py:380
  45.3 13.0 %all-to-all-start.2 = ((f32[16,32,128]{2,1,0:T(8,128)}), f32[16,32,128]{2,1,0:T(8,128)S(1)}, u32[]{:S(2)}, u32[]{:S(2)}) async-start(f32[16,32,128]{2,1,0:T(8,128)} %bitcast.11), calls=%async_computation.2 | async-start | bytes 524288 | tf_op jit(solution)/shard_map/all_to_all | solution.py:364
  61.0 3.9 %collective-permute-start.2 = (f32[3,4,128]{2,1,0:T(4,128)S(1)}, f32[3,4,128]{2,1,0:T(4,128)S(1)}, u32[]{:S(2)}, u32[]{:S(2)}) collective-permute-start(f32[3,4,128]{2,1,0:T(4,128)S(1)} %get-tuple-element.57), channel_id=1, source_target_pairs={{0,1},{1,0},{2,3},{3,2},{4,5},{5,4},{6,7},{7,6},{8,9},{9,8},{10,11... | collective-permute-start | bytes 18440 | tf_op jit(solution)/shard_map/ppermute | solution.py:379
  61.8 4.9 %collective-permute-start.3 = (f32[3,4,128]{2,1,0:T(4,128)S(1)}, f32[3,4,128]{2,1,0:T(4,128)S(1)}, u32[]{:S(2)}, u32[]{:S(2)}) collective-permute-start(f32[3,4,128]{2,1,0:T(4,128)S(1)} %get-tuple-element.58), channel_id=1, source_target_pairs={{1,2},{3,4},{5,6},{7,8},{9,10},{11,12},{13,14},{2,1},{4,3},{6,5},{... | collective-permute-start | bytes 18440 | tf_op jit(solution)/shard_map/ppermute | solution.py:380
  69.8 13.0 %all-to-all-start.3 = ((f32[16,32,128]{2,1,0:T(8,128)}), f32[16,32,128]{2,1,0:T(8,128)S(1)}, u32[]{:S(2)}, u32[]{:S(2)}) async-start(f32[16,32,128]{2,1,0:T(8,128)} %bitcast.13), calls=%async_computation.3 | async-start | bytes 524288 | tf_op jit(solution)/shard_map/all_to_all | solution.py:364
  85.7 3.7 %collective-permute-start.4 = (f32[3,4,128]{2,1,0:T(4,128)S(1)}, f32[3,4,128]{2,1,0:T(4,128)S(1)}, u32[]{:S(2)}, u32[]{:S(2)}) collective-permute-start(f32[3,4,128]{2,1,0:T(4,128)S(1)} %get-tuple-element.67), channel_id=1, source_target_pairs={{0,1},{1,0},{2,3},{3,2},{4,5},{5,4},{6,7},{7,6},{8,9},{9,8},{10,11... | collective-permute-start | bytes 18440 | tf_op jit(solution)/shard_map/ppermute | solution.py:379
  86.4 4.9 %collective-permute-start.5 = (f32[3,4,128]{2,1,0:T(4,128)S(1)}, f32[3,4,128]{2,1,0:T(4,128)S(1)}, u32[]{:S(2)}, u32[]{:S(2)}) collective-permute-start(f32[3,4,128]{2,1,0:T(4,128)S(1)} %get-tuple-element.68), channel_id=1, source_target_pairs={{1,2},{3,4},{5,6},{7,8},{9,10},{11,12},{13,14},{2,1},{4,3},{6,5},{... | collective-permute-start | bytes 18440 | tf_op jit(solution)/shard_map/ppermute | solution.py:380

commit v2 on v0

v2 whole, which is shorter than its diff:
```python
import functools

import jax
import jax.numpy as jnp
from jax import lax
from jax.experimental import pallas as pl
from jax.experimental.pallas import tpu as pltpu
from jax.sharding import PartitionSpec as P

LANES = 128
STEPS = 3
TIME_STEP = 0.1
SLOTS = 256
GROUP = 4

F32 = jnp.float32
BF16 = jnp.bfloat16
HIGH = lax.Precision.HIGHEST
NN = (((1,), (0,)), ((), ()))
NT = (((1,), (1,)), ((), ()))
TN = (((0,), (0,)), ((), ()))

MAIN = 16
ROWS = 56
FACTOR_ROWS = 112


def dot_exact(a, b, dims):
    return lax.dot_general(a, b, dims, precision=HIGH, preferred_element_type=F32)


def iota(shape, dim):
    return lax.broadcasted_iota(jnp.int32, shape, dim)


def field_row(c, h):
    return c * MAIN + h if h < MAIN else 3 * MAIN + c


def to_field(flat_ref, field_ref):
    field_ref[...] = jnp.zeros_like(field_ref)
    for c in range(3):
        for h in range(MAIN + 1):
            r = field_row(c, h)
            field_ref[r : r + 1, :] = flat_ref[c : c + 1, h * LANES : (h + 1) * LANES]


def from_field(field, flat_ref):
    for c in range(3):
        for h in range(MAIN + 1):
            r = field_row(c, h)
            flat_ref[c : c + 1, h * LANES : (h + 1) * LANES] = field[r : r + 1, :]


def gather8(field_ref, index):
    lane = index & (LANES - 1)
    row = index >> 7
    bits = [(row & (1 << q)) != 0 for q in range(4)]
    last = row >= MAIN
    found = []
    for c in range(3):
        values = []
        for h in range(MAIN + 1):
            r = field_row(c, h)
            table = jnp.broadcast_to(field_ref[r : r + 1, :], (8, LANES))
            values.append(jnp.take_along_axis(table, lane, axis=1, mode="promise_in_bounds"))
        tail = values.pop()
        for bit in bits:
            values = [jnp.where(bit, values[i + 1], values[i]) for i in range(0, len(values), 2)]
        found.append(jnp.where(last, tail, values[0]))
    return found


def value_factor(index, values):
    i16 = iota((MAIN, LANES), 0).astype(F32).astype(BF16)
    row = jnp.broadcast_to((index >> 7).astype(F32), (MAIN, LANES)).astype(BF16)
    zero = jnp.zeros((MAIN, LANES), BF16)
    here = i16 == row
    tail, out = zero, []
    for s in range(2):
        for c in range(3):
            high = values[c].astype(BF16).astype(F32)
            part = values[c] - high if s else high
            wide = jnp.broadcast_to(part, (MAIN, LANES)).astype(BF16)
            out.append(jnp.where(here, wide, zero))
            tail = jnp.where(i16 == jnp.full(i16.shape, c + 8 * s, BF16), wide, tail)
    out.append(jnp.where(row == jnp.full(row.shape, MAIN, BF16), tail, zero))
    return jnp.concatenate(out, axis=0)


def lane_factor(index):
    i128 = iota((LANES, LANES), 0).astype(F32).astype(BF16)
    lane = jnp.broadcast_to((index & (LANES - 1)).astype(F32), (LANES, LANES)).astype(BF16)
    return jnp.where(i128 == lane, jnp.ones((LANES, LANES), BF16), jnp.zeros((LANES, LANES), BF16))


def scatter(rows, total=None):
    for j in range(0, len(rows), GROUP):
        group = rows[j : j + GROUP]
        a = jnp.concatenate([value_factor(index, values) for index, values in group], axis=1)
        b = jnp.concatenate([lane_factor(index) for index, _ in group], axis=1)
        part = lax.dot_general(a, b, NT, preferred_element_type=F32)
        total = part if total is None else total + part
    return total


def factor_sum(total):
    m = 3 * MAIN
    return jnp.concatenate([total[:m] + total[m : 2 * m], total[2 * m : 2 * m + 8] + total[2 * m + 8 :]], axis=0)


def two_parts(x):
    high = x.astype(BF16)
    return high, (x - high.astype(F32)).astype(BF16)


def as_left(x, axis=1):
    high, low = two_parts(x)
    return jnp.concatenate([high, high, low], axis=axis)


def as_right(x, axis=0):
    high, low = two_parts(x)
    return jnp.concatenate([high, low, high], axis=axis)


def product(a, b):
    return lax.dot_general(a, b, NN, preferred_element_type=F32)


def take_slots(block_ref, half, cap):
    n_dom = block_ref.shape[0]
    rows = slice(half * cap, (half + 1) * cap)
    if cap % 8 == 0:
        return block_ref[:, rows, :].reshape(n_dom * cap, LANES)
    return jnp.concatenate([block_ref[o, rows, :] for o in range(n_dom)], axis=0)


def put_slots(block_ref, half, cap, value):
    n_dom = block_ref.shape[0]
    rows = slice(half * cap, (half + 1) * cap)
    if cap % 8 == 0:
        block_ref[:, rows, :] = value.reshape(n_dom, cap, LANES)
    else:
        for o in range(n_dom):
            block_ref[o, rows, :] = value[o * cap : (o + 1) * cap]


def ranks(owner):
    n = owner.shape[1]
    across = jnp.broadcast_to(owner.astype(F32), (n, n))
    same = (across.T == across) & (iota((n, n), 0) < iota((n, n), 1))
    return jnp.sum(same.astype(F32), axis=0, keepdims=True)


def info_kernel(owner_ref, master_ref, normal_ref, out_ref, *, n_dom, cap):
    owner = owner_ref[...]
    n = owner.shape[1]
    at = (iota((n_dom, n), 0) == owner).astype(F32)
    q = iota((4 * cap, n), 0)
    which = lax.div(q, cap)
    value = jnp.broadcast_to(master_ref[...].astype(F32), q.shape)
    for c in range(3):
        value = jnp.where(which == c, jnp.broadcast_to(normal_ref[c : c + 1, :], q.shape), value)
    value = jnp.where(lax.rem(q, cap).astype(F32) == ranks(owner), value, 0.0)
    out_ref[...] = dot_exact(at, value, NT)


def gathered(field_ref, nodes_ref):
    blocks = [gather8(field_ref, nodes_ref[j : j + 8, :]) for j in range(0, nodes_ref.shape[0], 8)]
    return [jnp.concatenate([b[c] for b in blocks], axis=0) for c in range(3)]


def pair_values(u_ref, snodes_ref, mnodes_ref, gap_ref, mortar_t_ref, slave_ref):
    um = jnp.concatenate(gathered(u_ref, mnodes_ref), axis=0)
    mapped = product(as_right(um, 1), mortar_t_ref[...])
    us = jnp.concatenate([*gathered(u_ref, snodes_ref), gap_ref[...]], axis=0)
    return mapped, product(slave_ref[...], as_right(us))


def prepare_kernel(
    owner_ref, pair_slave_ref, normal_ref, u_ref, v_ref, mass_ref, snodes_ref, mnodes_ref, gap_ref, mortar_ref,
    slave_ref, slave_t_ref, mortar_left_ref, mortar_t_ref, fu_ref, fv_ref, fm_ref, mapped_ref, neg_gap_ref, *, cap,
):
    owner, patches = owner_ref[...], snodes_ref.shape[0]
    n = owner.shape[1]
    slot = owner.astype(F32) * cap + ranks(owner)
    place = (iota((SLOTS, n), 0).astype(F32) == slot).astype(F32)
    hit = iota((patches, n), 0) == pair_slave_ref[...]
    parts = [jnp.where(hit, jnp.broadcast_to(-normal_ref[c : c + 1, :], hit.shape), 0.0) for c in range(3)]
    slave_t_ref[...] = as_left(dot_exact(jnp.concatenate(parts, axis=0), place, NT))
    parts.append(jnp.where(hit, -1.0, 0.0))
    slave_ref[...] = as_left(dot_exact(place, jnp.concatenate(parts, axis=0), NT))
    mortar = mortar_ref[...]
    mortar_left_ref[...] = as_left(mortar, 0)
    mortar_t_ref[...] = as_left(mortar.T, 0)
    to_field(u_ref, fu_ref)
    to_field(v_ref, fv_ref)
    fm_ref[...] = jnp.ones_like(fm_ref)
    for c in range(3):
        for h in range(MAIN + 1):
            r = field_row(c, h)
            fm_ref[r : r + 1, :] = mass_ref[0:1, h * LANES : (h + 1) * LANES]
    mapped, neg_gap = pair_values(fu_ref, snodes_ref, mnodes_ref, gap_ref, mortar_t_ref, slave_ref)
    mapped_ref[...] = mapped
    neg_gap_ref[...] = neg_gap


def first_kernel(info_ref, mapped_ref, neg_gap_ref, out_ref, master_ref, *, cap):
    n_dom, masters = info_ref.shape[0], mapped_ref.shape[0] // 3
    taken = jnp.concatenate([jnp.broadcast_to(info_ref[o : o + 1, :], (cap, 4 * cap)) for o in range(n_dom)], axis=0)
    mine = lax.rem(iota(taken.shape, 1), cap) == lax.rem(iota(taken.shape, 0), cap)
    f = lax.div(iota((4 * cap, 2 * LANES), 0), cap)
    column = iota(f.shape, 1)
    spread = ((f == lax.div(column, masters)) & (column < LANES)) | ((f == 3) & (column >= LANES))
    both = dot_exact(jnp.where(mine, taken, 0.0), spread.astype(F32), NN)
    number = lax.rem(iota((SLOTS, LANES), 1), masters).astype(F32)
    owned = jnp.where(jnp.abs(both[:, LANES:] - number) < 0.5, both[:, :LANES], 0.0)[:, : 3 * masters]
    master_ref[...] = owned
    put_slots(out_ref, 0, cap, product(as_left(owned), as_right(mapped_ref[...])))
    put_slots(out_ref, 1, cap, neg_gap_ref[...])


def turn_kernel(owned_ref, master_ref, master_t_ref):
    owned = owned_ref[...]
    master_ref[...] = as_left(owned)
    n = owned.shape[1]
    eye = (iota((n, n), 0) == iota((n, n), 1)).astype(F32)
    master_t_ref[...] = as_left(dot_exact(eye, owned, NT))


def elastic_kernel(u_ref, conn_ref, modulus_ref, stiff_ref, out_ref, ue_ref):
    tiles = conn_ref.shape[1] // LANES

    def gather_body(j, _):
        columns = pl.ds(pl.multiple_of(j * LANES, LANES), LANES)
        found = gather8(u_ref, conn_ref[:, columns])
        for c in range(3):
            ue_ref[c * 8 : (c + 1) * 8, columns] = found[c]
        return 0

    lax.fori_loop(0, tiles, gather_body, 0, unroll=4)
    ue_ref[...] = dot_exact(stiff_ref[...], ue_ref[...], NN) * modulus_ref[...]

    def body(j, total):
        columns = pl.ds(pl.multiple_of(j * LANES, LANES), LANES)
        rows = []
        for a in range(8):
            rows.append((conn_ref[a : a + 1, columns], [ue_ref[c * 8 + a : c * 8 + a + 1, columns] for c in range(3)]))
        return scatter(rows, total)

    total = lax.fori_loop(0, tiles, body, jnp.zeros((FACTOR_ROWS, LANES), F32), unroll=2)
    out_ref[...] = factor_sum(total)


def patch_rows(nodes_ref, values_ref):
    patches = nodes_ref.shape[0]
    return [
        (nodes_ref[r : r + 1, :], [values_ref[c * patches + r : c * patches + r + 1, :] for c in range(3)])
        for r in range(patches)
    ]


def contact_kernel(
    recv_ref, sent_ref, slave_t_ref, elastic_ref, snodes_ref, faces_ref, local_ref, fa_ref, fb_ref, y_ref, *, cap
):
    press = jnp.maximum(take_slots(recv_ref, 0, cap) + take_slots(sent_ref, 1, cap), 0.0)
    y_ref[...] = product(slave_t_ref[...], as_right(press))
    local_ref[...] = elastic_ref[...] + factor_sum(scatter(patch_rows(snodes_ref, y_ref)))
    found = gather8(local_ref, faces_ref[...])
    for c in range(3):
        fa_ref[c, :, :] = found[c][:4]
        fb_ref[c, :, :] = found[c][4:]


def master_kernel(recv_ref, sent_ref, master_t_ref, mortar_ref, local_ref, mnodes_ref, out_ref, y_ref, *, cap):
    press = jnp.maximum(take_slots(sent_ref, 0, cap) + take_slots(recv_ref, 1, cap), 0.0)
    summed = product(master_t_ref[...], as_right(press))
    y_ref[...] = product(as_right(summed, 1), mortar_ref[...])
    out_ref[...] = local_ref[...] + factor_sum(scatter(patch_rows(mnodes_ref, y_ref)))


def advance(negforce_ref, ra_ref, rb_ref, faces_ref, u_ref, v_ref, mass_ref):
    rows = []
    for k in range(8):
        r_ref = ra_ref if k < 4 else rb_ref
        rows.append((faces_ref[k : k + 1, :], [r_ref[c, k % 4 : k % 4 + 1, :] for c in range(3)]))
    force = negforce_ref[...] + factor_sum(scatter(rows))
    v = v_ref[...] - TIME_STEP * force / mass_ref[...]
    return u_ref[...] + TIME_STEP * v, v


def next_kernel(
    negforce_ref, ra_ref, rb_ref, faces_ref, u_ref, v_ref, mass_ref, snodes_ref, mnodes_ref, gap_ref, mortar_t_ref, slave_ref,
    master_ref, nu_ref, nv_ref, out_ref, *, cap,
):
    u, v = advance(negforce_ref, ra_ref, rb_ref, faces_ref, u_ref, v_ref, mass_ref)
    nu_ref[...] = u
    nv_ref[...] = v
    mapped, neg_gap = pair_values(nu_ref, snodes_ref, mnodes_ref, gap_ref, mortar_t_ref, slave_ref)
    put_slots(out_ref, 1, cap, neg_gap)
    put_slots(out_ref, 0, cap, product(master_ref[...], as_right(mapped)))


def last_kernel(negforce_ref, ra_ref, rb_ref, faces_ref, u_ref, v_ref, mass_ref, nu_ref, nv_ref):
    u, v = advance(negforce_ref, ra_ref, rb_ref, faces_ref, u_ref, v_ref, mass_ref)
    from_field(u, nu_ref)
    from_field(v, nv_ref)


def call(kernel, outs, args, scratch=(), us=1.0):
    vmem = pl.BlockSpec(memory_space=pltpu.VMEM)
    return pl.pallas_call(
        kernel,
        out_shape=outs,
        in_specs=[vmem] * len(args),
        out_specs=[vmem] * len(outs),
        scratch_shapes=list(scratch),
        compiler_params=pltpu.CompilerParams(vmem_limit_bytes=40 << 20),
        cost_estimate=pl.CostEstimate(flops=int(us * 1e9), bytes_accessed=int(us * 3e6), transcendentals=0),
    )(*args)


def shards(
    displacement,
    velocity,
    node_mass,
    connectivity,
    modulus,
    elem_stiffness,
    slave_nodes,
    slave_gap,
    master_nodes,
    pair_slave,
    pair_owner,
    pair_master,
    pair_normal,
    lower_face,
    upper_face,
    mortar,
):
    n_dom = lax.axis_size("dom")
    cap = SLOTS // n_dom
    slaves, masters = slave_nodes.shape[0], master_nodes.shape[0]
    f32 = lambda *shape: jax.ShapeDtypeStruct(shape, F32)
    bf16 = lambda *shape: jax.ShapeDtypeStruct(shape, BF16)
    field = f32(ROWS, LANES)
    owner = pair_owner.reshape(1, -1)
    even = lax.axis_index("dom") % 2 == 0
    faces = jnp.concatenate(
        [jnp.where(even, upper_face, lower_face), jnp.where(even, lower_face, upper_face)]
    ).reshape(8, LANES)
    inside = [(i, i ^ 1) for i in range(n_dom)]
    across = [(i, i + 1) for i in range(1, n_dom - 1, 2)]
    across = across + [(j, i) for i, j in across]

    (info,) = call(
        functools.partial(info_kernel, n_dom=n_dom, cap=cap),
        [f32(n_dom, 4 * cap)],
        (owner, pair_master.reshape(1, -1), pair_normal),
    )
    info = lax.all_to_all(info, "dom", 0, 0, tiled=True)
    slave, slave_t, mortar_left, mortar_t, u, v, mass, mapped, neg_gap = call(
        functools.partial(prepare_kernel, cap=cap),
        [
            bf16(SLOTS, 12 * slaves),
            bf16(3 * slaves, 3 * SLOTS),
            bf16(3 * LANES, LANES),
            bf16(3 * LANES, LANES),
            field,
            field,
            field,
            f32(3 * masters, LANES),
            f32(SLOTS, LANES),
        ],
        (
            owner,
            pair_slave.reshape(1, -1),
            pair_normal,
            displacement,
            velocity,
            node_mass.reshape(1, -1),
            slave_nodes,
            master_nodes,
            slave_gap,
            mortar,
        ),
        us=3.0,
    )
    blocks = f32(n_dom, 2 * cap, LANES)
    out, owned = call(functools.partial(first_kernel, cap=cap), [blocks, f32(SLOTS, 3 * masters)], (info, mapped, neg_gap))
    for step in range(STEPS):
        recv = lax.all_to_all(out, "dom", 0, 0)
        (elastic,) = call(
            elastic_kernel,
            [field],
            (u, connectivity, modulus.reshape(1, -1), elem_stiffness),
            [pltpu.VMEM((24, connectivity.shape[1]), F32)],
            us=5.0,
        )
        if step == 0:
            master, master_t = call(turn_kernel, [bf16(SLOTS, 9 * masters), bf16(3 * masters, 3 * SLOTS)], (owned,))
        local, fa, fb = call(
            functools.partial(contact_kernel, cap=cap),
            [field, f32(3, 4, LANES), f32(3, 4, LANES)],
            (recv, out, slave_t, elastic, slave_nodes, faces),
            [pltpu.VMEM((3 * slaves, LANES), F32)],
            us=2.0,
        )
        ra = lax.ppermute(fa, "dom", inside)
        rb = lax.ppermute(fb, "dom", across)
        (negforce,) = call(
            functools.partial(master_kernel, cap=cap),
            [field],
            (recv, out, master_t, mortar_left, local, master_nodes),
            [pltpu.VMEM((3 * masters, LANES), F32)],
        )
        state = (negforce, ra, rb, faces, u, v, mass)
        if step < STEPS - 1:
            u, v, out = call(
                functools.partial(next_kernel, cap=cap),
                [field, field, blocks],
                (*state, slave_nodes, master_nodes, slave_gap, mortar_t, slave, master),
                us=2.0,
            )
        else:
            outs = [f32(*displacement.shape), f32(*velocity.shape)]
            u, v = call(last_kernel, outs, state)
    return (u, v)


def solution(mesh):
    return jax.shard_map(
        shards,
        mesh=mesh,
        in_specs=(
            P(None, ("groups", "dom")),
            P(None, ("groups", "dom")),
            P(("groups", "dom")),
            P(None, ("groups", "dom")),
            P(("groups", "dom")),
            P(),
            P(("groups", "dom"), None),
            P(("groups", "dom"), None),
            P(("groups", "dom"), None),
            P(("groups", "dom")),
            P(("groups", "dom"), None),
            P(("groups", "dom")),
            P(None, ("groups", "dom")),
            P(("groups", "dom")),
            P(("groups", "dom")),
            P(),
        ),
        out_specs=(P(None, ("groups", "dom")), P(None, ("groups", "dom"))),
        check_vma=False,
    )
```

time: 1270 us -> 85.8 us (0.07)
  other arithmetic: 629 us -> 0.01 us
  local copies, waits for them, and re-layouts: 449 us -> 1.98 us
  blocking collectives: 70.1 us -> 0 us
  waiting for transfers between devices: 83.8 us -> 22.8 us
  Pallas kernels: 0 us -> 32.3 us
  between operations: 16 us -> 0.94 us
  starting transfers between devices: 13.5 us -> 26.9 us
    scatter-add x18 -> x0, other arithmetic: 613 us -> none  [the longest x3 266 us: shards(): local.at[:, s_nodes.reshape(-1)]]
    gather x29 -> x0, local copies, waits for them, and re-layouts: 414 us -> none  [the longest x6 180 us: shards(): us = jnp.moveaxis(u[:, s_nodes], 0, 1)]
    unnamed x6 -> x0, waiting for transfers between devices: 80.9 us -> none
    all_gather x3 -> x0, blocking collectives: 70.1 us -> none  [shards(): table = lax.all_gather(own, 'dom', axis=0, tiled=True)]
    pallas_call x0 -> x16, Pallas kernels: none -> 32.3 us  [call(): pl.pallas_call(kernel, out_shape=outs, in_specs=[vmem] * len(args), out_s...]
    reshape x12 -> x1, local copies, waits for them, and re-layouts: 23 us -> 0.01 us  [shards(): node_mass.reshape(1, -1)]
    all_to_all x0 -> x4, waiting for transfers between devices: none -> 19.3 us  [the longest x3 16.2 us: shards(): recv = lax.all_to_all(out, 'dom', 0, 0)]
    all_to_all x0 -> x4, starting transfers between devices: none -> 18.6 us  [the longest x3 11.2 us: shards(): recv = lax.all_to_all(out, 'dom', 0, 0)]
  transfers between devices with their start and end apart: 9 -> 10, of which waited for: 5 -> 7; matrix products, arithmetic and copies ran while one was open for 41% -> 0% of each run, Pallas kernels for 0% -> 22%
where the time goes in v2:
time: 85.8 us; the launch traced here: 85 us
  Pallas kernels  32.3 us (38%)
  starting transfers between devices  26.9 us (31%)
  waiting for transfers between devices  22.8 us (27%)
  local copies, waits for them, and re-layouts  1.98 us (2%)
  between operations  0.94 us (1%)
    pallas_call x16, Pallas kernels, call(): pl.pallas_call(kernel, out_shape=outs, in_specs=[vmem] * len(args), out_s...  32.3 us
    all_to_all x3, waiting for transfers between devices, shards(): recv = lax.all_to_all(out, 'dom', 0, 0)  16.2 us
    all_to_all x3, starting transfers between devices, shards(): recv = lax.all_to_all(out, 'dom', 0, 0)  11.2 us
    all_to_all x1, starting transfers between devices, shards(): info = lax.all_to_all(info, 'dom', 0, 0, tiled=True)  7.48 us
    ppermute x3, starting transfers between devices, shards(): rb = lax.ppermute(fb, 'dom', across)  6.08 us
    ppermute x3, waiting for transfers between devices, shards(): rb = lax.ppermute(fb, 'dom', across)  3.51 us
    all_to_all x1, waiting for transfers between devices, shards(): info = lax.all_to_all(info, 'dom', 0, 0, tiled=True)  3.15 us
    ppermute x3, starting transfers between devices, shards(): ra = lax.ppermute(fa, 'dom', inside)  2.17 us
  transfers between devices with their start and end apart: 10, of which 7 were waited for; matrix products, arithmetic and copies ran while one was open for 0% of the time, Pallas kernels for 22%

profile of v2, /device:TPU:1, one launch (start us, length us, event | category | flops | bytes accessed | tf_op | source)
XLA Modules:
  0.0 85.0 jit_solution(13617180533862925570)
XLA Ops:
  0.6 0.0 copy-start.9
  0.7 0.7 copy-done.9
  1.3 0.0 copy-done.11
  1.3 0.0 copy-start.2
  1.3 0.0 copy-start.3
  1.3 0.0 copy-start.4
  1.4 0.0 copy-start.5
  1.4 0.0 copy-start.6
  1.4 0.9 %shard_map.167 = f32[16,64]{1,0:T(8,128)} custom-call(s32[1,128]{1,0:T(1,128)S(1)} %bitcast.17, s32[1,128]{1,0:T(1,128)S(1)} %bitcast.16, f32[3,128]{1,0:T(4,128)S(1)} %copy-done.9), custom_call_target="tpu_custom_call" | custom-call | flops 1000000000 | bytes 3000000 | tf_op jit(solution)/shard_map/pallas_call | solution.py:313
  2.3 7.5 %all-to-all-start = ((f32[16,1,64]{2,1,0:T(1,128)}), f32[16,1,64]{2,1,0:T(1,128)S(1)}, u32[]{:S(2)}, u32[]{:S(2)}) async-start(f32[16,1,64]{2,1,0:T(1,128)} %bitcast.3), calls=%async_computation | async-start | bytes 16384 | tf_op jit(solution)/shard_map/all_to_all | solution.py:362
  9.8 0.0 copy-start.14
  9.8 0.7 copy-done.14
  10.5 0.0 copy-done.2
  10.5 0.6 copy-done.12
  11.1 1.2 %shard_map.168 = (bf16[256,768]{1,0:T(8,128)(2,1)S(1)}, bf16[192,768]{1,0:T(8,128)(2,1)S(1)}, bf16[384,128]{1,0:T(8,128)(2,1)S(1)}, bf16[384,128]{1,0:T(8,128)(2...) custom-call(s32[1,128]{1,0:T(1,128)S(1)} %bitcast.18, ...), custom_call_target="tpu_custom_call" | custom-call | flops 3000000000 | bytes 9000000 | tf_op jit(solution)/shard_map/pallas_call | solution.py:313
  12.3 3.1 %all-to-all-done = f32[16,1,64]{2,1,0:T(1,128)S(1)} async-done(((f32[16,1,64]{2,1,0:T(1,128)}), f32[16,1,64]{2,1,0:T(1,128)S(1)}, u32[]{:S(2)}, u32[]{:S(2)}) %all-to-all-start) | async-done | bytes 4128 | tf_op jit(solution)/shard_map/all_to_all | solution.py:362
  15.4 1.2 %shard_map.169 = (f32[16,32,128]{2,1,0:T(8,128)}, f32[256,96]{1,0:T(8,128)S(1)}) custom-call(f32[16,64]{1,0:T(8,128)S(1)} %bitcast.12, f32[96,128]{1,0:T(8,128)S(1)} %get-tuple-element.30.mapped_ref, f32[256,128]{1,0:T(8,128)S(1)} %get-tuple-element.31.neg_gap_ref), custom_call_target="tpu_custom_call" | custom-call | flops 1000000000 | bytes 3000000 | tf_op jit(solution)/shard_map/pallas_call | solution.py:313
  16.7 4.2 %all-to-all-start.1 = ((f32[16,32,128]{2,1,0:T(8,128)}), f32[16,32,128]{2,1,0:T(8,128)S(1)}, u32[]{:S(2)}, u32[]{:S(2)}) async-start(f32[16,32,128]{2,1,0:T(8,128)} %get-tuple-element.32.sent_ref), calls=%async_computation.1 | async-start | bytes 524288 | tf_op jit(solution)/shard_map/all_to_all | solution.py:393
  20.9 4.0 %shard_map.171.elastic_ref = f32[56,128]{1,0:T(8,128)S(1)} custom-call(f32[56,128]{1,0:T(8,128)S(1)} %get-tuple-element.37.u_ref, s32[8,2048]{1,0:T(8,128)S(1)} %copy-done.1, f32[1,2048]{1,0:T(1,128)S(1)} %bitcast.13, f32[24,24]{1,0:T(8,128)S(1)} %copy-done.7), custom_call_target="tpu_custom_call" | custom-call | flops 5000000000 | bytes 15000000 | tf_op jit(solution)/shard_map/pallas_call | solution.py:313
  24.9 0.3 shard_map.170
  25.2 5.2 %all-to-all-done.1.recv_ref = f32[16,32,128]{2,1,0:T(8,128)S(1)} async-done(((f32[16,32,128]{2,1,0:T(8,128)}), f32[16,32,128]{2,1,0:T(8,128)S(1)}, u32[]{:S(2)}, u32[]{:S(2)}) %all-to-all-start.1) | async-done | bytes 262176 | tf_op jit(solution)/shard_map/all_to_all | solution.py:393
  30.4 2.1 %shard_map.172 = (f32[56,128]{1,0:T(8,128)S(1)}, f32[3,4,128]{2,1,0:T(4,128)S(1)}, f32[3,4,128]{2,1,0:T(4,128)S(1)}) custom-call(f32[16,32,128]{2,1,0:T(8,128)S(1)} %all-to-all-done.1.recv_ref, f32[16,32,128]{2,1,0:T(8,128)} %get-tuple-element.32.sent_ref, bf16[192,768]{1,0:T(8,128)(2,1)S(1)} %get-tuple-element.36.slave_t_ref, ...), custom_call_target="tpu_custom_call" | custom-call | flops 2000000000 | bytes 6000000 | tf_op jit(solution)/shard_map/pallas_call | solution.py:313
  32.5 0.7 collective-permute-start
  33.3 2.0 %collective-permute-start.1 = (f32[3,4,128]{2,1,0:T(4,128)S(1)}, f32[3,4,128]{2,1,0:T(4,128)S(1)}, u32[]{:S(2)}, u32[]{:S(2)}) collective-permute-start(f32[3,4,128]{2,1,0:T(4,128)S(1)} %get-tuple-element.40), channel_id=1, source_target_pairs={{1,2},{3,4},{5,6},{7,8},{9,10},{11,12},{13,14},{2,1},{4,3},{6,5},{... | collective-permute-start | bytes 18440 | tf_op jit(solution)/shard_map/ppermute | solution.py:411
  35.3 1.7 %shard_map.173.negforce_ref = f32[56,128]{1,0:T(8,128)S(1)} custom-call(f32[16,32,128]{2,1,0:T(8,128)S(1)} %all-to-all-done.1.recv_ref, f32[16,32,128]{2,1,0:T(8,128)} %get-tuple-element.32.sent_ref, bf16[96,768]{1,0:T(8,128)(2,1)S(1)} %get-tuple-element.34.master_t_ref, bf16[384,128]{1,0:T(8,128)(2,1)S(1)} %get-tuple-element.35.mortar_ref, ...), custom_call_target="tpu_custom_call" | custom-call | flops 1000000000 | bytes 3000000 | tf_op jit(solution)/shard_map/pallas_call | solution.py:313
  37.0 0.0 collective-permute-done.ra_ref
  37.0 1.2 %collective-permute-done.1.rb_ref = f32[3,4,128]{2,1,0:T(4,128)S(1)} collective-permute-done((f32[3,4,128]{2,1,0:T(4,128)S(1)}, f32[3,4,128]{2,1,0:T(4,128)S(1)}, u32[]{:S(2)}, u32[]{:S(2)}) %collective-permute-start.1) | collective-permute-done | bytes 6176 | tf_op jit(solution)/shard_map/ppermute | solution.py:411
  38.2 2.2 %shard_map.174 = (f32[56,128]{1,0:T(8,128)S(1)}, f32[56,128]{1,0:T(8,128)S(1)}, f32[16,32,128]{2,1,0:T(8,128)}) custom-call(f32[56,128]{1,0:T(8,128)S(1)} %shard_map.173.negforce_ref, f32[3,4,128]{2,1,0:T(4,128)S(1)} %collective-permute-done.ra_ref, f32[3,4,128]{2,1,0:T(4,128)S(1)} %collective-permute-done.1.rb_ref, s32[8,128]{1,0:T(8,128)S(1)} %pad_add_fusion.faces_ref, ...), custom_call_target="tpu_custom_call" | custom-call | flops 2000000000 | bytes 6000000 | tf_op jit(solution)/shard_map/pallas_call | solution.py:313
  40.4 3.5 %all-to-all-start.2 = ((f32[16,32,128]{2,1,0:T(8,128)}), f32[16,32,128]{2,1,0:T(8,128)S(1)}, u32[]{:S(2)}, u32[]{:S(2)}) async-start(f32[16,32,128]{2,1,0:T(8,128)} %get-tuple-element.46.sent_ref), calls=%async_computation.2 | async-start | bytes 524288 | tf_op jit(solution)/shard_map/all_to_all | solution.py:393
  43.8 4.0 %shard_map.175.elastic_ref = f32[56,128]{1,0:T(8,128)S(1)} custom-call(f32[56,128]{1,0:T(8,128)S(1)} %get-tuple-element.47.u_ref, s32[8,2048]{1,0:T(8,128)S(1)} %copy-done.1, f32[1,2048]{1,0:T(1,128)S(1)} %bitcast.14, f32[24,24]{1,0:T(8,128)S(1)} %copy-done.7), custom_call_target="tpu_custom_call" | custom-call | flops 5000000000 | bytes 15000000 | tf_op jit(solution)/shard_map/pallas_call | solution.py:313
  47.9 5.5 %all-to-all-done.2.recv_ref = f32[16,32,128]{2,1,0:T(8,128)S(1)} async-done(((f32[16,32,128]{2,1,0:T(8,128)}), f32[16,32,128]{2,1,0:T(8,128)S(1)}, u32[]{:S(2)}, u32[]{:S(2)}) %all-to-all-start.2) | async-done | bytes 262176 | tf_op jit(solution)/shard_map/all_to_all | solution.py:393
  53.3 2.1 %shard_map.176 = (f32[56,128]{1,0:T(8,128)S(1)}, f32[3,4,128]{2,1,0:T(4,128)S(1)}, f32[3,4,128]{2,1,0:T(4,128)S(1)}) custom-call(f32[16,32,128]{2,1,0:T(8,128)S(1)} %all-to-all-done.2.recv_ref, f32[16,32,128]{2,1,0:T(8,128)} %get-tuple-element.46.sent_ref, bf16[192,768]{1,0:T(8,128)(2,1)S(1)} %get-tuple-element.36.slave_t_ref, ...), custom_call_target="tpu_custom_call" | custom-call | flops 2000000000 | bytes 6000000 | tf_op jit(solution)/shard_map/pallas_call | solution.py:313
  55.4 0.7 collective-permute-start.2
  56.2 2.0 %collective-permute-start.3 = (f32[3,4,128]{2,1,0:T(4,128)S(1)}, f32[3,4,128]{2,1,0:T(4,128)S(1)}, u32[]{:S(2)}, u32[]{:S(2)}) collective-permute-start(f32[3,4,128]{2,1,0:T(4,128)S(1)} %get-tuple-element.50), channel_id=1, source_target_pairs={{1,2},{3,4},{5,6},{7,8},{9,10},{11,12},{13,14},{2,1},{4,3},{6,5},{... | collective-permute-start | bytes 18440 | tf_op jit(solution)/shard_map/ppermute | solution.py:411
  58.2 1.7 %shard_map.177.negforce_ref = f32[56,128]{1,0:T(8,128)S(1)} custom-call(f32[16,32,128]{2,1,0:T(8,128)S(1)} %all-to-all-done.2.recv_ref, f32[16,32,128]{2,1,0:T(8,128)} %get-tuple-element.46.sent_ref, bf16[96,768]{1,0:T(8,128)(2,1)S(1)} %get-tuple-element.34.master_t_ref, bf16[384,128]{1,0:T(8,128)(2,1)S(1)} %get-tuple-element.35.mortar_ref, ...), custom_call_target="tpu_custom_call" | custom-call | flops 1000000000 | bytes 3000000 | tf_op jit(solution)/shard_map/pallas_call | solution.py:313
  59.9 0.0 collective-permute-done.2.ra_ref
  59.9 1.2 %collective-permute-done.3.rb_ref = f32[3,4,128]{2,1,0:T(4,128)S(1)} collective-permute-done((f32[3,4,128]{2,1,0:T(4,128)S(1)}, f32[3,4,128]{2,1,0:T(4,128)S(1)}, u32[]{:S(2)}, u32[]{:S(2)}) %collective-permute-start.3) | collective-permute-done | bytes 6176 | tf_op jit(solution)/shard_map/ppermute | solution.py:411
  61.1 2.2 %shard_map.178 = (f32[56,128]{1,0:T(8,128)S(1)}, f32[56,128]{1,0:T(8,128)S(1)}, f32[16,32,128]{2,1,0:T(8,128)}) custom-call(f32[56,128]{1,0:T(8,128)S(1)} %shard_map.177.negforce_ref, f32[3,4,128]{2,1,0:T(4,128)S(1)} %collective-permute-done.2.ra_ref, f32[3,4,128]{2,1,0:T(4,128)S(1)} %collective-permute-done.3.rb_ref, s32[8,128]{1,0:T(8,128)S(1)} %pad_add_fusion.faces_ref, ...), custom_call_target="tpu_custom_call" | custom-call | flops 2000000000 | bytes 6000000 | tf_op jit(solution)/shard_map/pallas_call | solution.py:313
  63.3 3.5 %all-to-all-start.3 = ((f32[16,32,128]{2,1,0:T(8,128)}), f32[16,32,128]{2,1,0:T(8,128)S(1)}, u32[]{:S(2)}, u32[]{:S(2)}) async-start(f32[16,32,128]{2,1,0:T(8,128)} %get-tuple-element.52.sent_ref), calls=%async_computation.3 | async-start | bytes 524288 | tf_op jit(solution)/shard_map/all_to_all | solution.py:393
  66.8 4.0 %shard_map.179.elastic_ref = f32[56,128]{1,0:T(8,128)S(1)} custom-call(f32[56,128]{1,0:T(8,128)S(1)} %get-tuple-element.53.u_ref, s32[8,2048]{1,0:T(8,128)S(1)} %copy-done.1, f32[1,2048]{1,0:T(1,128)S(1)} %bitcast.15, f32[24,24]{1,0:T(8,128)S(1)} %copy-done.7), custom_call_target="tpu_custom_call" | custom-call | flops 5000000000 | bytes 15000000 | tf_op jit(solution)/shard_map/pallas_call | solution.py:313
  70.9 5.5 %all-to-all-done.3.recv_ref = f32[16,32,128]{2,1,0:T(8,128)S(1)} async-done(((f32[16,32,128]{2,1,0:T(8,128)}), f32[16,32,128]{2,1,0:T(8,128)S(1)}, u32[]{:S(2)}, u32[]{:S(2)}) %all-to-all-start.3) | async-done | bytes 262176 | tf_op jit(solution)/shard_map/all_to_all | solution.py:393
  76.3 2.1 %shard_map.180 = (f32[56,128]{1,0:T(8,128)S(1)}, f32[3,4,128]{2,1,0:T(4,128)S(1)}, f32[3,4,128]{2,1,0:T(4,128)S(1)}) custom-call(f32[16,32,128]{2,1,0:T(8,128)S(1)} %all-to-all-done.3.recv_ref, f32[16,32,128]{2,1,0:T(8,128)} %get-tuple-element.52.sent_ref, bf16[192,768]{1,0:T(8,128)(2,1)S(1)} %get-tuple-element.36.slave_t_ref, ...), custom_call_target="tpu_custom_call" | custom-call | flops 2000000000 | bytes 6000000 | tf_op jit(solution)/shard_map/pallas_call | solution.py:313
  78.4 0.7 collective-permute-start.4
  79.1 2.0 %collective-permute-start.5 = (f32[3,4,128]{2,1,0:T(4,128)S(1)}, f32[3,4,128]{2,1,0:T(4,128)S(1)}, u32[]{:S(2)}, u32[]{:S(2)}) collective-permute-start(f32[3,4,128]{2,1,0:T(4,128)S(1)} %get-tuple-element.56), channel_id=1, source_target_pairs={{1,2},{3,4},{5,6},{7,8},{9,10},{11,12},{13,14},{2,1},{4,3},{6,5},{... | collective-permute-start | bytes 18440 | tf_op jit(solution)/shard_map/ppermute | solution.py:411
  81.2 1.7 %shard_map.181.negforce_ref = f32[56,128]{1,0:T(8,128)S(1)} custom-call(f32[16,32,128]{2,1,0:T(8,128)S(1)} %all-to-all-done.3.recv_ref, f32[16,32,128]{2,1,0:T(8,128)} %get-tuple-element.52.sent_ref, bf16[96,768]{1,0:T(8,128)(2,1)S(1)} %get-tuple-element.34.master_t_ref, bf16[384,128]{1,0:T(8,128)(2,1)S(1)} %get-tuple-element.35.mortar_ref, ...), custom_call_target="tpu_custom_call" | custom-call | flops 1000000000 | bytes 3000000 | tf_op jit(solution)/shard_map/pallas_call | solution.py:313
  82.9 0.0 collective-permute-done.4.ra_ref
  82.9 1.2 %collective-permute-done.5.rb_ref = f32[3,4,128]{2,1,0:T(4,128)S(1)} collective-permute-done((f32[3,4,128]{2,1,0:T(4,128)S(1)}, f32[3,4,128]{2,1,0:T(4,128)S(1)}, u32[]{:S(2)}, u32[]{:S(2)}) %collective-permute-start.5) | collective-permute-done | bytes 6176 | tf_op jit(solution)/shard_map/ppermute | solution.py:411
  84.1 0.9 %shard_map.182 = (f32[3,2176]{1,0:T(4,128)}, f32[3,2176]{1,0:T(4,128)}) custom-call(f32[56,128]{1,0:T(8,128)S(1)} %shard_map.181.negforce_ref, f32[3,4,128]{2,1,0:T(4,128)S(1)} %collective-permute-done.4.ra_ref, f32[3,4,128]{2,1,0:T(4,128)S(1)} %collective-permute-done.5.rb_ref, s32[8,128]{1,0:T(8,128)S(1)} %pad_add_fusion.faces_ref, ...), custom_call_target="tpu_custom_call" | custom-call | flops 1000000000 | bytes 3000000 | tf_op jit(solution)/shard_map/pallas_call | solution.py:313
  (23 shorter events, 0.1 us)
Async XLA Ops:
  0.6 0.7 copy-start.9
  0.6 0.7 copy-start.10
  0.7 0.7 copy-start.11
  1.3 8.4 %copy-start.13 = (f32[2176]{0:T(1024)S(1)}, f32[2176]{0:T(1024)}, u32[]{:S(2)}) copy-start(f32[2176]{0:T(1024)} %param.18) | copy-start | bytes 26116
  1.3 8.5 %copy-start.15 = (s32[512]{0:T(512)S(1)}, s32[512]{0:T(512)}, u32[]{:S(2)}) copy-start(s32[512]{0:T(512)} %param.29) | copy-start | bytes 6148
  1.3 9.1 %copy-start.2 = (f32[3,2176]{1,0:T(4,128)S(1)}, f32[3,2176]{1,0:T(4,128)}, u32[]{:S(2)}) copy-start(f32[3,2176]{1,0:T(4,128)} %u_ref.1) | copy-start | bytes 78340
  1.3 9.1 %copy-start.3 = (f32[3,2176]{1,0:T(4,128)S(1)}, f32[3,2176]{1,0:T(4,128)}, u32[]{:S(2)}) copy-start(f32[3,2176]{1,0:T(4,128)} %v_ref.1) | copy-start | bytes 78340
  1.3 9.1 %copy-start.4 = (f32[64,128]{1,0:T(8,128)S(1)}, f32[64,128]{1,0:T(8,128)}, u32[]{:S(2)}) copy-start(f32[64,128]{1,0:T(8,128)} %gap_ref.5) | copy-start | bytes 98308
  1.4 9.1 %copy-start.5 = (s32[64,128]{1,0:T(8,128)S(1)}, s32[64,128]{1,0:T(8,128)}, u32[]{:S(2)}) copy-start(s32[64,128]{1,0:T(8,128)} %snodes_ref.11) | copy-start | bytes 98308
  1.4 9.1 %copy-start.6 = (s32[32,128]{1,0:T(8,128)S(1)}, s32[32,128]{1,0:T(8,128)}, u32[]{:S(2)}) copy-start(s32[32,128]{1,0:T(8,128)} %mnodes_ref.11) | copy-start | bytes 49156
  2.3 8.3 %copy-start = (f32[128,128]{1,0:T(8,128)S(1)}, f32[128,128]{1,0:T(8,128)}, u32[]{:S(2)}) copy-start(f32[128,128]{1,0:T(8,128)} %mortar_ref.1) | copy-start | bytes 196612
  2.3 13.2 %all-to-all-start = ((f32[16,1,64]{2,1,0:T(1,128)}), f32[16,1,64]{2,1,0:T(1,128)S(1)}, u32[]{:S(2)}, u32[]{:S(2)}) async-start(f32[16,1,64]{2,1,0:T(1,128)} %bitcast.3), calls=%async_computation | async-start | bytes 16384 | tf_op jit(solution)/shard_map/all_to_all | solution.py:362
  9.8 0.7 copy-start.14
  10.5 0.7 copy-start.12
  16.7 4.2 %copy-start.1 = (s32[8,2048]{1,0:T(8,128)S(1)}, s32[8,2048]{1,0:T(8,128)}, u32[]{:S(2)}) copy-start(s32[8,2048]{1,0:T(8,128)} %conn_ref.5) | copy-start | bytes 196612
  16.7 4.2 %copy-start.7 = (f32[24,24]{1,0:T(8,128)S(1)}, f32[24,24]{1,0:T(8,128)}, u32[]{:S(2)}) copy-start(f32[24,24]{1,0:T(8,128)} %stiff_ref.5) | copy-start | bytes 6916
  16.7 4.2 %copy-start.8 = (f32[2048]{0:T(1024)S(1)}, f32[2048]{0:T(1024)}, u32[]{:S(2)}) copy-start(f32[2048]{0:T(1024)} %param.20) | copy-start | bytes 24580
  16.7 13.7 %all-to-all-start.1 = ((f32[16,32,128]{2,1,0:T(8,128)}), f32[16,32,128]{2,1,0:T(8,128)S(1)}, u32[]{:S(2)}, u32[]{:S(2)}) async-start(f32[16,32,128]{2,1,0:T(8,128)} %get-tuple-element.32.sent_ref), calls=%async_computation.1 | async-start | bytes 524288 | tf_op jit(solution)/shard_map/all_to_all | solution.py:393
  32.5 4.5 %collective-permute-start = (f32[3,4,128]{2,1,0:T(4,128)S(1)}, f32[3,4,128]{2,1,0:T(4,128)S(1)}, u32[]{:S(2)}, u32[]{:S(2)}) collective-permute-start(f32[3,4,128]{2,1,0:T(4,128)S(1)} %get-tuple-element.39), channel_id=1, source_target_pairs={{0,1},{1,0},{2,3},{3,2},{4,5},{5,4},{6,7},{7,6},{8,9},{9,8},{10,11... | collective-permute-start | bytes 18440 | tf_op jit(solution)/shard_map/ppermute | solution.py:410
  33.3 4.9 %collective-permute-start.1 = (f32[3,4,128]{2,1,0:T(4,128)S(1)}, f32[3,4,128]{2,1,0:T(4,128)S(1)}, u32[]{:S(2)}, u32[]{:S(2)}) collective-permute-start(f32[3,4,128]{2,1,0:T(4,128)S(1)} %get-tuple-element.40), channel_id=1, source_target_pairs={{1,2},{3,4},{5,6},{7,8},{9,10},{11,12},{13,14},{2,1},{4,3},{6,5},{... | collective-permute-start | bytes 18440 | tf_op jit(solution)/shard_map/ppermute | solution.py:411
  40.4 13.0 %all-to-all-start.2 = ((f32[16,32,128]{2,1,0:T(8,128)}), f32[16,32,128]{2,1,0:T(8,128)S(1)}, u32[]{:S(2)}, u32[]{:S(2)}) async-start(f32[16,32,128]{2,1,0:T(8,128)} %get-tuple-element.46.sent_ref), calls=%async_computation.2 | async-start | bytes 524288 | tf_op jit(solution)/shard_map/all_to_all | solution.py:393
  55.4 4.5 %collective-permute-start.2 = (f32[3,4,128]{2,1,0:T(4,128)S(1)}, f32[3,4,128]{2,1,0:T(4,128)S(1)}, u32[]{:S(2)}, u32[]{:S(2)}) collective-permute-start(f32[3,4,128]{2,1,0:T(4,128)S(1)} %get-tuple-element.49), channel_id=1, source_target_pairs={{0,1},{1,0},{2,3},{3,2},{4,5},{5,4},{6,7},{7,6},{8,9},{9,8},{10,11... | collective-permute-start | bytes 18440 | tf_op jit(solution)/shard_map/ppermute | solution.py:410
  56.2 4.9 %collective-permute-start.3 = (f32[3,4,128]{2,1,0:T(4,128)S(1)}, f32[3,4,128]{2,1,0:T(4,128)S(1)}, u32[]{:S(2)}, u32[]{:S(2)}) collective-permute-start(f32[3,4,128]{2,1,0:T(4,128)S(1)} %get-tuple-element.50), channel_id=1, source_target_pairs={{1,2},{3,4},{5,6},{7,8},{9,10},{11,12},{13,14},{2,1},{4,3},{6,5},{... | collective-permute-start | bytes 18440 | tf_op jit(solution)/shard_map/ppermute | solution.py:411
  63.3 13.0 %all-to-all-start.3 = ((f32[16,32,128]{2,1,0:T(8,128)}), f32[16,32,128]{2,1,0:T(8,128)S(1)}, u32[]{:S(2)}, u32[]{:S(2)}) async-start(f32[16,32,128]{2,1,0:T(8,128)} %get-tuple-element.52.sent_ref), calls=%async_computation.3 | async-start | bytes 524288 | tf_op jit(solution)/shard_map/all_to_all | solution.py:393
  78.4 4.5 %collective-permute-start.4 = (f32[3,4,128]{2,1,0:T(4,128)S(1)}, f32[3,4,128]{2,1,0:T(4,128)S(1)}, u32[]{:S(2)}, u32[]{:S(2)}) collective-permute-start(f32[3,4,128]{2,1,0:T(4,128)S(1)} %get-tuple-element.55), channel_id=1, source_target_pairs={{0,1},{1,0},{2,3},{3,2},{4,5},{5,4},{6,7},{7,6},{8,9},{9,8},{10,11... | collective-permute-start | bytes 18440 | tf_op jit(solution)/shard_map/ppermute | solution.py:410
  79.1 4.9 %collective-permute-start.5 = (f32[3,4,128]{2,1,0:T(4,128)S(1)}, f32[3,4,128]{2,1,0:T(4,128)S(1)}, u32[]{:S(2)}, u32[]{:S(2)}) collective-permute-start(f32[3,4,128]{2,1,0:T(4,128)S(1)} %get-tuple-element.56), channel_id=1, source_target_pairs={{1,2},{3,4},{5,6},{7,8},{9,10},{11,12},{13,14},{2,1},{4,3},{6,5},{... | collective-permute-start | bytes 18440 | tf_op jit(solution)/shard_map/ppermute | solution.py:411

commit v3 on v2

--- a/solution.py
+++ b/solution.py
@@ -146,23 +146,22 @@
             block_ref[o, rows, :] = value[o * cap : (o + 1) * cap]
 
 
-def ranks(owner):
-    n = owner.shape[1]
-    across = jnp.broadcast_to(owner.astype(F32), (n, n))
-    same = (across.T == across) & (iota((n, n), 0) < iota((n, n), 1))
-    return jnp.sum(same.astype(F32), axis=0, keepdims=True)
-
-
-def info_kernel(owner_ref, master_ref, normal_ref, out_ref, *, n_dom, cap):
-    owner = owner_ref[...]
+def ranks(owner, n_dom):
     n = owner.shape[1]
     at = (iota((n_dom, n), 0) == owner).astype(F32)
-    q = iota((4 * cap, n), 0)
+    before = (iota((n, n), 0) < iota((n, n), 1)).astype(F32)
+    counts = lax.dot_general(at.astype(BF16), before.astype(BF16), NN, preferred_element_type=F32)
+    return jnp.sum(at * counts, axis=0, keepdims=True), at
+
+
+def info_kernel(owner_ref, master_ref, normal_ref, out_ref, *, n_dom, cap):
+    rank, at = ranks(owner_ref[...], n_dom)
+    q = iota((4 * cap, owner_ref.shape[1]), 0)
     which = lax.div(q, cap)
     value = jnp.broadcast_to(master_ref[...].astype(F32), q.shape)
     for c in range(3):
         value = jnp.where(which == c, jnp.broadcast_to(normal_ref[c : c + 1, :], q.shape), value)
-    value = jnp.where(lax.rem(q, cap).astype(F32) == ranks(owner), value, 0.0)
+    value = jnp.where(lax.rem(q, cap).astype(F32) == rank, value, 0.0)
     out_ref[...] = dot_exact(at, value, NT)
 
 
@@ -180,11 +179,11 @@
 
 def prepare_kernel(
     owner_ref, pair_slave_ref, normal_ref, u_ref, v_ref, mass_ref, snodes_ref, mnodes_ref, gap_ref, mortar_ref,
-    slave_ref, slave_t_ref, mortar_left_ref, mortar_t_ref, fu_ref, fv_ref, fm_ref, mapped_ref, neg_gap_ref, *, cap,
+    slave_ref, slave_t_ref, mortar_left_ref, mortar_t_ref, fu_ref, fv_ref, fm_ref, mapped_ref, neg_gap_ref, *, n_dom, cap,
 ):
     owner, patches = owner_ref[...], snodes_ref.shape[0]
     n = owner.shape[1]
-    slot = owner.astype(F32) * cap + ranks(owner)
+    slot = owner.astype(F32) * cap + ranks(owner, n_dom)[0]
     place = (iota((SLOTS, n), 0).astype(F32) == slot).astype(F32)
     hit = iota((patches, n), 0) == pair_slave_ref[...]
     parts = [jnp.where(hit, jnp.broadcast_to(-normal_ref[c : c + 1, :], hit.shape), 0.0) for c in range(3)]
@@ -206,7 +205,7 @@
     neg_gap_ref[...] = neg_gap
 
 
-def first_kernel(info_ref, mapped_ref, neg_gap_ref, out_ref, master_ref, *, cap):
+def first_kernel(info_ref, mapped_ref, neg_gap_ref, out_ref, m_ref, master_ref, *, cap):
     n_dom, masters = info_ref.shape[0], mapped_ref.shape[0] // 3
     taken = jnp.concatenate([jnp.broadcast_to(info_ref[o : o + 1, :], (cap, 4 * cap)) for o in range(n_dom)], axis=0)
     mine = lax.rem(iota(taken.shape, 1), cap) == lax.rem(iota(taken.shape, 0), cap)
@@ -217,8 +216,9 @@
     number = lax.rem(iota((SLOTS, LANES), 1), masters).astype(F32)
     owned = jnp.where(jnp.abs(both[:, LANES:] - number) < 0.5, both[:, :LANES], 0.0)[:, : 3 * masters]
     master_ref[...] = owned
-    put_slots(out_ref, 0, cap, product(as_left(owned), as_right(mapped_ref[...])))
     put_slots(out_ref, 1, cap, neg_gap_ref[...])
+    m_ref[...] = product(as_left(owned), as_right(mapped_ref[...]))
+    put_slots(out_ref, 0, cap, m_ref[...])
 
 
 def turn_kernel(owned_ref, master_ref, master_t_ref):
@@ -262,9 +262,9 @@
 
 
 def contact_kernel(
-    recv_ref, sent_ref, slave_t_ref, elastic_ref, snodes_ref, faces_ref, local_ref, fa_ref, fb_ref, y_ref, *, cap
+    recv_ref, neg_gap_ref, slave_t_ref, elastic_ref, snodes_ref, faces_ref, local_ref, fa_ref, fb_ref, y_ref, *, cap
 ):
-    press = jnp.maximum(take_slots(recv_ref, 0, cap) + take_slots(sent_ref, 1, cap), 0.0)
+    press = jnp.maximum(take_slots(recv_ref, 0, cap) + neg_gap_ref[...], 0.0)
     y_ref[...] = product(slave_t_ref[...], as_right(press))
     local_ref[...] = elastic_ref[...] + factor_sum(scatter(patch_rows(snodes_ref, y_ref)))
     found = gather8(local_ref, faces_ref[...])
@@ -273,8 +273,8 @@
         fb_ref[c, :, :] = found[c][4:]
 
 
-def master_kernel(recv_ref, sent_ref, master_t_ref, mortar_ref, local_ref, mnodes_ref, out_ref, y_ref, *, cap):
-    press = jnp.maximum(take_slots(sent_ref, 0, cap) + take_slots(recv_ref, 1, cap), 0.0)
+def master_kernel(recv_ref, m_ref, master_t_ref, mortar_ref, local_ref, mnodes_ref, out_ref, y_ref, *, cap):
+    press = jnp.maximum(m_ref[...] + take_slots(recv_ref, 1, cap), 0.0)
     summed = product(master_t_ref[...], as_right(press))
     y_ref[...] = product(as_right(summed, 1), mortar_ref[...])
     out_ref[...] = local_ref[...] + factor_sum(scatter(patch_rows(mnodes_ref, y_ref)))
@@ -292,14 +292,16 @@
 
 def next_kernel(
     negforce_ref, ra_ref, rb_ref, faces_ref, u_ref, v_ref, mass_ref, snodes_ref, mnodes_ref, gap_ref, mortar_t_ref, slave_ref,
-    master_ref, nu_ref, nv_ref, out_ref, *, cap,
+    master_ref, nu_ref, nv_ref, out_ref, m_ref, neg_gap_ref, *, cap,
 ):
     u, v = advance(negforce_ref, ra_ref, rb_ref, faces_ref, u_ref, v_ref, mass_ref)
     nu_ref[...] = u
     nv_ref[...] = v
     mapped, neg_gap = pair_values(nu_ref, snodes_ref, mnodes_ref, gap_ref, mortar_t_ref, slave_ref)
+    neg_gap_ref[...] = neg_gap
     put_slots(out_ref, 1, cap, neg_gap)
-    put_slots(out_ref, 0, cap, product(master_ref[...], as_right(mapped)))
+    m_ref[...] = product(master_ref[...], as_right(mapped))
+    put_slots(out_ref, 0, cap, m_ref[...])
 
 
 def last_kernel(negforce_ref, ra_ref, rb_ref, faces_ref, u_ref, v_ref, mass_ref, nu_ref, nv_ref):
@@ -361,7 +363,7 @@
     )
     info = lax.all_to_all(info, "dom", 0, 0, tiled=True)
     slave, slave_t, mortar_left, mortar_t, u, v, mass, mapped, neg_gap = call(
-        functools.partial(prepare_kernel, cap=cap),
+        functools.partial(prepare_kernel, n_dom=n_dom, cap=cap),
         [
             bf16(SLOTS, 12 * slaves),
             bf16(3 * slaves, 3 * SLOTS),
@@ -388,7 +390,10 @@
         us=3.0,
     )
     blocks = f32(n_dom, 2 * cap, LANES)
-    out, owned = call(functools.partial(first_kernel, cap=cap), [blocks, f32(SLOTS, 3 * masters)], (info, mapped, neg_gap))
+    slots = f32(SLOTS, LANES)
+    out, m, owned = call(
+        functools.partial(first_kernel, cap=cap), [blocks, slots, f32(SLOTS, 3 * masters)], (info, mapped, neg_gap)
+    )
     for step in range(STEPS):
         recv = lax.all_to_all(out, "dom", 0, 0)
         (elastic,) = call(
@@ -403,7 +408,7 @@
         local, fa, fb = call(
             functools.partial(contact_kernel, cap=cap),
             [field, f32(3, 4, LANES), f32(3, 4, LANES)],
-            (recv, out, slave_t, elastic, slave_nodes, faces),
+            (recv, neg_gap, slave_t, elastic, slave_nodes, faces),
             [pltpu.VMEM((3 * slaves, LANES), F32)],
             us=2.0,
         )
@@ -412,14 +417,14 @@
         (negforce,) = call(
             functools.partial(master_kernel, cap=cap),
             [field],
-            (recv, out, master_t, mortar_left, local, master_nodes),
+            (recv, m, master_t, mortar_left, local, master_nodes),
             [pltpu.VMEM((3 * masters, LANES), F32)],
         )
         state = (negforce, ra, rb, faces, u, v, mass)
         if step < STEPS - 1:
-            u, v, out = call(
+            u, v, out, m, neg_gap = call(
                 functools.partial(next_kernel, cap=cap),
-                [field, field, blocks],
+                [field, field, blocks, slots, slots],
                 (*state, slave_nodes, master_nodes, slave_gap, mortar_t, slave, master),
                 us=2.0,
             )

time: 85.8 us -> 82.8 us (0.965)
  Pallas kernels: 32.3 us -> 26.7 us
  waiting for transfers between devices: 22.8 us -> 25.7 us
    pallas_call x16, Pallas kernels: 32.3 us -> 26.7 us  [call(): pl.pallas_call(kernel, out_shape=outs, in_specs=[vmem] * len(args), out_s...]
    ppermute x3, waiting for transfers between devices: 3.51 us -> 6.34 us  [shards(): rb = lax.ppermute(fb, 'dom', across)]
  transfers between devices with their start and end apart: 10 -> 10, of which waited for: 7 -> 7; matrix products, arithmetic and copies ran while one was open for 0% -> 0% of each run, Pallas kernels for 22% -> 19%
where the time goes in v3:
time: 82.8 us; the launch traced here: 82.2 us
  starting transfers between devices  26.9 us (32%)
  Pallas kernels  26.7 us (32%)
  waiting for transfers between devices  25.7 us (31%)
  local copies, waits for them, and re-layouts  1.97 us (2%)
  between operations  0.93 us (1%)
    pallas_call x16, Pallas kernels, call(): pl.pallas_call(kernel, out_shape=outs, in_specs=[vmem] * len(args), out_s...  26.7 us
    all_to_all x3, waiting for transfers between devices, shards(): recv = lax.all_to_all(out, 'dom', 0, 0)  16.2 us
    all_to_all x3, starting transfers between devices, shards(): recv = lax.all_to_all(out, 'dom', 0, 0)  11.2 us
    all_to_all x1, starting transfers between devices, shards(): info = lax.all_to_all(info, 'dom', 0, 0, tiled=True)  7.48 us
    ppermute x3, waiting for transfers between devices, shards(): rb = lax.ppermute(fb, 'dom', across)  6.34 us
    ppermute x3, starting transfers between devices, shards(): rb = lax.ppermute(fb, 'dom', across)  6.09 us
    all_to_all x1, waiting for transfers between devices, shards(): info = lax.all_to_all(info, 'dom', 0, 0, tiled=True)  3.19 us
    ppermute x3, starting transfers between devices, shards(): ra = lax.ppermute(fa, 'dom', inside)  2.16 us
  transfers between devices with their start and end apart: 10, of which 7 were waited for; matrix products, arithmetic and copies ran while one was open for 0% of the time, Pallas kernels for 19%

profile of v3, /device:TPU:1, one launch (start us, length us, event | category | flops | bytes accessed | tf_op | source)
XLA Modules:
  0.0 82.2 jit_solution(11917318976907366653)
XLA Ops:
  0.6 0.0 copy-start.9
  0.6 0.0 copy-start.10
  0.7 0.7 copy-done.9
  1.3 0.0 copy-done.11
  1.3 0.0 copy-start.2
  1.3 0.0 copy-start.3
  1.3 0.0 copy-start.4
  1.4 0.0 copy-start.5
  1.4 0.0 copy-start.6
  1.4 0.9 %shard_map.167 = f32[16,64]{1,0:T(8,128)} custom-call(s32[1,128]{1,0:T(1,128)S(1)} %bitcast.17, s32[1,128]{1,0:T(1,128)S(1)} %bitcast.16, f32[3,128]{1,0:T(4,128)S(1)} %copy-done.9), custom_call_target="tpu_custom_call" | custom-call | flops 1000000000 | bytes 3000000 | tf_op jit(solution)/shard_map/pallas_call | solution.py:315
  2.3 7.5 %all-to-all-start = ((f32[16,1,64]{2,1,0:T(1,128)}), f32[16,1,64]{2,1,0:T(1,128)S(1)}, u32[]{:S(2)}, u32[]{:S(2)}) async-start(f32[16,1,64]{2,1,0:T(1,128)} %bitcast.3), calls=%async_computation | async-start | bytes 16384 | tf_op jit(solution)/shard_map/all_to_all | solution.py:364
  9.8 0.0 copy-start.14
  9.8 0.6 copy-done.14
  10.5 0.6 copy-done.12
  11.1 1.1 %shard_map.168 = (bf16[256,768]{1,0:T(8,128)(2,1)S(1)}, bf16[192,768]{1,0:T(8,128)(2,1)S(1)}, bf16[384,128]{1,0:T(8,128)(2,1)S(1)}, bf16[384,128]{1,0:T(8,128)(2...) custom-call(s32[1,128]{1,0:T(1,128)S(1)} %bitcast.18, ...), custom_call_target="tpu_custom_call" | custom-call | flops 3000000000 | bytes 9000000 | tf_op jit(solution)/shard_map/pallas_call | solution.py:315
  12.3 3.2 %all-to-all-done = f32[16,1,64]{2,1,0:T(1,128)S(1)} async-done(((f32[16,1,64]{2,1,0:T(1,128)}), f32[16,1,64]{2,1,0:T(1,128)S(1)}, u32[]{:S(2)}, u32[]{:S(2)}) %all-to-all-start) | async-done | bytes 4128 | tf_op jit(solution)/shard_map/all_to_all | solution.py:364
  15.5 1.2 %shard_map.169 = (f32[16,32,128]{2,1,0:T(8,128)}, f32[256,128]{1,0:T(8,128)S(1)}, f32[256,96]{1,0:T(8,128)S(1)}) custom-call(f32[16,64]{1,0:T(8,128)S(1)} %bitcast.12, f32[96,128]{1,0:T(8,128)S(1)} %get-tuple-element.35.mapped_ref, f32[256,128]{1,0:T(8,128)S(1)} %get-tuple-element.36.neg_gap_ref), custom_call_target="tpu_custom_call" | custom-call | flops 1000000000 | bytes 3000000 | tf_op jit(solution)/shard_map/pallas_call | solution.py:315
  16.7 4.2 %all-to-all-start.1 = ((f32[16,32,128]{2,1,0:T(8,128)}), f32[16,32,128]{2,1,0:T(8,128)S(1)}, u32[]{:S(2)}, u32[]{:S(2)}) async-start(f32[16,32,128]{2,1,0:T(8,128)} %get-tuple-element.37), calls=%async_computation.1 | async-start | bytes 524288 | tf_op jit(solution)/shard_map/all_to_all | solution.py:398
  20.9 4.0 %shard_map.171.elastic_ref = f32[56,128]{1,0:T(8,128)S(1)} custom-call(f32[56,128]{1,0:T(8,128)S(1)} %get-tuple-element.43.u_ref, s32[8,2048]{1,0:T(8,128)S(1)} %copy-done.1, f32[1,2048]{1,0:T(1,128)S(1)} %bitcast.13, f32[24,24]{1,0:T(8,128)S(1)} %copy-done.7), custom_call_target="tpu_custom_call" | custom-call | flops 5000000000 | bytes 15000000 | tf_op jit(solution)/shard_map/pallas_call | solution.py:315
  25.0 0.3 shard_map.170
  25.3 5.2 %all-to-all-done.1.recv_ref = f32[16,32,128]{2,1,0:T(8,128)S(1)} async-done(((f32[16,32,128]{2,1,0:T(8,128)}), f32[16,32,128]{2,1,0:T(8,128)S(1)}, u32[]{:S(2)}, u32[]{:S(2)}) %all-to-all-start.1) | async-done | bytes 262176 | tf_op jit(solution)/shard_map/all_to_all | solution.py:398
  30.5 1.2 %shard_map.172 = (f32[56,128]{1,0:T(8,128)S(1)}, f32[3,4,128]{2,1,0:T(4,128)S(1)}, f32[3,4,128]{2,1,0:T(4,128)S(1)}) custom-call(f32[16,32,128]{2,1,0:T(8,128)S(1)} %all-to-all-done.1.recv_ref, f32[256,128]{1,0:T(8,128)S(1)} %get-tuple-element.36.neg_gap_ref, bf16[192,768]{1,0:T(8,128)(2,1)S(1)} %get-tuple-element.42.slave_t_ref, ...), custom_call_target="tpu_custom_call" | custom-call | flops 2000000000 | bytes 6000000 | tf_op jit(solution)/shard_map/pallas_call | solution.py:315
  31.6 0.7 collective-permute-start
  32.4 2.0 %collective-permute-start.1 = (f32[3,4,128]{2,1,0:T(4,128)S(1)}, f32[3,4,128]{2,1,0:T(4,128)S(1)}, u32[]{:S(2)}, u32[]{:S(2)}) collective-permute-start(f32[3,4,128]{2,1,0:T(4,128)S(1)} %get-tuple-element.46), channel_id=1, source_target_pairs={{1,2},{3,4},{5,6},{7,8},{9,10},{11,12},{13,14},{2,1},{4,3},{6,5},{... | collective-permute-start | bytes 18440 | tf_op jit(solution)/shard_map/ppermute | solution.py:416
  34.4 0.8 shard_map.173.negforce_ref
  35.2 0.0 collective-permute-done.ra_ref
  35.2 2.1 %collective-permute-done.1.rb_ref = f32[3,4,128]{2,1,0:T(4,128)S(1)} collective-permute-done((f32[3,4,128]{2,1,0:T(4,128)S(1)}, f32[3,4,128]{2,1,0:T(4,128)S(1)}, u32[]{:S(2)}, u32[]{:S(2)}) %collective-permute-start.1) | collective-permute-done | bytes 6176 | tf_op jit(solution)/shard_map/ppermute | solution.py:416
  37.3 2.2 %shard_map.174 = (f32[56,128]{1,0:T(8,128)S(1)}, f32[56,128]{1,0:T(8,128)S(1)}, f32[16,32,128]{2,1,0:T(8,128)}, f32[256,128]{1,0:T(8,128)S(1)}, f32[256,128]{1,0:T(8,128)S(1)}) custom-call(f32[56,128]{1,0:T(8,128)S(1)} %shard_map.173.negforce_ref, f32[3,4,128]{2,1,0:T(4,128)S(1)} %collective-permute-done.ra_ref, ...), custom_call_target="tpu_custom_call" | custom-call | flops 2000000000 | bytes 6000000 | tf_op jit(solution)/shard_map/pallas_call | solution.py:315
  39.5 3.5 %all-to-all-start.2 = ((f32[16,32,128]{2,1,0:T(8,128)}), f32[16,32,128]{2,1,0:T(8,128)S(1)}, u32[]{:S(2)}, u32[]{:S(2)}) async-start(f32[16,32,128]{2,1,0:T(8,128)} %get-tuple-element.52), calls=%async_computation.2 | async-start | bytes 524288 | tf_op jit(solution)/shard_map/all_to_all | solution.py:398
  43.0 4.0 %shard_map.175.elastic_ref = f32[56,128]{1,0:T(8,128)S(1)} custom-call(f32[56,128]{1,0:T(8,128)S(1)} %get-tuple-element.55.u_ref, s32[8,2048]{1,0:T(8,128)S(1)} %copy-done.1, f32[1,2048]{1,0:T(1,128)S(1)} %bitcast.14, f32[24,24]{1,0:T(8,128)S(1)} %copy-done.7), custom_call_target="tpu_custom_call" | custom-call | flops 5000000000 | bytes 15000000 | tf_op jit(solution)/shard_map/pallas_call | solution.py:315
  47.0 5.5 %all-to-all-done.2.recv_ref = f32[16,32,128]{2,1,0:T(8,128)S(1)} async-done(((f32[16,32,128]{2,1,0:T(8,128)}), f32[16,32,128]{2,1,0:T(8,128)S(1)}, u32[]{:S(2)}, u32[]{:S(2)}) %all-to-all-start.2) | async-done | bytes 262176 | tf_op jit(solution)/shard_map/all_to_all | solution.py:398
  52.5 1.2 %shard_map.176 = (f32[56,128]{1,0:T(8,128)S(1)}, f32[3,4,128]{2,1,0:T(4,128)S(1)}, f32[3,4,128]{2,1,0:T(4,128)S(1)}) custom-call(f32[16,32,128]{2,1,0:T(8,128)S(1)} %all-to-all-done.2.recv_ref, f32[256,128]{1,0:T(8,128)S(1)} %get-tuple-element.54.neg_gap_ref, bf16[192,768]{1,0:T(8,128)(2,1)S(1)} %get-tuple-element.42.slave_t_ref, ...), custom_call_target="tpu_custom_call" | custom-call | flops 2000000000 | bytes 6000000 | tf_op jit(solution)/shard_map/pallas_call | solution.py:315
  53.6 0.7 collective-permute-start.2
  54.3 2.0 %collective-permute-start.3 = (f32[3,4,128]{2,1,0:T(4,128)S(1)}, f32[3,4,128]{2,1,0:T(4,128)S(1)}, u32[]{:S(2)}, u32[]{:S(2)}) collective-permute-start(f32[3,4,128]{2,1,0:T(4,128)S(1)} %get-tuple-element.58), channel_id=1, source_target_pairs={{1,2},{3,4},{5,6},{7,8},{9,10},{11,12},{13,14},{2,1},{4,3},{6,5},{... | collective-permute-start | bytes 18440 | tf_op jit(solution)/shard_map/ppermute | solution.py:416
  56.4 0.8 shard_map.177.negforce_ref
  57.2 0.0 collective-permute-done.2.ra_ref
  57.2 2.1 %collective-permute-done.3.rb_ref = f32[3,4,128]{2,1,0:T(4,128)S(1)} collective-permute-done((f32[3,4,128]{2,1,0:T(4,128)S(1)}, f32[3,4,128]{2,1,0:T(4,128)S(1)}, u32[]{:S(2)}, u32[]{:S(2)}) %collective-permute-start.3) | collective-permute-done | bytes 6176 | tf_op jit(solution)/shard_map/ppermute | solution.py:416
  59.3 2.2 %shard_map.178 = (f32[56,128]{1,0:T(8,128)S(1)}, f32[56,128]{1,0:T(8,128)S(1)}, f32[16,32,128]{2,1,0:T(8,128)}, f32[256,128]{1,0:T(8,128)S(1)}, f32[256,128]{1,0:T(8,128)S(1)}) custom-call(f32[56,128]{1,0:T(8,128)S(1)} %shard_map.177.negforce_ref, f32[3,4,128]{2,1,0:T(4,128)S(1)} %collective-permute-done.2.ra_ref, ...), custom_call_target="tpu_custom_call" | custom-call | flops 2000000000 | bytes 6000000 | tf_op jit(solution)/shard_map/pallas_call | solution.py:315
  61.5 3.5 %all-to-all-start.3 = ((f32[16,32,128]{2,1,0:T(8,128)}), f32[16,32,128]{2,1,0:T(8,128)S(1)}, u32[]{:S(2)}, u32[]{:S(2)}) async-start(f32[16,32,128]{2,1,0:T(8,128)} %get-tuple-element.60), calls=%async_computation.3 | async-start | bytes 524288 | tf_op jit(solution)/shard_map/all_to_all | solution.py:398
  65.0 4.0 %shard_map.179.elastic_ref = f32[56,128]{1,0:T(8,128)S(1)} custom-call(f32[56,128]{1,0:T(8,128)S(1)} %get-tuple-element.63.u_ref, s32[8,2048]{1,0:T(8,128)S(1)} %copy-done.1, f32[1,2048]{1,0:T(1,128)S(1)} %bitcast.15, f32[24,24]{1,0:T(8,128)S(1)} %copy-done.7), custom_call_target="tpu_custom_call" | custom-call | flops 5000000000 | bytes 15000000 | tf_op jit(solution)/shard_map/pallas_call | solution.py:315
  69.0 5.5 %all-to-all-done.3.recv_ref = f32[16,32,128]{2,1,0:T(8,128)S(1)} async-done(((f32[16,32,128]{2,1,0:T(8,128)}), f32[16,32,128]{2,1,0:T(8,128)S(1)}, u32[]{:S(2)}, u32[]{:S(2)}) %all-to-all-start.3) | async-done | bytes 262176 | tf_op jit(solution)/shard_map/all_to_all | solution.py:398
  74.5 1.2 %shard_map.180 = (f32[56,128]{1,0:T(8,128)S(1)}, f32[3,4,128]{2,1,0:T(4,128)S(1)}, f32[3,4,128]{2,1,0:T(4,128)S(1)}) custom-call(f32[16,32,128]{2,1,0:T(8,128)S(1)} %all-to-all-done.3.recv_ref, f32[256,128]{1,0:T(8,128)S(1)} %get-tuple-element.62.neg_gap_ref, bf16[192,768]{1,0:T(8,128)(2,1)S(1)} %get-tuple-element.42.slave_t_ref, ...), custom_call_target="tpu_custom_call" | custom-call | flops 2000000000 | bytes 6000000 | tf_op jit(solution)/shard_map/pallas_call | solution.py:315
  75.7 0.7 collective-permute-start.4
  76.4 2.0 %collective-permute-start.5 = (f32[3,4,128]{2,1,0:T(4,128)S(1)}, f32[3,4,128]{2,1,0:T(4,128)S(1)}, u32[]{:S(2)}, u32[]{:S(2)}) collective-permute-start(f32[3,4,128]{2,1,0:T(4,128)S(1)} %get-tuple-element.66), channel_id=1, source_target_pairs={{1,2},{3,4},{5,6},{7,8},{9,10},{11,12},{13,14},{2,1},{4,3},{6,5},{... | collective-permute-start | bytes 18440 | tf_op jit(solution)/shard_map/ppermute | solution.py:416
  78.4 0.8 shard_map.181.negforce_ref
  79.2 0.0 collective-permute-done.4.ra_ref
  79.2 2.1 %collective-permute-done.5.rb_ref = f32[3,4,128]{2,1,0:T(4,128)S(1)} collective-permute-done((f32[3,4,128]{2,1,0:T(4,128)S(1)}, f32[3,4,128]{2,1,0:T(4,128)S(1)}, u32[]{:S(2)}, u32[]{:S(2)}) %collective-permute-start.5) | collective-permute-done | bytes 6176 | tf_op jit(solution)/shard_map/ppermute | solution.py:416
  81.3 0.9 %shard_map.182 = (f32[3,2176]{1,0:T(4,128)}, f32[3,2176]{1,0:T(4,128)}) custom-call(f32[56,128]{1,0:T(8,128)S(1)} %shard_map.181.negforce_ref, f32[3,4,128]{2,1,0:T(4,128)S(1)} %collective-permute-done.4.ra_ref, f32[3,4,128]{2,1,0:T(4,128)S(1)} %collective-permute-done.5.rb_ref, s32[8,128]{1,0:T(8,128)S(1)} %pad_add_fusion.faces_ref, ...), custom_call_target="tpu_custom_call" | custom-call | flops 1000000000 | bytes 3000000 | tf_op jit(solution)/shard_map/pallas_call | solution.py:315
  (23 shorter events, 0.1 us)
Async XLA Ops:
  0.6 0.7 copy-start.9
  0.6 0.7 copy-start.10
  0.7 0.7 copy-start.11
  1.3 8.5 %copy-start.13 = (f32[2176]{0:T(1024)S(1)}, f32[2176]{0:T(1024)}, u32[]{:S(2)}) copy-start(f32[2176]{0:T(1024)} %param.18) | copy-start | bytes 26116
  1.3 8.5 %copy-start.15 = (s32[512]{0:T(512)S(1)}, s32[512]{0:T(512)}, u32[]{:S(2)}) copy-start(s32[512]{0:T(512)} %param.29) | copy-start | bytes 6148
  1.3 9.2 %copy-start.2 = (f32[3,2176]{1,0:T(4,128)S(1)}, f32[3,2176]{1,0:T(4,128)}, u32[]{:S(2)}) copy-start(f32[3,2176]{1,0:T(4,128)} %u_ref.1) | copy-start | bytes 78340
  1.3 9.2 %copy-start.3 = (f32[3,2176]{1,0:T(4,128)S(1)}, f32[3,2176]{1,0:T(4,128)}, u32[]{:S(2)}) copy-start(f32[3,2176]{1,0:T(4,128)} %v_ref.1) | copy-start | bytes 78340
  1.3 9.2 %copy-start.4 = (f32[64,128]{1,0:T(8,128)S(1)}, f32[64,128]{1,0:T(8,128)}, u32[]{:S(2)}) copy-start(f32[64,128]{1,0:T(8,128)} %gap_ref.5) | copy-start | bytes 98308
  1.4 9.2 %copy-start.5 = (s32[64,128]{1,0:T(8,128)S(1)}, s32[64,128]{1,0:T(8,128)}, u32[]{:S(2)}) copy-start(s32[64,128]{1,0:T(8,128)} %snodes_ref.11) | copy-start | bytes 98308
  1.4 9.2 %copy-start.6 = (s32[32,128]{1,0:T(8,128)S(1)}, s32[32,128]{1,0:T(8,128)}, u32[]{:S(2)}) copy-start(s32[32,128]{1,0:T(8,128)} %mnodes_ref.11) | copy-start | bytes 49156
  2.3 8.2 %copy-start = (f32[128,128]{1,0:T(8,128)S(1)}, f32[128,128]{1,0:T(8,128)}, u32[]{:S(2)}) copy-start(f32[128,128]{1,0:T(8,128)} %mortar_ref.1) | copy-start | bytes 196612
  2.3 13.2 %all-to-all-start = ((f32[16,1,64]{2,1,0:T(1,128)}), f32[16,1,64]{2,1,0:T(1,128)S(1)}, u32[]{:S(2)}, u32[]{:S(2)}) async-start(f32[16,1,64]{2,1,0:T(1,128)} %bitcast.3), calls=%async_computation | async-start | bytes 16384 | tf_op jit(solution)/shard_map/all_to_all | solution.py:364
  9.8 0.7 copy-start.14
  10.5 0.7 copy-start.12
  16.7 4.2 %copy-start.1 = (s32[8,2048]{1,0:T(8,128)S(1)}, s32[8,2048]{1,0:T(8,128)}, u32[]{:S(2)}) copy-start(s32[8,2048]{1,0:T(8,128)} %conn_ref.5) | copy-start | bytes 196612
  16.7 4.2 %copy-start.7 = (f32[24,24]{1,0:T(8,128)S(1)}, f32[24,24]{1,0:T(8,128)}, u32[]{:S(2)}) copy-start(f32[24,24]{1,0:T(8,128)} %stiff_ref.5) | copy-start | bytes 6916
  16.7 4.2 %copy-start.8 = (f32[2048]{0:T(1024)S(1)}, f32[2048]{0:T(1024)}, u32[]{:S(2)}) copy-start(f32[2048]{0:T(1024)} %param.20) | copy-start | bytes 24580
  16.7 13.7 %all-to-all-start.1 = ((f32[16,32,128]{2,1,0:T(8,128)}), f32[16,32,128]{2,1,0:T(8,128)S(1)}, u32[]{:S(2)}, u32[]{:S(2)}) async-start(f32[16,32,128]{2,1,0:T(8,128)} %get-tuple-element.37), calls=%async_computation.1 | async-start | bytes 524288 | tf_op jit(solution)/shard_map/all_to_all | solution.py:398
  31.6 3.5 %collective-permute-start = (f32[3,4,128]{2,1,0:T(4,128)S(1)}, f32[3,4,128]{2,1,0:T(4,128)S(1)}, u32[]{:S(2)}, u32[]{:S(2)}) collective-permute-start(f32[3,4,128]{2,1,0:T(4,128)S(1)} %get-tuple-element.45), channel_id=1, source_target_pairs={{0,1},{1,0},{2,3},{3,2},{4,5},{5,4},{6,7},{7,6},{8,9},{9,8},{10,11... | collective-permute-start | bytes 18440 | tf_op jit(solution)/shard_map/ppermute | solution.py:415
  32.4 4.9 %collective-permute-start.1 = (f32[3,4,128]{2,1,0:T(4,128)S(1)}, f32[3,4,128]{2,1,0:T(4,128)S(1)}, u32[]{:S(2)}, u32[]{:S(2)}) collective-permute-start(f32[3,4,128]{2,1,0:T(4,128)S(1)} %get-tuple-element.46), channel_id=1, source_target_pairs={{1,2},{3,4},{5,6},{7,8},{9,10},{11,12},{13,14},{2,1},{4,3},{6,5},{... | collective-permute-start | bytes 18440 | tf_op jit(solution)/shard_map/ppermute | solution.py:416
  39.5 13.0 %all-to-all-start.2 = ((f32[16,32,128]{2,1,0:T(8,128)}), f32[16,32,128]{2,1,0:T(8,128)S(1)}, u32[]{:S(2)}, u32[]{:S(2)}) async-start(f32[16,32,128]{2,1,0:T(8,128)} %get-tuple-element.52), calls=%async_computation.2 | async-start | bytes 524288 | tf_op jit(solution)/shard_map/all_to_all | solution.py:398
  53.6 3.5 %collective-permute-start.2 = (f32[3,4,128]{2,1,0:T(4,128)S(1)}, f32[3,4,128]{2,1,0:T(4,128)S(1)}, u32[]{:S(2)}, u32[]{:S(2)}) collective-permute-start(f32[3,4,128]{2,1,0:T(4,128)S(1)} %get-tuple-element.57), channel_id=1, source_target_pairs={{0,1},{1,0},{2,3},{3,2},{4,5},{5,4},{6,7},{7,6},{8,9},{9,8},{10,11... | collective-permute-start | bytes 18440 | tf_op jit(solution)/shard_map/ppermute | solution.py:415
  54.3 4.9 %collective-permute-start.3 = (f32[3,4,128]{2,1,0:T(4,128)S(1)}, f32[3,4,128]{2,1,0:T(4,128)S(1)}, u32[]{:S(2)}, u32[]{:S(2)}) collective-permute-start(f32[3,4,128]{2,1,0:T(4,128)S(1)} %get-tuple-element.58), channel_id=1, source_target_pairs={{1,2},{3,4},{5,6},{7,8},{9,10},{11,12},{13,14},{2,1},{4,3},{6,5},{... | collective-permute-start | bytes 18440 | tf_op jit(solution)/shard_map/ppermute | solution.py:416
  61.5 13.0 %all-to-all-start.3 = ((f32[16,32,128]{2,1,0:T(8,128)}), f32[16,32,128]{2,1,0:T(8,128)S(1)}, u32[]{:S(2)}, u32[]{:S(2)}) async-start(f32[16,32,128]{2,1,0:T(8,128)} %get-tuple-element.60), calls=%async_computation.3 | async-start | bytes 524288 | tf_op jit(solution)/shard_map/all_to_all | solution.py:398
  75.7 3.5 %collective-permute-start.4 = (f32[3,4,128]{2,1,0:T(4,128)S(1)}, f32[3,4,128]{2,1,0:T(4,128)S(1)}, u32[]{:S(2)}, u32[]{:S(2)}) collective-permute-start(f32[3,4,128]{2,1,0:T(4,128)S(1)} %get-tuple-element.65), channel_id=1, source_target_pairs={{0,1},{1,0},{2,3},{3,2},{4,5},{5,4},{6,7},{7,6},{8,9},{9,8},{10,11... | collective-permute-start | bytes 18440 | tf_op jit(solution)/shard_map/ppermute | solution.py:415
  76.4 4.9 %collective-permute-start.5 = (f32[3,4,128]{2,1,0:T(4,128)S(1)}, f32[3,4,128]{2,1,0:T(4,128)S(1)}, u32[]{:S(2)}, u32[]{:S(2)}) collective-permute-start(f32[3,4,128]{2,1,0:T(4,128)S(1)} %get-tuple-element.66), channel_id=1, source_target_pairs={{1,2},{3,4},{5,6},{7,8},{9,10},{11,12},{13,14},{2,1},{4,3},{6,5},{... | collective-permute-start | bytes 18440 | tf_op jit(solution)/shard_map/ppermute | solution.py:416

commit v4 on v3

--- a/solution.py
+++ b/solution.py
@@ -128,22 +128,30 @@
     return lax.dot_general(a, b, NN, preferred_element_type=F32)
 
 
-def take_slots(block_ref, half, cap):
-    n_dom = block_ref.shape[0]
-    rows = slice(half * cap, (half + 1) * cap)
+def take_slots(block_ref, first, cap):
+    rows = slice(first, first + cap)
     if cap % 8 == 0:
-        return block_ref[:, rows, :].reshape(n_dom * cap, LANES)
-    return jnp.concatenate([block_ref[o, rows, :] for o in range(n_dom)], axis=0)
-
-
-def put_slots(block_ref, half, cap, value):
-    n_dom = block_ref.shape[0]
-    rows = slice(half * cap, (half + 1) * cap)
+        return block_ref[:, rows, :].reshape(-1, LANES)
+    return jnp.concatenate([block_ref[o, rows, :] for o in range(block_ref.shape[0])], axis=0)
+
+
+def put_slots(block_ref, first, cap, value):
+    rows = slice(first, first + cap)
     if cap % 8 == 0:
-        block_ref[:, rows, :] = value.reshape(n_dom, cap, LANES)
+        block_ref[:, rows, :] = value.reshape(-1, cap, LANES)
     else:
-        for o in range(n_dom):
+        for o in range(block_ref.shape[0]):
             block_ref[o, rows, :] = value[o * cap : (o + 1) * cap]
+
+
+def send_slots(slots_ref, out_ref, first, sem):
+    cap = slots_ref.shape[1]
+    if cap % 8:
+        put_slots(out_ref, first, cap, take_slots(slots_ref, 0, cap))
+        return []
+    copy = pltpu.make_async_copy(slots_ref, out_ref.at[:, pl.ds(first, cap), :], sem)
+    copy.start()
+    return [copy]
 
 
 def ranks(owner, n_dom):
@@ -170,11 +178,10 @@
     return [jnp.concatenate([b[c] for b in blocks], axis=0) for c in range(3)]
 
 
-def pair_values(u_ref, snodes_ref, mnodes_ref, gap_ref, mortar_t_ref, slave_ref):
+def pair_values(u_ref, snodes_ref, mnodes_ref, gap_ref, mortar_t_ref):
     um = jnp.concatenate(gathered(u_ref, mnodes_ref), axis=0)
-    mapped = product(as_right(um, 1), mortar_t_ref[...])
     us = jnp.concatenate([*gathered(u_ref, snodes_ref), gap_ref[...]], axis=0)
-    return mapped, product(slave_ref[...], as_right(us))
+    return product(as_right(um, 1), mortar_t_ref[...]), as_right(us)
 
 
 def prepare_kernel(
@@ -200,25 +207,28 @@
         for h in range(MAIN + 1):
             r = field_row(c, h)
             fm_ref[r : r + 1, :] = mass_ref[0:1, h * LANES : (h + 1) * LANES]
-    mapped, neg_gap = pair_values(fu_ref, snodes_ref, mnodes_ref, gap_ref, mortar_t_ref, slave_ref)
+    mapped, parts = pair_values(fu_ref, snodes_ref, mnodes_ref, gap_ref, mortar_t_ref)
     mapped_ref[...] = mapped
-    neg_gap_ref[...] = neg_gap
-
-
-def first_kernel(info_ref, mapped_ref, neg_gap_ref, out_ref, m_ref, master_ref, *, cap):
-    n_dom, masters = info_ref.shape[0], mapped_ref.shape[0] // 3
+    put_slots(neg_gap_ref, 0, cap, product(slave_ref[...], parts))
+
+
+def first_kernel(info_ref, mapped_ref, neg_gap_ref, out_ref, m_ref, master_ref, sem_ref):
+    n_dom, cap, _ = m_ref.shape
+    masters = mapped_ref.shape[0] // 3
+    copies = send_slots(neg_gap_ref, out_ref, cap, sem_ref.at[0])
     taken = jnp.concatenate([jnp.broadcast_to(info_ref[o : o + 1, :], (cap, 4 * cap)) for o in range(n_dom)], axis=0)
     mine = lax.rem(iota(taken.shape, 1), cap) == lax.rem(iota(taken.shape, 0), cap)
-    f = lax.div(iota((4 * cap, 2 * LANES), 0), cap)
+    f = lax.div(lax.rem(iota((8 * cap, 2 * LANES), 0), 4 * cap), cap)
     column = iota(f.shape, 1)
     spread = ((f == lax.div(column, masters)) & (column < LANES)) | ((f == 3) & (column >= LANES))
-    both = dot_exact(jnp.where(mine, taken, 0.0), spread.astype(F32), NN)
+    both = product(jnp.concatenate(two_parts(jnp.where(mine, taken, 0.0)), axis=1), spread.astype(F32).astype(BF16))
     number = lax.rem(iota((SLOTS, LANES), 1), masters).astype(F32)
     owned = jnp.where(jnp.abs(both[:, LANES:] - number) < 0.5, both[:, :LANES], 0.0)[:, : 3 * masters]
+    put_slots(m_ref, 0, cap, product(as_left(owned), as_right(mapped_ref[...])))
+    copies += send_slots(m_ref, out_ref, 0, sem_ref.at[1])
     master_ref[...] = owned
-    put_slots(out_ref, 1, cap, neg_gap_ref[...])
-    m_ref[...] = product(as_left(owned), as_right(mapped_ref[...]))
-    put_slots(out_ref, 0, cap, m_ref[...])
+    for copy in copies:
+        copy.wait()
 
 
 def turn_kernel(owned_ref, master_ref, master_t_ref):
@@ -261,10 +271,14 @@
     ]
 
 
+def face_rows(faces_ref, received_ref, first):
+    return [(faces_ref[first + k : first + k + 1, :], [received_ref[c, k : k + 1, :] for c in range(3)]) for k in range(4)]
+
+
 def contact_kernel(
     recv_ref, neg_gap_ref, slave_t_ref, elastic_ref, snodes_ref, faces_ref, local_ref, fa_ref, fb_ref, y_ref, *, cap
 ):
-    press = jnp.maximum(take_slots(recv_ref, 0, cap) + neg_gap_ref[...], 0.0)
+    press = jnp.maximum(take_slots(recv_ref, 0, cap) + take_slots(neg_gap_ref, 0, cap), 0.0)
     y_ref[...] = product(slave_t_ref[...], as_right(press))
     local_ref[...] = elastic_ref[...] + factor_sum(scatter(patch_rows(snodes_ref, y_ref)))
     found = gather8(local_ref, faces_ref[...])
@@ -273,50 +287,50 @@
         fb_ref[c, :, :] = found[c][4:]
 
 
-def master_kernel(recv_ref, m_ref, master_t_ref, mortar_ref, local_ref, mnodes_ref, out_ref, y_ref, *, cap):
-    press = jnp.maximum(m_ref[...] + take_slots(recv_ref, 1, cap), 0.0)
+def master_kernel(recv_ref, m_ref, master_t_ref, mortar_ref, local_ref, mnodes_ref, faces_ref, ra_ref, out_ref, y_ref, *, cap):
+    press = jnp.maximum(take_slots(m_ref, 0, cap) + take_slots(recv_ref, cap, cap), 0.0)
     summed = product(master_t_ref[...], as_right(press))
     y_ref[...] = product(as_right(summed, 1), mortar_ref[...])
-    out_ref[...] = local_ref[...] + factor_sum(scatter(patch_rows(mnodes_ref, y_ref)))
-
-
-def advance(negforce_ref, ra_ref, rb_ref, faces_ref, u_ref, v_ref, mass_ref):
-    rows = []
-    for k in range(8):
-        r_ref = ra_ref if k < 4 else rb_ref
-        rows.append((faces_ref[k : k + 1, :], [r_ref[c, k % 4 : k % 4 + 1, :] for c in range(3)]))
-    force = negforce_ref[...] + factor_sum(scatter(rows))
+    rows = patch_rows(mnodes_ref, y_ref) + face_rows(faces_ref, ra_ref, 0)
+    out_ref[...] = local_ref[...] + factor_sum(scatter(rows))
+
+
+def advance(negforce_ref, rb_ref, faces_ref, u_ref, v_ref, mass_ref):
+    force = negforce_ref[...] + factor_sum(scatter(face_rows(faces_ref, rb_ref, 4)))
     v = v_ref[...] - TIME_STEP * force / mass_ref[...]
     return u_ref[...] + TIME_STEP * v, v
 
 
 def next_kernel(
-    negforce_ref, ra_ref, rb_ref, faces_ref, u_ref, v_ref, mass_ref, snodes_ref, mnodes_ref, gap_ref, mortar_t_ref, slave_ref,
-    master_ref, nu_ref, nv_ref, out_ref, m_ref, neg_gap_ref, *, cap,
+    negforce_ref, rb_ref, faces_ref, u_ref, v_ref, mass_ref, snodes_ref, mnodes_ref, gap_ref, mortar_t_ref, slave_ref,
+    master_ref, nu_ref, nv_ref, out_ref, m_ref, neg_gap_ref, sem_ref,
 ):
-    u, v = advance(negforce_ref, ra_ref, rb_ref, faces_ref, u_ref, v_ref, mass_ref)
+    cap = m_ref.shape[1]
+    u, v = advance(negforce_ref, rb_ref, faces_ref, u_ref, v_ref, mass_ref)
     nu_ref[...] = u
     nv_ref[...] = v
-    mapped, neg_gap = pair_values(nu_ref, snodes_ref, mnodes_ref, gap_ref, mortar_t_ref, slave_ref)
-    neg_gap_ref[...] = neg_gap
-    put_slots(out_ref, 1, cap, neg_gap)
-    m_ref[...] = product(master_ref[...], as_right(mapped))
-    put_slots(out_ref, 0, cap, m_ref[...])
-
-
-def last_kernel(negforce_ref, ra_ref, rb_ref, faces_ref, u_ref, v_ref, mass_ref, nu_ref, nv_ref):
-    u, v = advance(negforce_ref, ra_ref, rb_ref, faces_ref, u_ref, v_ref, mass_ref)
+    mapped, parts = pair_values(nu_ref, snodes_ref, mnodes_ref, gap_ref, mortar_t_ref)
+    put_slots(m_ref, 0, cap, product(master_ref[...], as_right(mapped)))
+    copies = send_slots(m_ref, out_ref, 0, sem_ref.at[0])
+    put_slots(neg_gap_ref, 0, cap, product(slave_ref[...], parts))
+    copies += send_slots(neg_gap_ref, out_ref, cap, sem_ref.at[1])
+    for copy in copies:
+        copy.wait()
+
+
+def last_kernel(negforce_ref, rb_ref, faces_ref, u_ref, v_ref, mass_ref, nu_ref, nv_ref):
+    u, v = advance(negforce_ref, rb_ref, faces_ref, u_ref, v_ref, mass_ref)
     from_field(u, nu_ref)
     from_field(v, nv_ref)
 
 
-def call(kernel, outs, args, scratch=(), us=1.0):
+def call(kernel, outs, args, scratch=(), us=1.0, far=()):
     vmem = pl.BlockSpec(memory_space=pltpu.VMEM)
     return pl.pallas_call(
         kernel,
         out_shape=outs,
         in_specs=[vmem] * len(args),
-        out_specs=[vmem] * len(outs),
+        out_specs=[pl.BlockSpec(memory_space=pl.ANY) if i in far else vmem for i in range(len(outs))],
         scratch_shapes=list(scratch),
         compiler_params=pltpu.CompilerParams(vmem_limit_bytes=40 << 20),
         cost_estimate=pl.CostEstimate(flops=int(us * 1e9), bytes_accessed=int(us * 3e6), transcendentals=0),
@@ -347,6 +361,7 @@
     f32 = lambda *shape: jax.ShapeDtypeStruct(shape, F32)
     bf16 = lambda *shape: jax.ShapeDtypeStruct(shape, BF16)
     field = f32(ROWS, LANES)
+    slots = f32(n_dom, cap, LANES)
     owner = pair_owner.reshape(1, -1)
     even = lax.axis_index("dom") % 2 == 0
     faces = jnp.concatenate(
@@ -373,7 +388,7 @@
             field,
             field,
             f32(3 * masters, LANES),
-            f32(SLOTS, LANES),
+            slots,
         ],
         (
             owner,
@@ -390,10 +405,12 @@
         us=3.0,
     )
     blocks = f32(n_dom, 2 * cap, LANES)
-    slots = f32(SLOTS, LANES)
+    sems = [pltpu.SemaphoreType.DMA((2,))]
+    far = [] if cap % 8 else [0]
     out, m, owned = call(
-        functools.partial(first_kernel, cap=cap), [blocks, slots, f32(SLOTS, 3 * masters)], (info, mapped, neg_gap)
+        first_kernel, [blocks, slots, f32(SLOTS, 3 * masters)], (info, mapped, neg_gap), sems, far=far
     )
+    far = [] if cap % 8 else [2]
     for step in range(STEPS):
         recv = lax.all_to_all(out, "dom", 0, 0)
         (elastic,) = call(
@@ -417,16 +434,18 @@
         (negforce,) = call(
             functools.partial(master_kernel, cap=cap),
             [field],
-            (recv, m, master_t, mortar_left, local, master_nodes),
+            (recv, m, master_t, mortar_left, local, master_nodes, faces, ra),
             [pltpu.VMEM((3 * masters, LANES), F32)],
         )
-        state = (negforce, ra, rb, faces, u, v, mass)
+        state = (negforce, rb, faces, u, v, mass)
         if step < STEPS - 1:
             u, v, out, m, neg_gap = call(
-                functools.partial(next_kernel, cap=cap),
+                next_kernel,
                 [field, field, blocks, slots, slots],
                 (*state, slave_nodes, master_nodes, slave_gap, mortar_t, slave, master),
+                sems,
                 us=2.0,
+                far=far,
             )
         else:
             outs = [f32(*displacement.shape), f32(*velocity.shape)]

time: 82.8 us -> 82.8 us (level)
  no operation moved by 1% of the time
where the time goes in v4:
time: 82.8 us; the launch traced here: 82.1 us
  starting transfers between devices  27 us (33%)
  Pallas kernels  26.4 us (32%)
  waiting for transfers between devices  25.8 us (31%)
  local copies, waits for them, and re-layouts  1.98 us (2%)
  between operations  0.98 us (1%)
    pallas_call x16, Pallas kernels, call(): pl.pallas_call(kernel, out_shape=outs, in_specs=[vmem] * len(args), out_s...  26.4 us
    all_to_all x3, waiting for transfers between devices, shards(): recv = lax.all_to_all(out, 'dom', 0, 0)  15.7 us
    all_to_all x3, starting transfers between devices, shards(): recv = lax.all_to_all(out, 'dom', 0, 0)  11.2 us
    all_to_all x1, starting transfers between devices, shards(): info = lax.all_to_all(info, 'dom', 0, 0, tiled=True)  7.48 us
    ppermute x3, waiting for transfers between devices, shards(): rb = lax.ppermute(fb, 'dom', across)  6.19 us
    ppermute x3, starting transfers between devices, shards(): rb = lax.ppermute(fb, 'dom', across)  6.1 us
    all_to_all x1, waiting for transfers between devices, shards(): info = lax.all_to_all(info, 'dom', 0, 0, tiled=True)  3.83 us
    ppermute x3, starting transfers between devices, shards(): ra = lax.ppermute(fa, 'dom', inside)  2.17 us
  transfers between devices with their start and end apart: 10, of which 7 were waited for; matrix products, arithmetic and copies ran while one was open for 0% of the time, Pallas kernels for 19%

profile of v4, /device:TPU:1, one launch (start us, length us, event | category | flops | bytes accessed | tf_op | source)
XLA Modules:
  0.0 82.1 jit_solution(9615261325938640619)
XLA Ops:
  0.6 0.0 copy-start.9
  0.6 0.0 copy-start.10
  0.7 0.0 copy-start.11
  0.7 0.7 copy-done.9
  1.4 0.9 %shard_map.167 = f32[16,64]{1,0:T(8,128)} custom-call(s32[1,128]{1,0:T(1,128)S(1)} %bitcast.17, s32[1,128]{1,0:T(1,128)S(1)} %bitcast.16, f32[3,128]{1,0:T(4,128)S(1)} %copy-done.9), custom_call_target="tpu_custom_call" | custom-call | flops 1000000000 | bytes 3000000 | tf_op jit(solution)/shard_map/pallas_call | solution.py:329
  2.3 7.5 %all-to-all-start = ((f32[16,1,64]{2,1,0:T(1,128)}), f32[16,1,64]{2,1,0:T(1,128)S(1)}, u32[]{:S(2)}, u32[]{:S(2)}) async-start(f32[16,1,64]{2,1,0:T(1,128)} %bitcast.3), calls=%async_computation | async-start | bytes 16384 | tf_op jit(solution)/shard_map/all_to_all | solution.py:379
  9.8 0.0 copy-done.13
  9.8 0.0 copy-start.12
  9.8 0.0 copy-done.2
  9.8 0.0 copy-done.3
  9.9 0.6 copy-done.12
  10.5 1.2 %shard_map.168 = (bf16[256,768]{1,0:T(8,128)(2,1)S(1)}, bf16[192,768]{1,0:T(8,128)(2,1)S(1)}, bf16[384,128]{1,0:T(8,128)(2,1)S(1)}, bf16[384,128]{1,0:T(8,128)(2...) custom-call(s32[1,128]{1,0:T(1,128)S(1)} %bitcast.18, ...), custom_call_target="tpu_custom_call" | custom-call | flops 3000000000 | bytes 9000000 | tf_op jit(solution)/shard_map/pallas_call | solution.py:329
  11.7 3.8 %all-to-all-done = f32[16,1,64]{2,1,0:T(1,128)S(1)} async-done(((f32[16,1,64]{2,1,0:T(1,128)}), f32[16,1,64]{2,1,0:T(1,128)S(1)}, u32[]{:S(2)}, u32[]{:S(2)}) %all-to-all-start) | async-done | bytes 4128 | tf_op jit(solution)/shard_map/all_to_all | solution.py:379
  15.5 1.1 %shard_map.169 = (f32[16,32,128]{2,1,0:T(8,128)}, f32[16,16,128]{2,1,0:T(8,128)S(1)}, f32[256,96]{1,0:T(8,128)S(1)}) custom-call(f32[16,64]{1,0:T(8,128)S(1)} %bitcast.12, f32[96,128]{1,0:T(8,128)S(1)} %get-tuple-element.35.mapped_ref, f32[16,16,128]{2,1,0:T(8,128)S(1)} %get-tuple-element.36.neg_gap_ref), custom_call_target="tpu_custom_call" | custom-call | flops 1000000000 | bytes 3000000 | tf_op jit(solution)/shard_map/pallas_call | solution.py:329
  16.6 0.0 copy-start.1
  16.6 0.0 copy-start.8
  16.7 4.2 %all-to-all-start.1 = ((f32[16,32,128]{2,1,0:T(8,128)}), f32[16,32,128]{2,1,0:T(8,128)S(1)}, u32[]{:S(2)}, u32[]{:S(2)}) async-start(f32[16,32,128]{2,1,0:T(8,128)} %get-tuple-element.37), calls=%async_computation.1 | async-start | bytes 524288 | tf_op jit(solution)/shard_map/all_to_all | solution.py:415
  20.9 0.7 copy-done.7
  21.5 4.0 %shard_map.171.elastic_ref = f32[56,128]{1,0:T(8,128)S(1)} custom-call(f32[56,128]{1,0:T(8,128)S(1)} %get-tuple-element.43.u_ref, s32[8,2048]{1,0:T(8,128)S(1)} %copy-done.1, f32[1,2048]{1,0:T(1,128)S(1)} %bitcast.13, f32[24,24]{1,0:T(8,128)S(1)} %copy-done.7), custom_call_target="tpu_custom_call" | custom-call | flops 5000000000 | bytes 15000000 | tf_op jit(solution)/shard_map/pallas_call | solution.py:329
  25.6 4.8 %all-to-all-done.1.recv_ref = f32[16,32,128]{2,1,0:T(8,128)S(1)} async-done(((f32[16,32,128]{2,1,0:T(8,128)}), f32[16,32,128]{2,1,0:T(8,128)S(1)}, u32[]{:S(2)}, u32[]{:S(2)}) %all-to-all-start.1) | async-done | bytes 262176 | tf_op jit(solution)/shard_map/all_to_all | solution.py:415
  30.4 1.2 %shard_map.172 = (f32[56,128]{1,0:T(8,128)S(1)}, f32[3,4,128]{2,1,0:T(4,128)S(1)}, f32[3,4,128]{2,1,0:T(4,128)S(1)}) custom-call(f32[16,32,128]{2,1,0:T(8,128)S(1)} %all-to-all-done.1.recv_ref, f32[16,16,128]{2,1,0:T(8,128)S(1)} %get-tuple-element.36.neg_gap_ref, bf16[192,768]{1,0:T(8,128)(2,1)S(1)} %get-tuple-element.42.slave_t_ref, ...), custom_call_target="tpu_custom_call" | custom-call | flops 2000000000 | bytes 6000000 | tf_op jit(solution)/shard_map/pallas_call | solution.py:329
  31.6 0.7 collective-permute-start
  32.3 0.3 shard_map.170
  32.6 2.0 %collective-permute-start.1 = (f32[3,4,128]{2,1,0:T(4,128)S(1)}, f32[3,4,128]{2,1,0:T(4,128)S(1)}, u32[]{:S(2)}, u32[]{:S(2)}) collective-permute-start(f32[3,4,128]{2,1,0:T(4,128)S(1)} %get-tuple-element.46), channel_id=1, source_target_pairs={{1,2},{3,4},{5,6},{7,8},{9,10},{11,12},{13,14},{2,1},{4,3},{6,5},{... | collective-permute-start | bytes 18440 | tf_op jit(solution)/shard_map/ppermute | solution.py:433
  34.6 0.0 collective-permute-done.ra_ref
  34.6 0.8 shard_map.173.negforce_ref
  35.4 2.1 %collective-permute-done.1.rb_ref = f32[3,4,128]{2,1,0:T(4,128)S(1)} collective-permute-done((f32[3,4,128]{2,1,0:T(4,128)S(1)}, f32[3,4,128]{2,1,0:T(4,128)S(1)}, u32[]{:S(2)}, u32[]{:S(2)}) %collective-permute-start.1) | collective-permute-done | bytes 6176 | tf_op jit(solution)/shard_map/ppermute | solution.py:433
  37.5 2.0 %shard_map.174 = (f32[56,128]{1,0:T(8,128)S(1)}, f32[56,128]{1,0:T(8,128)S(1)}, f32[16,32,128]{2,1,0:T(8,128)}, f32[16,16,128]{2,1,0:T(8,128)S(1)}, f32[16,16,128]{2,1,0:T(8,128)S(1)}) custom-call(f32[56,128]{1,0:T(8,128)S(1)} %shard_map.173.negforce_ref, f32[3,4,128]{2,1,0:T(4,128)S(1)} %collective-permute-done.1.rb_ref, ...), custom_call_target="tpu_custom_call" | custom-call | flops 2000000000 | bytes 6000000 | tf_op jit(solution)/shard_map/pallas_call | solution.py:329
  39.5 3.5 %all-to-all-start.2 = ((f32[16,32,128]{2,1,0:T(8,128)}), f32[16,32,128]{2,1,0:T(8,128)S(1)}, u32[]{:S(2)}, u32[]{:S(2)}) async-start(f32[16,32,128]{2,1,0:T(8,128)} %get-tuple-element.52), calls=%async_computation.2 | async-start | bytes 524288 | tf_op jit(solution)/shard_map/all_to_all | solution.py:415
  43.0 4.0 %shard_map.175.elastic_ref = f32[56,128]{1,0:T(8,128)S(1)} custom-call(f32[56,128]{1,0:T(8,128)S(1)} %get-tuple-element.55.u_ref, s32[8,2048]{1,0:T(8,128)S(1)} %copy-done.1, f32[1,2048]{1,0:T(1,128)S(1)} %bitcast.14, f32[24,24]{1,0:T(8,128)S(1)} %copy-done.7), custom_call_target="tpu_custom_call" | custom-call | flops 5000000000 | bytes 15000000 | tf_op jit(solution)/shard_map/pallas_call | solution.py:329
  47.0 5.5 %all-to-all-done.2.recv_ref = f32[16,32,128]{2,1,0:T(8,128)S(1)} async-done(((f32[16,32,128]{2,1,0:T(8,128)}), f32[16,32,128]{2,1,0:T(8,128)S(1)}, u32[]{:S(2)}, u32[]{:S(2)}) %all-to-all-start.2) | async-done | bytes 262176 | tf_op jit(solution)/shard_map/all_to_all | solution.py:415
  52.5 1.2 %shard_map.176 = (f32[56,128]{1,0:T(8,128)S(1)}, f32[3,4,128]{2,1,0:T(4,128)S(1)}, f32[3,4,128]{2,1,0:T(4,128)S(1)}) custom-call(f32[16,32,128]{2,1,0:T(8,128)S(1)} %all-to-all-done.2.recv_ref, f32[16,16,128]{2,1,0:T(8,128)S(1)} %get-tuple-element.54.neg_gap_ref, bf16[192,768]{1,0:T(8,128)(2,1)S(1)} %get-tuple-element.42.slave_t_ref, ...), custom_call_target="tpu_custom_call" | custom-call | flops 2000000000 | bytes 6000000 | tf_op jit(solution)/shard_map/pallas_call | solution.py:329
  53.7 0.7 collective-permute-start.2
  54.4 2.0 %collective-permute-start.3 = (f32[3,4,128]{2,1,0:T(4,128)S(1)}, f32[3,4,128]{2,1,0:T(4,128)S(1)}, u32[]{:S(2)}, u32[]{:S(2)}) collective-permute-start(f32[3,4,128]{2,1,0:T(4,128)S(1)} %get-tuple-element.58), channel_id=1, source_target_pairs={{1,2},{3,4},{5,6},{7,8},{9,10},{11,12},{13,14},{2,1},{4,3},{6,5},{... | collective-permute-start | bytes 18440 | tf_op jit(solution)/shard_map/ppermute | solution.py:433
  56.4 0.0 collective-permute-done.2.ra_ref
  56.5 0.8 shard_map.177.negforce_ref
  57.3 2.1 %collective-permute-done.3.rb_ref = f32[3,4,128]{2,1,0:T(4,128)S(1)} collective-permute-done((f32[3,4,128]{2,1,0:T(4,128)S(1)}, f32[3,4,128]{2,1,0:T(4,128)S(1)}, u32[]{:S(2)}, u32[]{:S(2)}) %collective-permute-start.3) | collective-permute-done | bytes 6176 | tf_op jit(solution)/shard_map/ppermute | solution.py:433
  59.3 2.0 %shard_map.178 = (f32[56,128]{1,0:T(8,128)S(1)}, f32[56,128]{1,0:T(8,128)S(1)}, f32[16,32,128]{2,1,0:T(8,128)}, f32[16,16,128]{2,1,0:T(8,128)S(1)}, f32[16,16,128]{2,1,0:T(8,128)S(1)}) custom-call(f32[56,128]{1,0:T(8,128)S(1)} %shard_map.177.negforce_ref, f32[3,4,128]{2,1,0:T(4,128)S(1)} %collective-permute-done.3.rb_ref, ...), custom_call_target="tpu_custom_call" | custom-call | flops 2000000000 | bytes 6000000 | tf_op jit(solution)/shard_map/pallas_call | solution.py:329
  61.4 3.5 %all-to-all-start.3 = ((f32[16,32,128]{2,1,0:T(8,128)}), f32[16,32,128]{2,1,0:T(8,128)S(1)}, u32[]{:S(2)}, u32[]{:S(2)}) async-start(f32[16,32,128]{2,1,0:T(8,128)} %get-tuple-element.60), calls=%async_computation.3 | async-start | bytes 524288 | tf_op jit(solution)/shard_map/all_to_all | solution.py:415
  64.9 4.0 %shard_map.179.elastic_ref = f32[56,128]{1,0:T(8,128)S(1)} custom-call(f32[56,128]{1,0:T(8,128)S(1)} %get-tuple-element.63.u_ref, s32[8,2048]{1,0:T(8,128)S(1)} %copy-done.1, f32[1,2048]{1,0:T(1,128)S(1)} %bitcast.15, f32[24,24]{1,0:T(8,128)S(1)} %copy-done.7), custom_call_target="tpu_custom_call" | custom-call | flops 5000000000 | bytes 15000000 | tf_op jit(solution)/shard_map/pallas_call | solution.py:329
  69.0 5.5 %all-to-all-done.3.recv_ref = f32[16,32,128]{2,1,0:T(8,128)S(1)} async-done(((f32[16,32,128]{2,1,0:T(8,128)}), f32[16,32,128]{2,1,0:T(8,128)S(1)}, u32[]{:S(2)}, u32[]{:S(2)}) %all-to-all-start.3) | async-done | bytes 262176 | tf_op jit(solution)/shard_map/all_to_all | solution.py:415
  74.4 1.2 %shard_map.180 = (f32[56,128]{1,0:T(8,128)S(1)}, f32[3,4,128]{2,1,0:T(4,128)S(1)}, f32[3,4,128]{2,1,0:T(4,128)S(1)}) custom-call(f32[16,32,128]{2,1,0:T(8,128)S(1)} %all-to-all-done.3.recv_ref, f32[16,16,128]{2,1,0:T(8,128)S(1)} %get-tuple-element.62.neg_gap_ref, bf16[192,768]{1,0:T(8,128)(2,1)S(1)} %get-tuple-element.42.slave_t_ref, ...), custom_call_target="tpu_custom_call" | custom-call | flops 2000000000 | bytes 6000000 | tf_op jit(solution)/shard_map/pallas_call | solution.py:329
  75.6 0.7 collective-permute-start.4
  76.3 2.0 %collective-permute-start.5 = (f32[3,4,128]{2,1,0:T(4,128)S(1)}, f32[3,4,128]{2,1,0:T(4,128)S(1)}, u32[]{:S(2)}, u32[]{:S(2)}) collective-permute-start(f32[3,4,128]{2,1,0:T(4,128)S(1)} %get-tuple-element.66), channel_id=1, source_target_pairs={{1,2},{3,4},{5,6},{7,8},{9,10},{11,12},{13,14},{2,1},{4,3},{6,5},{... | collective-permute-start | bytes 18440 | tf_op jit(solution)/shard_map/ppermute | solution.py:433
  78.3 0.0 collective-permute-done.4.ra_ref
  78.4 0.8 shard_map.181.negforce_ref
  79.2 2.1 %collective-permute-done.5.rb_ref = f32[3,4,128]{2,1,0:T(4,128)S(1)} collective-permute-done((f32[3,4,128]{2,1,0:T(4,128)S(1)}, f32[3,4,128]{2,1,0:T(4,128)S(1)}, u32[]{:S(2)}, u32[]{:S(2)}) %collective-permute-start.5) | collective-permute-done | bytes 6176 | tf_op jit(solution)/shard_map/ppermute | solution.py:433
  81.2 0.8 %shard_map.182 = (f32[3,2176]{1,0:T(4,128)}, f32[3,2176]{1,0:T(4,128)}) custom-call(f32[56,128]{1,0:T(8,128)S(1)} %shard_map.181.negforce_ref, f32[3,4,128]{2,1,0:T(4,128)S(1)} %collective-permute-done.5.rb_ref, s32[8,128]{1,0:T(8,128)S(1)} %pad_add_fusion.faces_ref, f32[56,128]{1,0:T(8,128)S(1)} %get-tuple-element.63.u_ref, ...), custom_call_target="tpu_custom_call" | custom-call | flops 1000000000 | bytes 3000000 | tf_op jit(solution)/shard_map/pallas_call | solution.py:329
  (23 shorter events, 0.1 us)
Async XLA Ops:
  0.6 0.7 copy-start.9
  0.6 0.7 copy-start.10
  0.7 0.7 copy-start.11
  1.3 8.5 %copy-start.13 = (f32[2176]{0:T(1024)S(1)}, f32[2176]{0:T(1024)}, u32[]{:S(2)}) copy-start(f32[2176]{0:T(1024)} %param.18) | copy-start | bytes 26116
  1.3 8.5 %copy-start.2 = (f32[3,2176]{1,0:T(4,128)S(1)}, f32[3,2176]{1,0:T(4,128)}, u32[]{:S(2)}) copy-start(f32[3,2176]{1,0:T(4,128)} %u_ref.1) | copy-start | bytes 78340
  1.3 8.5 %copy-start.3 = (f32[3,2176]{1,0:T(4,128)S(1)}, f32[3,2176]{1,0:T(4,128)}, u32[]{:S(2)}) copy-start(f32[3,2176]{1,0:T(4,128)} %v_ref.1) | copy-start | bytes 78340
  1.3 8.5 %copy-start.4 = (f32[64,128]{1,0:T(8,128)S(1)}, f32[64,128]{1,0:T(8,128)}, u32[]{:S(2)}) copy-start(f32[64,128]{1,0:T(8,128)} %gap_ref.5) | copy-start | bytes 98308
  1.3 8.5 %copy-start.5 = (s32[64,128]{1,0:T(8,128)S(1)}, s32[64,128]{1,0:T(8,128)}, u32[]{:S(2)}) copy-start(s32[64,128]{1,0:T(8,128)} %snodes_ref.11) | copy-start | bytes 98308
  1.4 8.5 %copy-start.6 = (s32[32,128]{1,0:T(8,128)S(1)}, s32[32,128]{1,0:T(8,128)}, u32[]{:S(2)}) copy-start(s32[32,128]{1,0:T(8,128)} %mnodes_ref.11) | copy-start | bytes 49156
  2.3 7.6 %copy-start = (f32[128,128]{1,0:T(8,128)S(1)}, f32[128,128]{1,0:T(8,128)}, u32[]{:S(2)}) copy-start(f32[128,128]{1,0:T(8,128)} %mortar_ref.1) | copy-start | bytes 196612
  2.3 13.2 %all-to-all-start = ((f32[16,1,64]{2,1,0:T(1,128)}), f32[16,1,64]{2,1,0:T(1,128)S(1)}, u32[]{:S(2)}, u32[]{:S(2)}) async-start(f32[16,1,64]{2,1,0:T(1,128)} %bitcast.3), calls=%async_computation | async-start | bytes 16384 | tf_op jit(solution)/shard_map/all_to_all | solution.py:379
  9.8 0.7 copy-start.12
  10.5 1.2 %copy-start.14 = (s32[512]{0:T(512)S(1)}, s32[512]{0:T(512)}, u32[]{:S(2)}) copy-start(s32[512]{0:T(512)} %param.30) | copy-start | bytes 6148
  10.5 1.2 %copy-start.15 = (s32[512]{0:T(512)S(1)}, s32[512]{0:T(512)}, u32[]{:S(2)}) copy-start(s32[512]{0:T(512)} %param.29) | copy-start | bytes 6148
  16.6 4.2 %copy-start.1 = (s32[8,2048]{1,0:T(8,128)S(1)}, s32[8,2048]{1,0:T(8,128)}, u32[]{:S(2)}) copy-start(s32[8,2048]{1,0:T(8,128)} %conn_ref.5) | copy-start | bytes 196612
  16.6 4.2 %copy-start.8 = (f32[2048]{0:T(1024)S(1)}, f32[2048]{0:T(1024)}, u32[]{:S(2)}) copy-start(f32[2048]{0:T(1024)} %param.20) | copy-start | bytes 24580
  16.7 13.7 %all-to-all-start.1 = ((f32[16,32,128]{2,1,0:T(8,128)}), f32[16,32,128]{2,1,0:T(8,128)S(1)}, u32[]{:S(2)}, u32[]{:S(2)}) async-start(f32[16,32,128]{2,1,0:T(8,128)} %get-tuple-element.37), calls=%async_computation.1 | async-start | bytes 524288 | tf_op jit(solution)/shard_map/all_to_all | solution.py:415
  20.8 0.7 copy-start.7
  31.6 3.0 %collective-permute-start = (f32[3,4,128]{2,1,0:T(4,128)S(1)}, f32[3,4,128]{2,1,0:T(4,128)S(1)}, u32[]{:S(2)}, u32[]{:S(2)}) collective-permute-start(f32[3,4,128]{2,1,0:T(4,128)S(1)} %get-tuple-element.45), channel_id=1, source_target_pairs={{0,1},{1,0},{2,3},{3,2},{4,5},{5,4},{6,7},{7,6},{8,9},{9,8},{10,11... | collective-permute-start | bytes 18440 | tf_op jit(solution)/shard_map/ppermute | solution.py:432
  32.6 4.9 %collective-permute-start.1 = (f32[3,4,128]{2,1,0:T(4,128)S(1)}, f32[3,4,128]{2,1,0:T(4,128)S(1)}, u32[]{:S(2)}, u32[]{:S(2)}) collective-permute-start(f32[3,4,128]{2,1,0:T(4,128)S(1)} %get-tuple-element.46), channel_id=1, source_target_pairs={{1,2},{3,4},{5,6},{7,8},{9,10},{11,12},{13,14},{2,1},{4,3},{6,5},{... | collective-permute-start | bytes 18440 | tf_op jit(solution)/shard_map/ppermute | solution.py:433
  39.5 13.0 %all-to-all-start.2 = ((f32[16,32,128]{2,1,0:T(8,128)}), f32[16,32,128]{2,1,0:T(8,128)S(1)}, u32[]{:S(2)}, u32[]{:S(2)}) async-start(f32[16,32,128]{2,1,0:T(8,128)} %get-tuple-element.52), calls=%async_computation.2 | async-start | bytes 524288 | tf_op jit(solution)/shard_map/all_to_all | solution.py:415
  53.7 2.8 %collective-permute-start.2 = (f32[3,4,128]{2,1,0:T(4,128)S(1)}, f32[3,4,128]{2,1,0:T(4,128)S(1)}, u32[]{:S(2)}, u32[]{:S(2)}) collective-permute-start(f32[3,4,128]{2,1,0:T(4,128)S(1)} %get-tuple-element.57), channel_id=1, source_target_pairs={{0,1},{1,0},{2,3},{3,2},{4,5},{5,4},{6,7},{7,6},{8,9},{9,8},{10,11... | collective-permute-start | bytes 18440 | tf_op jit(solution)/shard_map/ppermute | solution.py:432
  54.4 4.9 %collective-permute-start.3 = (f32[3,4,128]{2,1,0:T(4,128)S(1)}, f32[3,4,128]{2,1,0:T(4,128)S(1)}, u32[]{:S(2)}, u32[]{:S(2)}) collective-permute-start(f32[3,4,128]{2,1,0:T(4,128)S(1)} %get-tuple-element.58), channel_id=1, source_target_pairs={{1,2},{3,4},{5,6},{7,8},{9,10},{11,12},{13,14},{2,1},{4,3},{6,5},{... | collective-permute-start | bytes 18440 | tf_op jit(solution)/shard_map/ppermute | solution.py:433
  61.4 13.0 %all-to-all-start.3 = ((f32[16,32,128]{2,1,0:T(8,128)}), f32[16,32,128]{2,1,0:T(8,128)S(1)}, u32[]{:S(2)}, u32[]{:S(2)}) async-start(f32[16,32,128]{2,1,0:T(8,128)} %get-tuple-element.60), calls=%async_computation.3 | async-start | bytes 524288 | tf_op jit(solution)/shard_map/all_to_all | solution.py:415
  75.6 2.8 %collective-permute-start.4 = (f32[3,4,128]{2,1,0:T(4,128)S(1)}, f32[3,4,128]{2,1,0:T(4,128)S(1)}, u32[]{:S(2)}, u32[]{:S(2)}) collective-permute-start(f32[3,4,128]{2,1,0:T(4,128)S(1)} %get-tuple-element.65), channel_id=1, source_target_pairs={{0,1},{1,0},{2,3},{3,2},{4,5},{5,4},{6,7},{7,6},{8,9},{9,8},{10,11... | collective-permute-start | bytes 18440 | tf_op jit(solution)/shard_map/ppermute | solution.py:432
  76.3 4.9 %collective-permute-start.5 = (f32[3,4,128]{2,1,0:T(4,128)S(1)}, f32[3,4,128]{2,1,0:T(4,128)S(1)}, u32[]{:S(2)}, u32[]{:S(2)}) collective-permute-start(f32[3,4,128]{2,1,0:T(4,128)S(1)} %get-tuple-element.66), channel_id=1, source_target_pairs={{1,2},{3,4},{5,6},{7,8},{9,10},{11,12},{13,14},{2,1},{4,3},{6,5},{... | collective-permute-start | bytes 18440 | tf_op jit(solution)/shard_map/ppermute | solution.py:433

commit v5 on v4

--- a/solution.py
+++ b/solution.py
@@ -156,10 +156,9 @@
 
 def ranks(owner, n_dom):
     n = owner.shape[1]
-    at = (iota((n_dom, n), 0) == owner).astype(F32)
-    before = (iota((n, n), 0) < iota((n, n), 1)).astype(F32)
-    counts = lax.dot_general(at.astype(BF16), before.astype(BF16), NN, preferred_element_type=F32)
-    return jnp.sum(at * counts, axis=0, keepdims=True), at
+    across = jnp.broadcast_to(owner.astype(F32), (n, n))
+    same = (across.T == across) & (iota((n, n), 0) < iota((n, n), 1))
+    return jnp.sum(same.astype(F32), axis=0, keepdims=True), (iota((n_dom, n), 0) == owner).astype(F32)
 
 
 def info_kernel(owner_ref, master_ref, normal_ref, out_ref, *, n_dom, cap):
@@ -178,15 +177,34 @@
     return [jnp.concatenate([b[c] for b in blocks], axis=0) for c in range(3)]
 
 
-def pair_values(u_ref, snodes_ref, mnodes_ref, gap_ref, mortar_t_ref):
+def gathered_by_product(field, nodes_ref, out_ref):
+    high, low = two_parts(field)
+    m, patches = 3 * MAIN, nodes_ref.shape[0]
+    tails = jnp.concatenate([high[m:].astype(F32), low[m:].astype(F32)], axis=0).astype(BF16)
+    table = jnp.concatenate([high[:m], low[:m], tails], axis=0)
+    for j in range(0, patches, GROUP):
+        hot = jnp.concatenate([lane_factor(nodes_ref[j + k : j + k + 1, :]) for k in range(GROUP)], axis=1)
+        found = lax.dot_general(table, hot, NN, preferred_element_type=F32)
+        body, tail = found[:m] + found[m : 2 * m], found[2 * m : 2 * m + 8] + found[2 * m + 8 :]
+        for k in range(GROUP):
+            columns = slice(k * LANES, (k + 1) * LANES)
+            upper = nodes_ref[j + k : j + k + 1, :] >> 7
+            here = iota((MAIN, LANES), 0) == upper
+            for c in range(3):
+                picked = jnp.where(here, body[c * MAIN : (c + 1) * MAIN, columns], 0.0)
+                row = jnp.sum(picked, axis=0, keepdims=True)
+                out_ref[c * patches + j + k : c * patches + j + k + 1, :] = jnp.where(upper < MAIN, row, tail[c : c + 1, columns])
+
+
+def pair_values(u_ref, snodes_ref, mnodes_ref, mortar_t_ref):
     um = jnp.concatenate(gathered(u_ref, mnodes_ref), axis=0)
-    us = jnp.concatenate([*gathered(u_ref, snodes_ref), gap_ref[...]], axis=0)
+    us = jnp.concatenate(gathered(u_ref, snodes_ref), axis=0)
     return product(as_right(um, 1), mortar_t_ref[...]), as_right(us)
 
 
 def prepare_kernel(
     owner_ref, pair_slave_ref, normal_ref, u_ref, v_ref, mass_ref, snodes_ref, mnodes_ref, gap_ref, mortar_ref,
-    slave_ref, slave_t_ref, mortar_left_ref, mortar_t_ref, fu_ref, fv_ref, fm_ref, mapped_ref, neg_gap_ref, *, n_dom, cap,
+    slave_ref, slave_t_ref, mortar_left_ref, mortar_t_ref, fu_ref, fv_ref, fm_ref, mapped_ref, neg_gap_ref, start_ref, *, n_dom, cap,
 ):
     owner, patches = owner_ref[...], snodes_ref.shape[0]
     n = owner.shape[1]
@@ -195,8 +213,9 @@
     hit = iota((patches, n), 0) == pair_slave_ref[...]
     parts = [jnp.where(hit, jnp.broadcast_to(-normal_ref[c : c + 1, :], hit.shape), 0.0) for c in range(3)]
     slave_t_ref[...] = as_left(dot_exact(jnp.concatenate(parts, axis=0), place, NT))
-    parts.append(jnp.where(hit, -1.0, 0.0))
     slave_ref[...] = as_left(dot_exact(place, jnp.concatenate(parts, axis=0), NT))
+    start = dot_exact(dot_exact(place, jnp.where(hit, -1.0, 0.0), NT), gap_ref[...], NN)
+    start_ref[...] = start
     mortar = mortar_ref[...]
     mortar_left_ref[...] = as_left(mortar, 0)
     mortar_t_ref[...] = as_left(mortar.T, 0)
@@ -207,9 +226,9 @@
         for h in range(MAIN + 1):
             r = field_row(c, h)
             fm_ref[r : r + 1, :] = mass_ref[0:1, h * LANES : (h + 1) * LANES]
-    mapped, parts = pair_values(fu_ref, snodes_ref, mnodes_ref, gap_ref, mortar_t_ref)
+    mapped, parts = pair_values(fu_ref, snodes_ref, mnodes_ref, mortar_t_ref)
     mapped_ref[...] = mapped
-    put_slots(neg_gap_ref, 0, cap, product(slave_ref[...], parts))
+    put_slots(neg_gap_ref, 0, cap, start + product(slave_ref[...], parts))
 
 
 def first_kernel(info_ref, mapped_ref, neg_gap_ref, out_ref, m_ref, master_ref, sem_ref):
@@ -302,17 +321,19 @@
 
 
 def next_kernel(
-    negforce_ref, rb_ref, faces_ref, u_ref, v_ref, mass_ref, snodes_ref, mnodes_ref, gap_ref, mortar_t_ref, slave_ref,
-    master_ref, nu_ref, nv_ref, out_ref, m_ref, neg_gap_ref, sem_ref,
+    negforce_ref, rb_ref, faces_ref, u_ref, v_ref, mass_ref, snodes_ref, mnodes_ref, start_ref, mortar_t_ref, slave_ref,
+    master_ref, nu_ref, nv_ref, out_ref, m_ref, neg_gap_ref, sem_ref, um_ref,
 ):
     cap = m_ref.shape[1]
     u, v = advance(negforce_ref, rb_ref, faces_ref, u_ref, v_ref, mass_ref)
     nu_ref[...] = u
     nv_ref[...] = v
-    mapped, parts = pair_values(nu_ref, snodes_ref, mnodes_ref, gap_ref, mortar_t_ref)
+    gathered_by_product(u, mnodes_ref, um_ref)
+    mapped = product(as_right(um_ref[...], 1), mortar_t_ref[...])
+    parts = as_right(jnp.concatenate(gathered(nu_ref, snodes_ref), axis=0))
     put_slots(m_ref, 0, cap, product(master_ref[...], as_right(mapped)))
     copies = send_slots(m_ref, out_ref, 0, sem_ref.at[0])
-    put_slots(neg_gap_ref, 0, cap, product(slave_ref[...], parts))
+    put_slots(neg_gap_ref, 0, cap, start_ref[...] + product(slave_ref[...], parts))
     copies += send_slots(neg_gap_ref, out_ref, cap, sem_ref.at[1])
     for copy in copies:
         copy.wait()
@@ -377,10 +398,10 @@
         (owner, pair_master.reshape(1, -1), pair_normal),
     )
     info = lax.all_to_all(info, "dom", 0, 0, tiled=True)
-    slave, slave_t, mortar_left, mortar_t, u, v, mass, mapped, neg_gap = call(
+    slave, slave_t, mortar_left, mortar_t, u, v, mass, mapped, neg_gap, start = call(
         functools.partial(prepare_kernel, n_dom=n_dom, cap=cap),
         [
-            bf16(SLOTS, 12 * slaves),
+            bf16(SLOTS, 9 * slaves),
             bf16(3 * slaves, 3 * SLOTS),
             bf16(3 * LANES, LANES),
             bf16(3 * LANES, LANES),
@@ -389,6 +410,7 @@
             field,
             f32(3 * masters, LANES),
             slots,
+            f32(SLOTS, LANES),
         ],
         (
             owner,
@@ -442,8 +464,8 @@
             u, v, out, m, neg_gap = call(
                 next_kernel,
                 [field, field, blocks, slots, slots],
-                (*state, slave_nodes, master_nodes, slave_gap, mortar_t, slave, master),
-                sems,
+                (*state, slave_nodes, master_nodes, start, mortar_t, slave, master),
+                [*sems, pltpu.VMEM((3 * masters, LANES), F32)],
                 us=2.0,
                 far=far,
             )

time: 82.8 us -> 82.2 us (level)
  transfers between devices with their start and end apart: 10 -> 10, of which waited for: 7 -> 7; matrix products, arithmetic and copies ran while one was open for 0% -> 0% of each run, Pallas kernels for 19% -> 20%
where the time goes in v5:
time: 82.2 us; the launch traced here: 81.5 us
  starting transfers between devices  27 us (33%)
  Pallas kernels  25.8 us (31%)
  waiting for transfers between devices  25.8 us (31%)
  local copies, waits for them, and re-layouts  1.98 us (2%)
  between operations  0.98 us (1%)
    pallas_call x16, Pallas kernels, call(): pl.pallas_call(kernel, out_shape=outs, in_specs=[vmem] * len(args), out_s...  25.8 us
    all_to_all x3, waiting for transfers between devices, shards(): recv = lax.all_to_all(out, 'dom', 0, 0)  15.8 us
    all_to_all x3, starting transfers between devices, shards(): recv = lax.all_to_all(out, 'dom', 0, 0)  11.2 us
    all_to_all x1, starting transfers between devices, shards(): info = lax.all_to_all(info, 'dom', 0, 0, tiled=True)  7.48 us
    ppermute x3, waiting for transfers between devices, shards(): rb = lax.ppermute(fb, 'dom', across)  6.19 us
    ppermute x3, starting transfers between devices, shards(): rb = lax.ppermute(fb, 'dom', across)  6.09 us
    all_to_all x1, waiting for transfers between devices, shards(): info = lax.all_to_all(info, 'dom', 0, 0, tiled=True)  3.79 us
    ppermute x3, starting transfers between devices, shards(): ra = lax.ppermute(fa, 'dom', inside)  2.18 us
  transfers between devices with their start and end apart: 10, of which 7 were waited for; matrix products, arithmetic and copies ran while one was open for 0% of the time, Pallas kernels for 20%

profile of v5, /device:TPU:1, one launch (start us, length us, event | category | flops | bytes accessed | tf_op | source)
XLA Modules:
  0.0 81.5 jit_solution(14512992008113414304)
XLA Ops:
  0.6 0.0 copy-start.9
  0.6 0.0 copy-start.10
  0.7 0.0 copy-start.11
  0.7 0.7 copy-done.9
  1.3 0.0 copy-done.10
  1.3 0.0 copy-done.11
  1.4 0.9 %shard_map.167 = f32[16,64]{1,0:T(8,128)} custom-call(s32[1,128]{1,0:T(1,128)S(1)} %bitcast.17, s32[1,128]{1,0:T(1,128)S(1)} %bitcast.16, f32[3,128]{1,0:T(4,128)S(1)} %copy-done.9), custom_call_target="tpu_custom_call" | custom-call | flops 1000000000 | bytes 3000000 | tf_op jit(solution)/shard_map/pallas_call | solution.py:350
  2.2 7.5 %all-to-all-start = ((f32[16,1,64]{2,1,0:T(1,128)}), f32[16,1,64]{2,1,0:T(1,128)S(1)}, u32[]{:S(2)}, u32[]{:S(2)}) async-start(f32[16,1,64]{2,1,0:T(1,128)} %bitcast.3), calls=%async_computation | async-start | bytes 16384 | tf_op jit(solution)/shard_map/all_to_all | solution.py:400
  9.7 0.0 copy-done.13
  9.8 0.0 copy-start.12
  9.8 0.6 copy-done.12
  10.4 1.2 %shard_map.168 = (bf16[256,576]{1,0:T(8,128)(2,1)S(1)}, bf16[192,768]{1,0:T(8,128)(2,1)S(1)}, bf16[384,128]{1,0:T(8,128)(2,1)S(1)}, bf16[384,128]{1,0:T(8,128)(2...) custom-call(s32[1,128]{1,0:T(1,128)S(1)} %bitcast.18, ...), custom_call_target="tpu_custom_call" | custom-call | flops 3000000000 | bytes 9000000 | tf_op jit(solution)/shard_map/pallas_call | solution.py:350
  11.7 3.8 %all-to-all-done = f32[16,1,64]{2,1,0:T(1,128)S(1)} async-done(((f32[16,1,64]{2,1,0:T(1,128)}), f32[16,1,64]{2,1,0:T(1,128)S(1)}, u32[]{:S(2)}, u32[]{:S(2)}) %all-to-all-start) | async-done | bytes 4128 | tf_op jit(solution)/shard_map/all_to_all | solution.py:400
  15.4 1.1 %shard_map.169 = (f32[16,32,128]{2,1,0:T(8,128)}, f32[16,16,128]{2,1,0:T(8,128)S(1)}, f32[256,96]{1,0:T(8,128)S(1)}) custom-call(f32[16,64]{1,0:T(8,128)S(1)} %bitcast.12, f32[96,128]{1,0:T(8,128)S(1)} %get-tuple-element.36.mapped_ref, f32[16,16,128]{2,1,0:T(8,128)S(1)} %get-tuple-element.37.neg_gap_ref), custom_call_target="tpu_custom_call" | custom-call | flops 1000000000 | bytes 3000000 | tf_op jit(solution)/shard_map/pallas_call | solution.py:350
  16.6 0.0 copy-start.1
  16.6 0.0 copy-start.8
  16.6 4.2 %all-to-all-start.1 = ((f32[16,32,128]{2,1,0:T(8,128)}), f32[16,32,128]{2,1,0:T(8,128)S(1)}, u32[]{:S(2)}, u32[]{:S(2)}) async-start(f32[16,32,128]{2,1,0:T(8,128)} %get-tuple-element.38), calls=%async_computation.1 | async-start | bytes 524288 | tf_op jit(solution)/shard_map/all_to_all | solution.py:437
  20.8 0.7 copy-done.7
  21.5 4.0 %shard_map.171.elastic_ref = f32[56,128]{1,0:T(8,128)S(1)} custom-call(f32[56,128]{1,0:T(8,128)S(1)} %get-tuple-element.44.u_ref, s32[8,2048]{1,0:T(8,128)S(1)} %copy-done.1, f32[1,2048]{1,0:T(1,128)S(1)} %bitcast.13, f32[24,24]{1,0:T(8,128)S(1)} %copy-done.7), custom_call_target="tpu_custom_call" | custom-call | flops 5000000000 | bytes 15000000 | tf_op jit(solution)/shard_map/pallas_call | solution.py:350
  25.5 4.8 %all-to-all-done.1.recv_ref = f32[16,32,128]{2,1,0:T(8,128)S(1)} async-done(((f32[16,32,128]{2,1,0:T(8,128)}), f32[16,32,128]{2,1,0:T(8,128)S(1)}, u32[]{:S(2)}, u32[]{:S(2)}) %all-to-all-start.1) | async-done | bytes 262176 | tf_op jit(solution)/shard_map/all_to_all | solution.py:437
  30.3 1.2 %shard_map.172 = (f32[56,128]{1,0:T(8,128)S(1)}, f32[3,4,128]{2,1,0:T(4,128)S(1)}, f32[3,4,128]{2,1,0:T(4,128)S(1)}) custom-call(f32[16,32,128]{2,1,0:T(8,128)S(1)} %all-to-all-done.1.recv_ref, f32[16,16,128]{2,1,0:T(8,128)S(1)} %get-tuple-element.37.neg_gap_ref, bf16[192,768]{1,0:T(8,128)(2,1)S(1)} %get-tuple-element.43.slave_t_ref, ...), custom_call_target="tpu_custom_call" | custom-call | flops 2000000000 | bytes 6000000 | tf_op jit(solution)/shard_map/pallas_call | solution.py:350
  31.5 0.7 collective-permute-start
  32.2 0.3 shard_map.170
  32.5 2.0 %collective-permute-start.1 = (f32[3,4,128]{2,1,0:T(4,128)S(1)}, f32[3,4,128]{2,1,0:T(4,128)S(1)}, u32[]{:S(2)}, u32[]{:S(2)}) collective-permute-start(f32[3,4,128]{2,1,0:T(4,128)S(1)} %get-tuple-element.47), channel_id=1, source_target_pairs={{1,2},{3,4},{5,6},{7,8},{9,10},{11,12},{13,14},{2,1},{4,3},{6,5},{... | collective-permute-start | bytes 18440 | tf_op jit(solution)/shard_map/ppermute | solution.py:455
  34.5 0.0 collective-permute-done.ra_ref
  34.6 0.8 %shard_map.173.negforce_ref = f32[56,128]{1,0:T(8,128)S(1)} custom-call(f32[16,32,128]{2,1,0:T(8,128)S(1)} %all-to-all-done.1.recv_ref, f32[16,16,128]{2,1,0:T(8,128)S(1)} %get-tuple-element.39.m_ref, bf16[96,768]{1,0:T(8,128)(2,1)S(1)} %get-tuple-element.41.master_t_ref, bf16[384,128]{1,0:T(8,128)(2,1)S(1)} %get-tuple-element.42.mortar_ref, ...), custom_call_target="tpu_custom_call" | custom-call | flops 1000000000 | bytes 3000000 | tf_op jit(solution)/shard_map/pallas_call | solution.py:350
  35.4 2.1 %collective-permute-done.1.rb_ref = f32[3,4,128]{2,1,0:T(4,128)S(1)} collective-permute-done((f32[3,4,128]{2,1,0:T(4,128)S(1)}, f32[3,4,128]{2,1,0:T(4,128)S(1)}, u32[]{:S(2)}, u32[]{:S(2)}) %collective-permute-start.1) | collective-permute-done | bytes 6176 | tf_op jit(solution)/shard_map/ppermute | solution.py:455
  37.5 1.8 %shard_map.174 = (f32[56,128]{1,0:T(8,128)S(1)}, f32[56,128]{1,0:T(8,128)S(1)}, f32[16,32,128]{2,1,0:T(8,128)}, f32[16,16,128]{2,1,0:T(8,128)S(1)}, f32[16,16,128]{2,1,0:T(8,128)S(1)}) custom-call(f32[56,128]{1,0:T(8,128)S(1)} %shard_map.173.negforce_ref, f32[3,4,128]{2,1,0:T(4,128)S(1)} %collective-permute-done.1.rb_ref, ...), custom_call_target="tpu_custom_call" | custom-call | flops 2000000000 | bytes 6000000 | tf_op jit(solution)/shard_map/pallas_call | solution.py:350
  39.2 3.5 %all-to-all-start.2 = ((f32[16,32,128]{2,1,0:T(8,128)}), f32[16,32,128]{2,1,0:T(8,128)S(1)}, u32[]{:S(2)}, u32[]{:S(2)}) async-start(f32[16,32,128]{2,1,0:T(8,128)} %get-tuple-element.54), calls=%async_computation.2 | async-start | bytes 524288 | tf_op jit(solution)/shard_map/all_to_all | solution.py:437
  42.7 4.0 %shard_map.175.elastic_ref = f32[56,128]{1,0:T(8,128)S(1)} custom-call(f32[56,128]{1,0:T(8,128)S(1)} %get-tuple-element.57.u_ref, s32[8,2048]{1,0:T(8,128)S(1)} %copy-done.1, f32[1,2048]{1,0:T(1,128)S(1)} %bitcast.14, f32[24,24]{1,0:T(8,128)S(1)} %copy-done.7), custom_call_target="tpu_custom_call" | custom-call | flops 5000000000 | bytes 15000000 | tf_op jit(solution)/shard_map/pallas_call | solution.py:350
  46.7 5.5 %all-to-all-done.2.recv_ref = f32[16,32,128]{2,1,0:T(8,128)S(1)} async-done(((f32[16,32,128]{2,1,0:T(8,128)}), f32[16,32,128]{2,1,0:T(8,128)S(1)}, u32[]{:S(2)}, u32[]{:S(2)}) %all-to-all-start.2) | async-done | bytes 262176 | tf_op jit(solution)/shard_map/all_to_all | solution.py:437
  52.2 1.2 %shard_map.176 = (f32[56,128]{1,0:T(8,128)S(1)}, f32[3,4,128]{2,1,0:T(4,128)S(1)}, f32[3,4,128]{2,1,0:T(4,128)S(1)}) custom-call(f32[16,32,128]{2,1,0:T(8,128)S(1)} %all-to-all-done.2.recv_ref, f32[16,16,128]{2,1,0:T(8,128)S(1)} %get-tuple-element.56.neg_gap_ref, bf16[192,768]{1,0:T(8,128)(2,1)S(1)} %get-tuple-element.43.slave_t_ref, ...), custom_call_target="tpu_custom_call" | custom-call | flops 2000000000 | bytes 6000000 | tf_op jit(solution)/shard_map/pallas_call | solution.py:350
  53.4 0.7 collective-permute-start.2
  54.1 2.0 %collective-permute-start.3 = (f32[3,4,128]{2,1,0:T(4,128)S(1)}, f32[3,4,128]{2,1,0:T(4,128)S(1)}, u32[]{:S(2)}, u32[]{:S(2)}) collective-permute-start(f32[3,4,128]{2,1,0:T(4,128)S(1)} %get-tuple-element.60), channel_id=1, source_target_pairs={{1,2},{3,4},{5,6},{7,8},{9,10},{11,12},{13,14},{2,1},{4,3},{6,5},{... | collective-permute-start | bytes 18440 | tf_op jit(solution)/shard_map/ppermute | solution.py:455
  56.1 0.0 collective-permute-done.2.ra_ref
  56.1 0.8 %shard_map.177.negforce_ref = f32[56,128]{1,0:T(8,128)S(1)} custom-call(f32[16,32,128]{2,1,0:T(8,128)S(1)} %all-to-all-done.2.recv_ref, f32[16,16,128]{2,1,0:T(8,128)S(1)} %get-tuple-element.55.m_ref, bf16[96,768]{1,0:T(8,128)(2,1)S(1)} %get-tuple-element.41.master_t_ref, bf16[384,128]{1,0:T(8,128)(2,1)S(1)} %get-tuple-element.42.mortar_ref, ...), custom_call_target="tpu_custom_call" | custom-call | flops 1000000000 | bytes 3000000 | tf_op jit(solution)/shard_map/pallas_call | solution.py:350
  57.0 2.1 %collective-permute-done.3.rb_ref = f32[3,4,128]{2,1,0:T(4,128)S(1)} collective-permute-done((f32[3,4,128]{2,1,0:T(4,128)S(1)}, f32[3,4,128]{2,1,0:T(4,128)S(1)}, u32[]{:S(2)}, u32[]{:S(2)}) %collective-permute-start.3) | collective-permute-done | bytes 6176 | tf_op jit(solution)/shard_map/ppermute | solution.py:455
  59.0 1.8 %shard_map.178 = (f32[56,128]{1,0:T(8,128)S(1)}, f32[56,128]{1,0:T(8,128)S(1)}, f32[16,32,128]{2,1,0:T(8,128)}, f32[16,16,128]{2,1,0:T(8,128)S(1)}, f32[16,16,128]{2,1,0:T(8,128)S(1)}) custom-call(f32[56,128]{1,0:T(8,128)S(1)} %shard_map.177.negforce_ref, f32[3,4,128]{2,1,0:T(4,128)S(1)} %collective-permute-done.3.rb_ref, ...), custom_call_target="tpu_custom_call" | custom-call | flops 2000000000 | bytes 6000000 | tf_op jit(solution)/shard_map/pallas_call | solution.py:350
  60.8 3.5 %all-to-all-start.3 = ((f32[16,32,128]{2,1,0:T(8,128)}), f32[16,32,128]{2,1,0:T(8,128)S(1)}, u32[]{:S(2)}, u32[]{:S(2)}) async-start(f32[16,32,128]{2,1,0:T(8,128)} %get-tuple-element.62), calls=%async_computation.3 | async-start | bytes 524288 | tf_op jit(solution)/shard_map/all_to_all | solution.py:437
  64.3 4.0 %shard_map.179.elastic_ref = f32[56,128]{1,0:T(8,128)S(1)} custom-call(f32[56,128]{1,0:T(8,128)S(1)} %get-tuple-element.65.u_ref, s32[8,2048]{1,0:T(8,128)S(1)} %copy-done.1, f32[1,2048]{1,0:T(1,128)S(1)} %bitcast.15, f32[24,24]{1,0:T(8,128)S(1)} %copy-done.7), custom_call_target="tpu_custom_call" | custom-call | flops 5000000000 | bytes 15000000 | tf_op jit(solution)/shard_map/pallas_call | solution.py:350
  68.3 5.5 %all-to-all-done.3.recv_ref = f32[16,32,128]{2,1,0:T(8,128)S(1)} async-done(((f32[16,32,128]{2,1,0:T(8,128)}), f32[16,32,128]{2,1,0:T(8,128)S(1)}, u32[]{:S(2)}, u32[]{:S(2)}) %all-to-all-start.3) | async-done | bytes 262176 | tf_op jit(solution)/shard_map/all_to_all | solution.py:437
  73.8 1.2 %shard_map.180 = (f32[56,128]{1,0:T(8,128)S(1)}, f32[3,4,128]{2,1,0:T(4,128)S(1)}, f32[3,4,128]{2,1,0:T(4,128)S(1)}) custom-call(f32[16,32,128]{2,1,0:T(8,128)S(1)} %all-to-all-done.3.recv_ref, f32[16,16,128]{2,1,0:T(8,128)S(1)} %get-tuple-element.64.neg_gap_ref, bf16[192,768]{1,0:T(8,128)(2,1)S(1)} %get-tuple-element.43.slave_t_ref, ...), custom_call_target="tpu_custom_call" | custom-call | flops 2000000000 | bytes 6000000 | tf_op jit(solution)/shard_map/pallas_call | solution.py:350
  75.0 0.7 collective-permute-start.4
  75.7 2.0 %collective-permute-start.5 = (f32[3,4,128]{2,1,0:T(4,128)S(1)}, f32[3,4,128]{2,1,0:T(4,128)S(1)}, u32[]{:S(2)}, u32[]{:S(2)}) collective-permute-start(f32[3,4,128]{2,1,0:T(4,128)S(1)} %get-tuple-element.68), channel_id=1, source_target_pairs={{1,2},{3,4},{5,6},{7,8},{9,10},{11,12},{13,14},{2,1},{4,3},{6,5},{... | collective-permute-start | bytes 18440 | tf_op jit(solution)/shard_map/ppermute | solution.py:455
  77.7 0.0 collective-permute-done.4.ra_ref
  77.8 0.8 %shard_map.181.negforce_ref = f32[56,128]{1,0:T(8,128)S(1)} custom-call(f32[16,32,128]{2,1,0:T(8,128)S(1)} %all-to-all-done.3.recv_ref, f32[16,16,128]{2,1,0:T(8,128)S(1)} %get-tuple-element.63.m_ref, bf16[96,768]{1,0:T(8,128)(2,1)S(1)} %get-tuple-element.41.master_t_ref, bf16[384,128]{1,0:T(8,128)(2,1)S(1)} %get-tuple-element.42.mortar_ref, ...), custom_call_target="tpu_custom_call" | custom-call | flops 1000000000 | bytes 3000000 | tf_op jit(solution)/shard_map/pallas_call | solution.py:350
  78.6 2.1 %collective-permute-done.5.rb_ref = f32[3,4,128]{2,1,0:T(4,128)S(1)} collective-permute-done((f32[3,4,128]{2,1,0:T(4,128)S(1)}, f32[3,4,128]{2,1,0:T(4,128)S(1)}, u32[]{:S(2)}, u32[]{:S(2)}) %collective-permute-start.5) | collective-permute-done | bytes 6176 | tf_op jit(solution)/shard_map/ppermute | solution.py:455
  80.6 0.8 %shard_map.182 = (f32[3,2176]{1,0:T(4,128)}, f32[3,2176]{1,0:T(4,128)}) custom-call(f32[56,128]{1,0:T(8,128)S(1)} %shard_map.181.negforce_ref, f32[3,4,128]{2,1,0:T(4,128)S(1)} %collective-permute-done.5.rb_ref, s32[8,128]{1,0:T(8,128)S(1)} %pad_add_fusion.faces_ref, f32[56,128]{1,0:T(8,128)S(1)} %get-tuple-element.65.u_ref, ...), custom_call_target="tpu_custom_call" | custom-call | flops 1000000000 | bytes 3000000 | tf_op jit(solution)/shard_map/pallas_call | solution.py:350
  (23 shorter events, 0.1 us)
Async XLA Ops:
  0.6 0.7 copy-start.9
  0.6 0.7 copy-start.10
  0.7 0.7 copy-start.11
  1.3 8.4 %copy-start.13 = (f32[2176]{0:T(1024)S(1)}, f32[2176]{0:T(1024)}, u32[]{:S(2)}) copy-start(f32[2176]{0:T(1024)} %param.18) | copy-start | bytes 26116
  1.3 8.4 %copy-start.2 = (f32[3,2176]{1,0:T(4,128)S(1)}, f32[3,2176]{1,0:T(4,128)}, u32[]{:S(2)}) copy-start(f32[3,2176]{1,0:T(4,128)} %u_ref.1) | copy-start | bytes 78340
  1.3 8.4 %copy-start.3 = (f32[3,2176]{1,0:T(4,128)S(1)}, f32[3,2176]{1,0:T(4,128)}, u32[]{:S(2)}) copy-start(f32[3,2176]{1,0:T(4,128)} %v_ref.1) | copy-start | bytes 78340
  1.3 8.4 %copy-start.4 = (f32[64,128]{1,0:T(8,128)S(1)}, f32[64,128]{1,0:T(8,128)}, u32[]{:S(2)}) copy-start(f32[64,128]{1,0:T(8,128)} %gap_ref.1) | copy-start | bytes 98308
  1.3 8.4 %copy-start.5 = (s32[64,128]{1,0:T(8,128)S(1)}, s32[64,128]{1,0:T(8,128)}, u32[]{:S(2)}) copy-start(s32[64,128]{1,0:T(8,128)} %snodes_ref.11) | copy-start | bytes 98308
  1.4 8.4 %copy-start.6 = (s32[32,128]{1,0:T(8,128)S(1)}, s32[32,128]{1,0:T(8,128)}, u32[]{:S(2)}) copy-start(s32[32,128]{1,0:T(8,128)} %mnodes_ref.11) | copy-start | bytes 49156
  2.2 7.6 %copy-start = (f32[128,128]{1,0:T(8,128)S(1)}, f32[128,128]{1,0:T(8,128)}, u32[]{:S(2)}) copy-start(f32[128,128]{1,0:T(8,128)} %mortar_ref.1) | copy-start | bytes 196612
  2.2 13.2 %all-to-all-start = ((f32[16,1,64]{2,1,0:T(1,128)}), f32[16,1,64]{2,1,0:T(1,128)S(1)}, u32[]{:S(2)}, u32[]{:S(2)}) async-start(f32[16,1,64]{2,1,0:T(1,128)} %bitcast.3), calls=%async_computation | async-start | bytes 16384 | tf_op jit(solution)/shard_map/all_to_all | solution.py:400
  9.8 0.7 copy-start.12
  10.4 1.2 %copy-start.14 = (s32[512]{0:T(512)S(1)}, s32[512]{0:T(512)}, u32[]{:S(2)}) copy-start(s32[512]{0:T(512)} %param.30) | copy-start | bytes 6148
  10.4 1.2 %copy-start.15 = (s32[512]{0:T(512)S(1)}, s32[512]{0:T(512)}, u32[]{:S(2)}) copy-start(s32[512]{0:T(512)} %param.29) | copy-start | bytes 6148
  16.6 4.2 %copy-start.1 = (s32[8,2048]{1,0:T(8,128)S(1)}, s32[8,2048]{1,0:T(8,128)}, u32[]{:S(2)}) copy-start(s32[8,2048]{1,0:T(8,128)} %conn_ref.5) | copy-start | bytes 196612
  16.6 4.2 %copy-start.8 = (f32[2048]{0:T(1024)S(1)}, f32[2048]{0:T(1024)}, u32[]{:S(2)}) copy-start(f32[2048]{0:T(1024)} %param.20) | copy-start | bytes 24580
  16.6 13.7 %all-to-all-start.1 = ((f32[16,32,128]{2,1,0:T(8,128)}), f32[16,32,128]{2,1,0:T(8,128)S(1)}, u32[]{:S(2)}, u32[]{:S(2)}) async-start(f32[16,32,128]{2,1,0:T(8,128)} %get-tuple-element.38), calls=%async_computation.1 | async-start | bytes 524288 | tf_op jit(solution)/shard_map/all_to_all | solution.py:437
  20.8 0.7 copy-start.7
  31.5 3.0 %collective-permute-start = (f32[3,4,128]{2,1,0:T(4,128)S(1)}, f32[3,4,128]{2,1,0:T(4,128)S(1)}, u32[]{:S(2)}, u32[]{:S(2)}) collective-permute-start(f32[3,4,128]{2,1,0:T(4,128)S(1)} %get-tuple-element.46), channel_id=1, source_target_pairs={{0,1},{1,0},{2,3},{3,2},{4,5},{5,4},{6,7},{7,6},{8,9},{9,8},{10,11... | collective-permute-start | bytes 18440 | tf_op jit(solution)/shard_map/ppermute | solution.py:454
  32.5 4.9 %collective-permute-start.1 = (f32[3,4,128]{2,1,0:T(4,128)S(1)}, f32[3,4,128]{2,1,0:T(4,128)S(1)}, u32[]{:S(2)}, u32[]{:S(2)}) collective-permute-start(f32[3,4,128]{2,1,0:T(4,128)S(1)} %get-tuple-element.47), channel_id=1, source_target_pairs={{1,2},{3,4},{5,6},{7,8},{9,10},{11,12},{13,14},{2,1},{4,3},{6,5},{... | collective-permute-start | bytes 18440 | tf_op jit(solution)/shard_map/ppermute | solution.py:455
  39.2 13.0 %all-to-all-start.2 = ((f32[16,32,128]{2,1,0:T(8,128)}), f32[16,32,128]{2,1,0:T(8,128)S(1)}, u32[]{:S(2)}, u32[]{:S(2)}) async-start(f32[16,32,128]{2,1,0:T(8,128)} %get-tuple-element.54), calls=%async_computation.2 | async-start | bytes 524288 | tf_op jit(solution)/shard_map/all_to_all | solution.py:437
  53.4 2.8 %collective-permute-start.2 = (f32[3,4,128]{2,1,0:T(4,128)S(1)}, f32[3,4,128]{2,1,0:T(4,128)S(1)}, u32[]{:S(2)}, u32[]{:S(2)}) collective-permute-start(f32[3,4,128]{2,1,0:T(4,128)S(1)} %get-tuple-element.59), channel_id=1, source_target_pairs={{0,1},{1,0},{2,3},{3,2},{4,5},{5,4},{6,7},{7,6},{8,9},{9,8},{10,11... | collective-permute-start | bytes 18440 | tf_op jit(solution)/shard_map/ppermute | solution.py:454
  54.1 4.9 %collective-permute-start.3 = (f32[3,4,128]{2,1,0:T(4,128)S(1)}, f32[3,4,128]{2,1,0:T(4,128)S(1)}, u32[]{:S(2)}, u32[]{:S(2)}) collective-permute-start(f32[3,4,128]{2,1,0:T(4,128)S(1)} %get-tuple-element.60), channel_id=1, source_target_pairs={{1,2},{3,4},{5,6},{7,8},{9,10},{11,12},{13,14},{2,1},{4,3},{6,5},{... | collective-permute-start | bytes 18440 | tf_op jit(solution)/shard_map/ppermute | solution.py:455
  60.8 13.0 %all-to-all-start.3 = ((f32[16,32,128]{2,1,0:T(8,128)}), f32[16,32,128]{2,1,0:T(8,128)S(1)}, u32[]{:S(2)}, u32[]{:S(2)}) async-start(f32[16,32,128]{2,1,0:T(8,128)} %get-tuple-element.62), calls=%async_computation.3 | async-start | bytes 524288 | tf_op jit(solution)/shard_map/all_to_all | solution.py:437
  75.0 2.8 %collective-permute-start.4 = (f32[3,4,128]{2,1,0:T(4,128)S(1)}, f32[3,4,128]{2,1,0:T(4,128)S(1)}, u32[]{:S(2)}, u32[]{:S(2)}) collective-permute-start(f32[3,4,128]{2,1,0:T(4,128)S(1)} %get-tuple-element.67), channel_id=1, source_target_pairs={{0,1},{1,0},{2,3},{3,2},{4,5},{5,4},{6,7},{7,6},{8,9},{9,8},{10,11... | collective-permute-start | bytes 18440 | tf_op jit(solution)/shard_map/ppermute | solution.py:454
  75.7 4.9 %collective-permute-start.5 = (f32[3,4,128]{2,1,0:T(4,128)S(1)}, f32[3,4,128]{2,1,0:T(4,128)S(1)}, u32[]{:S(2)}, u32[]{:S(2)}) collective-permute-start(f32[3,4,128]{2,1,0:T(4,128)S(1)} %get-tuple-element.68), channel_id=1, source_target_pairs={{1,2},{3,4},{5,6},{7,8},{9,10},{11,12},{13,14},{2,1},{4,3},{6,5},{... | collective-permute-start | bytes 18440 | tf_op jit(solution)/shard_map/ppermute | solution.py:455

commit v6 on v5

--- a/solution.py
+++ b/solution.py
@@ -12,6 +12,7 @@
 TIME_STEP = 0.1
 SLOTS = 256
 GROUP = 4
+WIDE = 8
 
 F32 = jnp.float32
 BF16 = jnp.bfloat16
@@ -182,11 +183,11 @@
     m, patches = 3 * MAIN, nodes_ref.shape[0]
     tails = jnp.concatenate([high[m:].astype(F32), low[m:].astype(F32)], axis=0).astype(BF16)
     table = jnp.concatenate([high[:m], low[:m], tails], axis=0)
-    for j in range(0, patches, GROUP):
-        hot = jnp.concatenate([lane_factor(nodes_ref[j + k : j + k + 1, :]) for k in range(GROUP)], axis=1)
+    for j in range(0, patches, WIDE):
+        hot = jnp.concatenate([lane_factor(nodes_ref[j + k : j + k + 1, :]) for k in range(WIDE)], axis=1)
         found = lax.dot_general(table, hot, NN, preferred_element_type=F32)
         body, tail = found[:m] + found[m : 2 * m], found[2 * m : 2 * m + 8] + found[2 * m + 8 :]
-        for k in range(GROUP):
+        for k in range(WIDE):
             columns = slice(k * LANES, (k + 1) * LANES)
             upper = nodes_ref[j + k : j + k + 1, :] >> 7
             here = iota((MAIN, LANES), 0) == upper
@@ -225,7 +226,7 @@
     for c in range(3):
         for h in range(MAIN + 1):
             r = field_row(c, h)
-            fm_ref[r : r + 1, :] = mass_ref[0:1, h * LANES : (h + 1) * LANES]
+            fm_ref[r : r + 1, :] = TIME_STEP / mass_ref[0:1, h * LANES : (h + 1) * LANES]
     mapped, parts = pair_values(fu_ref, snodes_ref, mnodes_ref, mortar_t_ref)
     mapped_ref[...] = mapped
     put_slots(neg_gap_ref, 0, cap, start + product(slave_ref[...], parts))
@@ -314,9 +315,9 @@
     out_ref[...] = local_ref[...] + factor_sum(scatter(rows))
 
 
-def advance(negforce_ref, rb_ref, faces_ref, u_ref, v_ref, mass_ref):
+def advance(negforce_ref, rb_ref, faces_ref, u_ref, v_ref, rate_ref):
     force = negforce_ref[...] + factor_sum(scatter(face_rows(faces_ref, rb_ref, 4)))
-    v = v_ref[...] - TIME_STEP * force / mass_ref[...]
+    v = v_ref[...] - force * rate_ref[...]
     return u_ref[...] + TIME_STEP * v, v
 
 

time: 82.2 us -> 82.2 us (level)
  no operation moved by 1% of the time
where the time goes in v6:
time: 82.2 us; the launch traced here: 81.5 us
  starting transfers between devices  27 us (33%)
  Pallas kernels  25.8 us (31%)
  waiting for transfers between devices  25.8 us (31%)
  local copies, waits for them, and re-layouts  1.98 us (2%)
  between operations  0.98 us (1%)
    pallas_call x16, Pallas kernels, call(): pl.pallas_call(kernel, out_shape=outs, in_specs=[vmem] * len(args), out_s...  25.8 us
    all_to_all x3, waiting for transfers between devices, shards(): recv = lax.all_to_all(out, 'dom', 0, 0)  15.8 us
    all_to_all x3, starting transfers between devices, shards(): recv = lax.all_to_all(out, 'dom', 0, 0)  11.2 us
    all_to_all x1, starting transfers between devices, shards(): info = lax.all_to_all(info, 'dom', 0, 0, tiled=True)  7.48 us
    ppermute x3, waiting for transfers between devices, shards(): rb = lax.ppermute(fb, 'dom', across)  6.19 us
    ppermute x3, starting transfers between devices, shards(): rb = lax.ppermute(fb, 'dom', across)  6.09 us
    all_to_all x1, waiting for transfers between devices, shards(): info = lax.all_to_all(info, 'dom', 0, 0, tiled=True)  3.79 us
    ppermute x3, starting transfers between devices, shards(): ra = lax.ppermute(fa, 'dom', inside)  2.17 us
  transfers between devices with their start and end apart: 10, of which 7 were waited for; matrix products, arithmetic and copies ran while one was open for 0% of the time, Pallas kernels for 20%

profile of v6, /device:TPU:1, one launch (start us, length us, event | category | flops | bytes accessed | tf_op | source)
XLA Modules:
  0.0 81.5 jit_solution(11847613293421973)
XLA Ops:
  0.7 0.7 copy-done.9
  1.4 0.9 %shard_map.167 = f32[16,64]{1,0:T(8,128)} custom-call(s32[1,128]{1,0:T(1,128)S(1)} %bitcast.17, s32[1,128]{1,0:T(1,128)S(1)} %bitcast.16, f32[3,128]{1,0:T(4,128)S(1)} %copy-done.9), custom_call_target="tpu_custom_call" | custom-call | flops 1000000000 | bytes 3000000 | tf_op jit(solution)/shard_map/pallas_call | solution.py:351
  2.2 7.5 %all-to-all-start = ((f32[16,1,64]{2,1,0:T(1,128)}), f32[16,1,64]{2,1,0:T(1,128)S(1)}, u32[]{:S(2)}, u32[]{:S(2)}) async-start(f32[16,1,64]{2,1,0:T(1,128)} %bitcast.3), calls=%async_computation | async-start | bytes 16384 | tf_op jit(solution)/shard_map/all_to_all | solution.py:401
  9.7 0.0 copy-done.13
  9.8 0.0 copy-start.12
  9.8 0.0 copy-done.2
  9.8 0.0 copy-done.3
  9.8 0.0 copy-done.4
  9.8 0.0 copy-done.5
  9.8 0.0 copy-done.6
  9.8 0.6 copy-done.12
  10.4 1.2 %shard_map.168 = (bf16[256,576]{1,0:T(8,128)(2,1)S(1)}, bf16[192,768]{1,0:T(8,128)(2,1)S(1)}, bf16[384,128]{1,0:T(8,128)(2,1)S(1)}, bf16[384,128]{1,0:T(8,128)(2...) custom-call(s32[1,128]{1,0:T(1,128)S(1)} %bitcast.18, ...), custom_call_target="tpu_custom_call" | custom-call | flops 3000000000 | bytes 9000000 | tf_op jit(solution)/shard_map/pallas_call | solution.py:351
  11.7 3.8 %all-to-all-done = f32[16,1,64]{2,1,0:T(1,128)S(1)} async-done(((f32[16,1,64]{2,1,0:T(1,128)}), f32[16,1,64]{2,1,0:T(1,128)S(1)}, u32[]{:S(2)}, u32[]{:S(2)}) %all-to-all-start) | async-done | bytes 4128 | tf_op jit(solution)/shard_map/all_to_all | solution.py:401
  15.4 1.1 %shard_map.169 = (f32[16,32,128]{2,1,0:T(8,128)}, f32[16,16,128]{2,1,0:T(8,128)S(1)}, f32[256,96]{1,0:T(8,128)S(1)}) custom-call(f32[16,64]{1,0:T(8,128)S(1)} %bitcast.12, f32[96,128]{1,0:T(8,128)S(1)} %get-tuple-element.36.mapped_ref, f32[16,16,128]{2,1,0:T(8,128)S(1)} %get-tuple-element.37.neg_gap_ref), custom_call_target="tpu_custom_call" | custom-call | flops 1000000000 | bytes 3000000 | tf_op jit(solution)/shard_map/pallas_call | solution.py:351
  16.6 0.0 copy-start.1
  16.6 0.0 copy-start.8
  16.6 4.2 %all-to-all-start.1 = ((f32[16,32,128]{2,1,0:T(8,128)}), f32[16,32,128]{2,1,0:T(8,128)S(1)}, u32[]{:S(2)}, u32[]{:S(2)}) async-start(f32[16,32,128]{2,1,0:T(8,128)} %get-tuple-element.38), calls=%async_computation.1 | async-start | bytes 524288 | tf_op jit(solution)/shard_map/all_to_all | solution.py:438
  20.8 0.7 copy-done.7
  21.5 4.0 %shard_map.171.elastic_ref = f32[56,128]{1,0:T(8,128)S(1)} custom-call(f32[56,128]{1,0:T(8,128)S(1)} %get-tuple-element.44.u_ref, s32[8,2048]{1,0:T(8,128)S(1)} %copy-done.1, f32[1,2048]{1,0:T(1,128)S(1)} %bitcast.13, f32[24,24]{1,0:T(8,128)S(1)} %copy-done.7), custom_call_target="tpu_custom_call" | custom-call | flops 5000000000 | bytes 15000000 | tf_op jit(solution)/shard_map/pallas_call | solution.py:351
  25.5 4.8 %all-to-all-done.1.recv_ref = f32[16,32,128]{2,1,0:T(8,128)S(1)} async-done(((f32[16,32,128]{2,1,0:T(8,128)}), f32[16,32,128]{2,1,0:T(8,128)S(1)}, u32[]{:S(2)}, u32[]{:S(2)}) %all-to-all-start.1) | async-done | bytes 262176 | tf_op jit(solution)/shard_map/all_to_all | solution.py:438
  30.3 1.2 %shard_map.172 = (f32[56,128]{1,0:T(8,128)S(1)}, f32[3,4,128]{2,1,0:T(4,128)S(1)}, f32[3,4,128]{2,1,0:T(4,128)S(1)}) custom-call(f32[16,32,128]{2,1,0:T(8,128)S(1)} %all-to-all-done.1.recv_ref, f32[16,16,128]{2,1,0:T(8,128)S(1)} %get-tuple-element.37.neg_gap_ref, bf16[192,768]{1,0:T(8,128)(2,1)S(1)} %get-tuple-element.43.slave_t_ref, ...), custom_call_target="tpu_custom_call" | custom-call | flops 2000000000 | bytes 6000000 | tf_op jit(solution)/shard_map/pallas_call | solution.py:351
  31.5 0.7 collective-permute-start
  32.2 0.3 shard_map.170
  32.5 2.0 %collective-permute-start.1 = (f32[3,4,128]{2,1,0:T(4,128)S(1)}, f32[3,4,128]{2,1,0:T(4,128)S(1)}, u32[]{:S(2)}, u32[]{:S(2)}) collective-permute-start(f32[3,4,128]{2,1,0:T(4,128)S(1)} %get-tuple-element.47), channel_id=1, source_target_pairs={{1,2},{3,4},{5,6},{7,8},{9,10},{11,12},{13,14},{2,1},{4,3},{6,5},{... | collective-permute-start | bytes 18440 | tf_op jit(solution)/shard_map/ppermute | solution.py:456
  34.5 0.0 collective-permute-done.ra_ref
  34.6 0.8 %shard_map.173.negforce_ref = f32[56,128]{1,0:T(8,128)S(1)} custom-call(f32[16,32,128]{2,1,0:T(8,128)S(1)} %all-to-all-done.1.recv_ref, f32[16,16,128]{2,1,0:T(8,128)S(1)} %get-tuple-element.39.m_ref, bf16[96,768]{1,0:T(8,128)(2,1)S(1)} %get-tuple-element.41.master_t_ref, bf16[384,128]{1,0:T(8,128)(2,1)S(1)} %get-tuple-element.42.mortar_ref, ...), custom_call_target="tpu_custom_call" | custom-call | flops 1000000000 | bytes 3000000 | tf_op jit(solution)/shard_map/pallas_call | solution.py:351
  35.4 2.1 %collective-permute-done.1.rb_ref = f32[3,4,128]{2,1,0:T(4,128)S(1)} collective-permute-done((f32[3,4,128]{2,1,0:T(4,128)S(1)}, f32[3,4,128]{2,1,0:T(4,128)S(1)}, u32[]{:S(2)}, u32[]{:S(2)}) %collective-permute-start.1) | collective-permute-done | bytes 6176 | tf_op jit(solution)/shard_map/ppermute | solution.py:456
  37.5 1.8 %shard_map.174 = (f32[56,128]{1,0:T(8,128)S(1)}, f32[56,128]{1,0:T(8,128)S(1)}, f32[16,32,128]{2,1,0:T(8,128)}, f32[16,16,128]{2,1,0:T(8,128)S(1)}, f32[16,16,128]{2,1,0:T(8,128)S(1)}) custom-call(f32[56,128]{1,0:T(8,128)S(1)} %shard_map.173.negforce_ref, f32[3,4,128]{2,1,0:T(4,128)S(1)} %collective-permute-done.1.rb_ref, ...), custom_call_target="tpu_custom_call" | custom-call | flops 2000000000 | bytes 6000000 | tf_op jit(solution)/shard_map/pallas_call | solution.py:351
  39.2 3.5 %all-to-all-start.2 = ((f32[16,32,128]{2,1,0:T(8,128)}), f32[16,32,128]{2,1,0:T(8,128)S(1)}, u32[]{:S(2)}, u32[]{:S(2)}) async-start(f32[16,32,128]{2,1,0:T(8,128)} %get-tuple-element.54), calls=%async_computation.2 | async-start | bytes 524288 | tf_op jit(solution)/shard_map/all_to_all | solution.py:438
  42.7 4.0 %shard_map.175.elastic_ref = f32[56,128]{1,0:T(8,128)S(1)} custom-call(f32[56,128]{1,0:T(8,128)S(1)} %get-tuple-element.57.u_ref, s32[8,2048]{1,0:T(8,128)S(1)} %copy-done.1, f32[1,2048]{1,0:T(1,128)S(1)} %bitcast.14, f32[24,24]{1,0:T(8,128)S(1)} %copy-done.7), custom_call_target="tpu_custom_call" | custom-call | flops 5000000000 | bytes 15000000 | tf_op jit(solution)/shard_map/pallas_call | solution.py:351
  46.7 5.5 %all-to-all-done.2.recv_ref = f32[16,32,128]{2,1,0:T(8,128)S(1)} async-done(((f32[16,32,128]{2,1,0:T(8,128)}), f32[16,32,128]{2,1,0:T(8,128)S(1)}, u32[]{:S(2)}, u32[]{:S(2)}) %all-to-all-start.2) | async-done | bytes 262176 | tf_op jit(solution)/shard_map/all_to_all | solution.py:438
  52.2 1.2 %shard_map.176 = (f32[56,128]{1,0:T(8,128)S(1)}, f32[3,4,128]{2,1,0:T(4,128)S(1)}, f32[3,4,128]{2,1,0:T(4,128)S(1)}) custom-call(f32[16,32,128]{2,1,0:T(8,128)S(1)} %all-to-all-done.2.recv_ref, f32[16,16,128]{2,1,0:T(8,128)S(1)} %get-tuple-element.56.neg_gap_ref, bf16[192,768]{1,0:T(8,128)(2,1)S(1)} %get-tuple-element.43.slave_t_ref, ...), custom_call_target="tpu_custom_call" | custom-call | flops 2000000000 | bytes 6000000 | tf_op jit(solution)/shard_map/pallas_call | solution.py:351
  53.4 0.7 collective-permute-start.2
  54.1 2.0 %collective-permute-start.3 = (f32[3,4,128]{2,1,0:T(4,128)S(1)}, f32[3,4,128]{2,1,0:T(4,128)S(1)}, u32[]{:S(2)}, u32[]{:S(2)}) collective-permute-start(f32[3,4,128]{2,1,0:T(4,128)S(1)} %get-tuple-element.60), channel_id=1, source_target_pairs={{1,2},{3,4},{5,6},{7,8},{9,10},{11,12},{13,14},{2,1},{4,3},{6,5},{... | collective-permute-start | bytes 18440 | tf_op jit(solution)/shard_map/ppermute | solution.py:456
  56.1 0.0 collective-permute-done.2.ra_ref
  56.1 0.8 %shard_map.177.negforce_ref = f32[56,128]{1,0:T(8,128)S(1)} custom-call(f32[16,32,128]{2,1,0:T(8,128)S(1)} %all-to-all-done.2.recv_ref, f32[16,16,128]{2,1,0:T(8,128)S(1)} %get-tuple-element.55.m_ref, bf16[96,768]{1,0:T(8,128)(2,1)S(1)} %get-tuple-element.41.master_t_ref, bf16[384,128]{1,0:T(8,128)(2,1)S(1)} %get-tuple-element.42.mortar_ref, ...), custom_call_target="tpu_custom_call" | custom-call | flops 1000000000 | bytes 3000000 | tf_op jit(solution)/shard_map/pallas_call | solution.py:351
  57.0 2.1 %collective-permute-done.3.rb_ref = f32[3,4,128]{2,1,0:T(4,128)S(1)} collective-permute-done((f32[3,4,128]{2,1,0:T(4,128)S(1)}, f32[3,4,128]{2,1,0:T(4,128)S(1)}, u32[]{:S(2)}, u32[]{:S(2)}) %collective-permute-start.3) | collective-permute-done | bytes 6176 | tf_op jit(solution)/shard_map/ppermute | solution.py:456
  59.0 1.8 %shard_map.178 = (f32[56,128]{1,0:T(8,128)S(1)}, f32[56,128]{1,0:T(8,128)S(1)}, f32[16,32,128]{2,1,0:T(8,128)}, f32[16,16,128]{2,1,0:T(8,128)S(1)}, f32[16,16,128]{2,1,0:T(8,128)S(1)}) custom-call(f32[56,128]{1,0:T(8,128)S(1)} %shard_map.177.negforce_ref, f32[3,4,128]{2,1,0:T(4,128)S(1)} %collective-permute-done.3.rb_ref, ...), custom_call_target="tpu_custom_call" | custom-call | flops 2000000000 | bytes 6000000 | tf_op jit(solution)/shard_map/pallas_call | solution.py:351
  60.8 3.5 %all-to-all-start.3 = ((f32[16,32,128]{2,1,0:T(8,128)}), f32[16,32,128]{2,1,0:T(8,128)S(1)}, u32[]{:S(2)}, u32[]{:S(2)}) async-start(f32[16,32,128]{2,1,0:T(8,128)} %get-tuple-element.62), calls=%async_computation.3 | async-start | bytes 524288 | tf_op jit(solution)/shard_map/all_to_all | solution.py:438
  64.3 4.0 %shard_map.179.elastic_ref = f32[56,128]{1,0:T(8,128)S(1)} custom-call(f32[56,128]{1,0:T(8,128)S(1)} %get-tuple-element.65.u_ref, s32[8,2048]{1,0:T(8,128)S(1)} %copy-done.1, f32[1,2048]{1,0:T(1,128)S(1)} %bitcast.15, f32[24,24]{1,0:T(8,128)S(1)} %copy-done.7), custom_call_target="tpu_custom_call" | custom-call | flops 5000000000 | bytes 15000000 | tf_op jit(solution)/shard_map/pallas_call | solution.py:351
  68.4 5.5 %all-to-all-done.3.recv_ref = f32[16,32,128]{2,1,0:T(8,128)S(1)} async-done(((f32[16,32,128]{2,1,0:T(8,128)}), f32[16,32,128]{2,1,0:T(8,128)S(1)}, u32[]{:S(2)}, u32[]{:S(2)}) %all-to-all-start.3) | async-done | bytes 262176 | tf_op jit(solution)/shard_map/all_to_all | solution.py:438
  73.8 1.2 %shard_map.180 = (f32[56,128]{1,0:T(8,128)S(1)}, f32[3,4,128]{2,1,0:T(4,128)S(1)}, f32[3,4,128]{2,1,0:T(4,128)S(1)}) custom-call(f32[16,32,128]{2,1,0:T(8,128)S(1)} %all-to-all-done.3.recv_ref, f32[16,16,128]{2,1,0:T(8,128)S(1)} %get-tuple-element.64.neg_gap_ref, bf16[192,768]{1,0:T(8,128)(2,1)S(1)} %get-tuple-element.43.slave_t_ref, ...), custom_call_target="tpu_custom_call" | custom-call | flops 2000000000 | bytes 6000000 | tf_op jit(solution)/shard_map/pallas_call | solution.py:351
  75.0 0.7 collective-permute-start.4
  75.7 2.0 %collective-permute-start.5 = (f32[3,4,128]{2,1,0:T(4,128)S(1)}, f32[3,4,128]{2,1,0:T(4,128)S(1)}, u32[]{:S(2)}, u32[]{:S(2)}) collective-permute-start(f32[3,4,128]{2,1,0:T(4,128)S(1)} %get-tuple-element.68), channel_id=1, source_target_pairs={{1,2},{3,4},{5,6},{7,8},{9,10},{11,12},{13,14},{2,1},{4,3},{6,5},{... | collective-permute-start | bytes 18440 | tf_op jit(solution)/shard_map/ppermute | solution.py:456
  77.8 0.0 collective-permute-done.4.ra_ref
  77.8 0.8 %shard_map.181.negforce_ref = f32[56,128]{1,0:T(8,128)S(1)} custom-call(f32[16,32,128]{2,1,0:T(8,128)S(1)} %all-to-all-done.3.recv_ref, f32[16,16,128]{2,1,0:T(8,128)S(1)} %get-tuple-element.63.m_ref, bf16[96,768]{1,0:T(8,128)(2,1)S(1)} %get-tuple-element.41.master_t_ref, bf16[384,128]{1,0:T(8,128)(2,1)S(1)} %get-tuple-element.42.mortar_ref, ...), custom_call_target="tpu_custom_call" | custom-call | flops 1000000000 | bytes 3000000 | tf_op jit(solution)/shard_map/pallas_call | solution.py:351
  78.6 2.1 %collective-permute-done.5.rb_ref = f32[3,4,128]{2,1,0:T(4,128)S(1)} collective-permute-done((f32[3,4,128]{2,1,0:T(4,128)S(1)}, f32[3,4,128]{2,1,0:T(4,128)S(1)}, u32[]{:S(2)}, u32[]{:S(2)}) %collective-permute-start.5) | collective-permute-done | bytes 6176 | tf_op jit(solution)/shard_map/ppermute | solution.py:456
  80.6 0.8 %shard_map.182 = (f32[3,2176]{1,0:T(4,128)}, f32[3,2176]{1,0:T(4,128)}) custom-call(f32[56,128]{1,0:T(8,128)S(1)} %shard_map.181.negforce_ref, f32[3,4,128]{2,1,0:T(4,128)S(1)} %collective-permute-done.5.rb_ref, s32[8,128]{1,0:T(8,128)S(1)} %pad_add_fusion.faces_ref, f32[56,128]{1,0:T(8,128)S(1)} %get-tuple-element.65.u_ref, ...), custom_call_target="tpu_custom_call" | custom-call | flops 1000000000 | bytes 3000000 | tf_op jit(solution)/shard_map/pallas_call | solution.py:351
  (23 shorter events, 0.1 us)
Async XLA Ops:
  0.6 0.7 copy-start.9
  0.6 0.7 copy-start.10
  0.7 0.7 copy-start.11
  1.3 8.4 %copy-start.13 = (f32[2176]{0:T(1024)S(1)}, f32[2176]{0:T(1024)}, u32[]{:S(2)}) copy-start(f32[2176]{0:T(1024)} %param.18) | copy-start | bytes 26116
  1.3 8.4 %copy-start.2 = (f32[3,2176]{1,0:T(4,128)S(1)}, f32[3,2176]{1,0:T(4,128)}, u32[]{:S(2)}) copy-start(f32[3,2176]{1,0:T(4,128)} %u_ref.1) | copy-start | bytes 78340
  1.3 8.4 %copy-start.3 = (f32[3,2176]{1,0:T(4,128)S(1)}, f32[3,2176]{1,0:T(4,128)}, u32[]{:S(2)}) copy-start(f32[3,2176]{1,0:T(4,128)} %v_ref.1) | copy-start | bytes 78340
  1.3 8.4 %copy-start.4 = (f32[64,128]{1,0:T(8,128)S(1)}, f32[64,128]{1,0:T(8,128)}, u32[]{:S(2)}) copy-start(f32[64,128]{1,0:T(8,128)} %gap_ref.1) | copy-start | bytes 98308
  1.3 8.4 %copy-start.5 = (s32[64,128]{1,0:T(8,128)S(1)}, s32[64,128]{1,0:T(8,128)}, u32[]{:S(2)}) copy-start(s32[64,128]{1,0:T(8,128)} %snodes_ref.11) | copy-start | bytes 98308
  1.4 8.4 %copy-start.6 = (s32[32,128]{1,0:T(8,128)S(1)}, s32[32,128]{1,0:T(8,128)}, u32[]{:S(2)}) copy-start(s32[32,128]{1,0:T(8,128)} %mnodes_ref.11) | copy-start | bytes 49156
  2.2 7.6 %copy-start = (f32[128,128]{1,0:T(8,128)S(1)}, f32[128,128]{1,0:T(8,128)}, u32[]{:S(2)}) copy-start(f32[128,128]{1,0:T(8,128)} %mortar_ref.1) | copy-start | bytes 196612
  2.2 13.2 %all-to-all-start = ((f32[16,1,64]{2,1,0:T(1,128)}), f32[16,1,64]{2,1,0:T(1,128)S(1)}, u32[]{:S(2)}, u32[]{:S(2)}) async-start(f32[16,1,64]{2,1,0:T(1,128)} %bitcast.3), calls=%async_computation | async-start | bytes 16384 | tf_op jit(solution)/shard_map/all_to_all | solution.py:401
  9.8 0.7 copy-start.12
  10.4 1.2 %copy-start.14 = (s32[512]{0:T(512)S(1)}, s32[512]{0:T(512)}, u32[]{:S(2)}) copy-start(s32[512]{0:T(512)} %param.30) | copy-start | bytes 6148
  10.4 1.2 %copy-start.15 = (s32[512]{0:T(512)S(1)}, s32[512]{0:T(512)}, u32[]{:S(2)}) copy-start(s32[512]{0:T(512)} %param.29) | copy-start | bytes 6148
  16.6 4.2 %copy-start.1 = (s32[8,2048]{1,0:T(8,128)S(1)}, s32[8,2048]{1,0:T(8,128)}, u32[]{:S(2)}) copy-start(s32[8,2048]{1,0:T(8,128)} %conn_ref.5) | copy-start | bytes 196612
  16.6 4.2 %copy-start.8 = (f32[2048]{0:T(1024)S(1)}, f32[2048]{0:T(1024)}, u32[]{:S(2)}) copy-start(f32[2048]{0:T(1024)} %param.20) | copy-start | bytes 24580
  16.6 13.7 %all-to-all-start.1 = ((f32[16,32,128]{2,1,0:T(8,128)}), f32[16,32,128]{2,1,0:T(8,128)S(1)}, u32[]{:S(2)}, u32[]{:S(2)}) async-start(f32[16,32,128]{2,1,0:T(8,128)} %get-tuple-element.38), calls=%async_computation.1 | async-start | bytes 524288 | tf_op jit(solution)/shard_map/all_to_all | solution.py:438
  20.8 0.7 copy-start.7
  31.5 3.0 %collective-permute-start = (f32[3,4,128]{2,1,0:T(4,128)S(1)}, f32[3,4,128]{2,1,0:T(4,128)S(1)}, u32[]{:S(2)}, u32[]{:S(2)}) collective-permute-start(f32[3,4,128]{2,1,0:T(4,128)S(1)} %get-tuple-element.46), channel_id=1, source_target_pairs={{0,1},{1,0},{2,3},{3,2},{4,5},{5,4},{6,7},{7,6},{8,9},{9,8},{10,11... | collective-permute-start | bytes 18440 | tf_op jit(solution)/shard_map/ppermute | solution.py:455
  32.5 4.9 %collective-permute-start.1 = (f32[3,4,128]{2,1,0:T(4,128)S(1)}, f32[3,4,128]{2,1,0:T(4,128)S(1)}, u32[]{:S(2)}, u32[]{:S(2)}) collective-permute-start(f32[3,4,128]{2,1,0:T(4,128)S(1)} %get-tuple-element.47), channel_id=1, source_target_pairs={{1,2},{3,4},{5,6},{7,8},{9,10},{11,12},{13,14},{2,1},{4,3},{6,5},{... | collective-permute-start | bytes 18440 | tf_op jit(solution)/shard_map/ppermute | solution.py:456
  39.2 13.0 %all-to-all-start.2 = ((f32[16,32,128]{2,1,0:T(8,128)}), f32[16,32,128]{2,1,0:T(8,128)S(1)}, u32[]{:S(2)}, u32[]{:S(2)}) async-start(f32[16,32,128]{2,1,0:T(8,128)} %get-tuple-element.54), calls=%async_computation.2 | async-start | bytes 524288 | tf_op jit(solution)/shard_map/all_to_all | solution.py:438
  53.4 2.8 %collective-permute-start.2 = (f32[3,4,128]{2,1,0:T(4,128)S(1)}, f32[3,4,128]{2,1,0:T(4,128)S(1)}, u32[]{:S(2)}, u32[]{:S(2)}) collective-permute-start(f32[3,4,128]{2,1,0:T(4,128)S(1)} %get-tuple-element.59), channel_id=1, source_target_pairs={{0,1},{1,0},{2,3},{3,2},{4,5},{5,4},{6,7},{7,6},{8,9},{9,8},{10,11... | collective-permute-start | bytes 18440 | tf_op jit(solution)/shard_map/ppermute | solution.py:455
  54.1 4.9 %collective-permute-start.3 = (f32[3,4,128]{2,1,0:T(4,128)S(1)}, f32[3,4,128]{2,1,0:T(4,128)S(1)}, u32[]{:S(2)}, u32[]{:S(2)}) collective-permute-start(f32[3,4,128]{2,1,0:T(4,128)S(1)} %get-tuple-element.60), channel_id=1, source_target_pairs={{1,2},{3,4},{5,6},{7,8},{9,10},{11,12},{13,14},{2,1},{4,3},{6,5},{... | collective-permute-start | bytes 18440 | tf_op jit(solution)/shard_map/ppermute | solution.py:456
  60.8 13.0 %all-to-all-start.3 = ((f32[16,32,128]{2,1,0:T(8,128)}), f32[16,32,128]{2,1,0:T(8,128)S(1)}, u32[]{:S(2)}, u32[]{:S(2)}) async-start(f32[16,32,128]{2,1,0:T(8,128)} %get-tuple-element.62), calls=%async_computation.3 | async-start | bytes 524288 | tf_op jit(solution)/shard_map/all_to_all | solution.py:438
  75.0 2.8 %collective-permute-start.4 = (f32[3,4,128]{2,1,0:T(4,128)S(1)}, f32[3,4,128]{2,1,0:T(4,128)S(1)}, u32[]{:S(2)}, u32[]{:S(2)}) collective-permute-start(f32[3,4,128]{2,1,0:T(4,128)S(1)} %get-tuple-element.67), channel_id=1, source_target_pairs={{0,1},{1,0},{2,3},{3,2},{4,5},{5,4},{6,7},{7,6},{8,9},{9,8},{10,11... | collective-permute-start | bytes 18440 | tf_op jit(solution)/shard_map/ppermute | solution.py:455
  75.7 4.9 %collective-permute-start.5 = (f32[3,4,128]{2,1,0:T(4,128)S(1)}, f32[3,4,128]{2,1,0:T(4,128)S(1)}, u32[]{:S(2)}, u32[]{:S(2)}) collective-permute-start(f32[3,4,128]{2,1,0:T(4,128)S(1)} %get-tuple-element.68), channel_id=1, source_target_pairs={{1,2},{3,4},{5,6},{7,8},{9,10},{11,12},{13,14},{2,1},{4,3},{6,5},{... | collective-permute-start | bytes 18440 | tf_op jit(solution)/shard_map/ppermute | solution.py:456
